TPU v7x, 32 devices: a whole 2x2x4 slice. The times are simulated.
32 devices in a mesh: grp: 4 (over y, core), wsh: 8 (over z, x).
Axes of the slice: x: 2, y: 2, z: 4, core: 2. Of those that a mesh axis runs over, the one named last changes fastest.
Arguments:
- tokens: bfloat16 [2048, 2048], P('grp', 'wsh'), may hold values from -6 to 6
- gate_weight: bfloat16 [2048, 7168], P(None, 'wsh'), may hold values from -0.125 to 0.125
- up_weight: bfloat16 [2048, 7168], P(None, 'wsh'), may hold values from -0.125 to 0.125
- down_weight: bfloat16 [7168, 2048], P('wsh'), may hold values from -0.0625 to 0.0625
- gate_left: bfloat16 [256, 2048], P('grp'), may hold values from -0.125 to 0.125
- gate_right: float32 [256, 7168], P('grp', 'wsh'), may hold values from -6 to 6
- up_left: bfloat16 [256, 2048], P('grp'), may hold values from -0.125 to 0.125
- up_right: float32 [256, 7168], P('grp', 'wsh'), may hold values from -6 to 6
- down_left: bfloat16 [256, 7168], P('grp', 'wsh'), may hold values from -0.0625 to 0.0625
- down_right: float32 [256, 2048], P('grp'), may hold values from -6 to 6
- fitness_rank: int32 [256], P('grp'), may hold values from 0 to 255, each once
Outputs:
- mixed: bfloat16 [2048, 2048], P('grp', 'wsh')
- gate_step: bfloat16 [2048, 7168], P('grp', 'wsh')
- up_step: bfloat16 [2048, 7168], P('grp', 'wsh')
All inputs are finite; a program needn't handle non-finite values.
Results may differ from a plain program's by a relative error of at most 0.005.
Values may be sent and summed in bfloat16 or wider, within the bound.
No kernel may reach another device: no remote copies, remote signals or barrier semaphores. Data moves between devices by JAX's collectives and lax.ppermute only.
A program may use at most 64 MiB of HBM per device.

v0:
```python
import math

import jax
import jax.numpy as jnp
from jax import lax
from jax.sharding import PartitionSpec as P

noise_scale = 0.5


def silu(value):
    return value / (1.0 + jnp.exp(-value))


def per_device(
    tokens,
    gate_weight,
    up_weight,
    down_weight,
    gate_left,
    gate_right,
    up_left,
    up_right,
    down_left,
    down_right,
    fitness_rank,
):
    members = gate_left.shape[0]
    rows = tokens.shape[0]
    per_member = rows // members
    width = gate_left.shape[1]
    hidden_cols = gate_weight.shape[1]
    piece = lax.all_gather(tokens, "wsh", axis=1, tiled=True)
    count = piece.shape[1]
    grouped = piece.reshape(members, per_member, count)
    gate_sum = jnp.dot(piece, gate_weight, preferred_element_type=jnp.float32)
    up_sum = jnp.dot(piece, up_weight, preferred_element_type=jnp.float32)
    gate_score = jnp.einsum("mtk,mk->mt", grouped, gate_left, preferred_element_type=jnp.float32)
    up_score = jnp.einsum("mtk,mk->mt", grouped, up_left, preferred_element_type=jnp.float32)
    gate = gate_sum + noise_scale * (gate_score[:, :, None] * gate_right[:, None, :]).reshape(
        rows, hidden_cols
    )
    up = up_sum + noise_scale * (up_score[:, :, None] * up_right[:, None, :]).reshape(
        rows, hidden_cols
    )
    hidden = (silu(gate) * up).astype(jnp.bfloat16)
    down_score = jnp.einsum(
        "mtf,mf->mt",
        hidden.reshape(members, per_member, hidden_cols),
        down_left,
        preferred_element_type=jnp.float32,
    )
    span = width // lax.axis_size("wsh")
    product = jnp.dot(hidden, down_weight, preferred_element_type=jnp.float32)
    mixed = lax.psum_scatter(product, "wsh", scatter_dimension=1, tiled=True)
    total_score = lax.psum(down_score, "wsh")
    right_part = lax.dynamic_slice_in_dim(down_right, lax.axis_index("wsh") * span, span, 1)
    mixed = mixed + noise_scale * (total_score[:, :, None] * right_part[:, None, :]).reshape(
        rows, span
    )
    mixed = mixed.astype(jnp.bfloat16)
    groups = lax.axis_size("grp")
    total_members = members * groups
    weight_fit = (2.0 * fitness_rank.astype(jnp.float32) - (total_members - 1)) / (
        total_members - 1
    )
    gate_cols, up_cols, fit_all = (
        lax.all_gather(gate_right, "grp", axis=0, tiled=True),
        lax.all_gather(up_right, "grp", axis=0, tiled=True),
        lax.all_gather(weight_fit, "grp", axis=0, tiled=True),
    )
    block = width // groups
    gate_all, up_all = (
        lax.all_gather(gate_left, "grp", axis=0, tiled=True),
        lax.all_gather(up_left, "grp", axis=0, tiled=True),
    )
    offset = lax.axis_index("grp") * block
    gate_block = lax.dynamic_slice_in_dim(gate_all, offset, block, 1)
    up_block = lax.dynamic_slice_in_dim(up_all, offset, block, 1)
    scale = math.sqrt(width / total_members)

    def outer(left, right):
        weighted = fit_all[:, None] * left.astype(jnp.float32)
        return (
            scale
            * jnp.dot(
                weighted.T,
                right,
                precision=lax.Precision.HIGHEST,
                preferred_element_type=jnp.float32,
            )
        ).astype(jnp.bfloat16)

    return (mixed, outer(gate_block, gate_cols), outer(up_block, up_cols))


def solution(mesh):
    in_specs = (
        P("grp", "wsh"),
        P(None, "wsh"),
        P(None, "wsh"),
        P("wsh", None),
        P("grp", None),
        P("grp", "wsh"),
        P("grp", None),
        P("grp", "wsh"),
        P("grp", "wsh"),
        P("grp", None),
        P("grp"),
    )
    out_specs = (P("grp", "wsh"), P("grp", "wsh"), P("grp", "wsh"))
    return jax.shard_map(
        per_device, mesh=mesh, in_specs=in_specs, out_specs=out_specs, check_vma=False
    )
```

profile of v0, /device:TPU:0, one launch (start us, length us, event | category | flops | bytes accessed | tf_op | source)
XLA Modules:
  0.0 202.6 jit_solution(4435544491906365299)
XLA Ops:
  7.2 0.0 copy-start
  7.2 0.0 all-gather.4.cloned.1.call-start
  7.2 0.7 all-gather.4.cloned.1.call-update
  7.9 0.0 all-gather.8.cloned.1.call-start
  8.0 0.7 all-gather.8.cloned.1.call-update
  8.7 0.0 all-gather.6.cloned.1.call-start
  8.7 0.7 all-gather.6.cloned.1.call-update
  9.4 0.0 reduce-scatter.2.cloned.1.call-start
  9.4 54.4 %all-gather.4.cloned.1.call-done = bf16[512,2048]{1,0:T(8,128)(2,1)} async-done(((bf16[512,256]{1,0:T(8,128)(2,1)}), bf16[512,2048]{1,0:T(8,128)(2,1)}) %all-gather.4.cloned.1.call-update) | async-done | bytes 2097168 | tf_op jit(solution)/shard_map/all_gather | solution.py:33
  63.9 0.0 copy-start.5
  63.9 3.2 %fusion.2 = f32[64,1,8]{2,1,0:T(1,128)S(1)} fusion(bf16[512,2048]{1,0:T(8,128)(2,1)} %all-gather.4.cloned.1.call-done, bf16[64,2048,1]{1,0,2:T(8,128)(2,1)} %bitcast.53), kind=kOutput, calls=%fused_computation.2 | convolution fusion | flops 2097152 | bytes 2361344 | tf_op jit(solution)/shard_map/mtk,mk->mt/dot_general | solution.py:38
  67.0 0.1 mul.101
  67.1 0.0 copy-done.5
  67.1 0.0 copy-start.1
  67.1 5.7 %fusion.28 = f32[512,896]{1,0:T(8,128)} fusion(bf16[512,2048]{1,0:T(8,128)(2,1)S(1)} %copy-done.5, bf16[2048,896]{1,0:T(8,128)(2,1)} %param.12), kind=kOutput, calls=%fused_computation.35 | convolution fusion | flops 1879048192 | bytes 7602176 | tf_op jit(solution)/shard_map/dot_general | solution.py:36
  72.8 0.0 copy-done.1
  72.8 0.0 copy-start.2
  72.8 0.0 copy-start.3
  72.8 1.4 fusion
  74.2 0.1 mul.107
  74.3 0.0 copy-done.2
  74.3 0.0 copy-done.3
  74.3 0.0 copy-start.4
  74.4 5.5 %fusion.7 = bf16[512,896]{1,0:T(8,128)(2,1)S(1)} fusion(f32[512,896]{1,0:T(8,128)} %fusion.28, bf16[512,2048]{1,0:T(8,128)(2,1)S(1)} %copy-done.5, bf16[2048,896]{1,0:T(8,128)(2,1)} %param.13, f32[64,896]{1,0:T(8,128)S(1)} %copy-done.2, f32[512]{0:T(512)S(1)} %mul.107, f32[64,896]{1,0:T(8,128)S(1)} %copy-done.3, f32[512]{0:T(512)S(1)} %mul.101), kind=kOutput, calls=%fused_computation.8 | convolution fusion | flops 1884094464 | bytes 8982528 | tf_op jit(solution)/shard_map/dot_general | solution.py:37
  79.8 0.0 copy-start.9
  79.8 0.9 copy-done.9
  80.8 0.0 copy-done.4
  80.8 4.3 %fusion.29 = f32[512,2048]{1,0:T(8,128)} fusion(bf16[512,896]{1,0:T(8,128)(2,1)S(1)} %fusion.7, bf16[896,2048]{1,0:T(8,128)(2,1)S(1)} %copy-done.4), kind=kOutput, calls=%fused_computation.36 | convolution fusion | flops 1879048192 | bytes 8781824 | tf_op jit(solution)/shard_map/dot_general | solution.py:54
  85.1 0.0 copy-start.8
  85.1 0.0 copy-start.7
  85.1 0.0 reduce-scatter.2.cloned.1.call-update
  85.1 0.6 copy-done.8
  85.7 0.6 dynamic-slice
  87.0 0.0 copy-done.7
  87.0 0.1 multiply_dynamic-update-slice_fusion
  87.1 6.5 %all-reduce = f32[256]{0:T(256)S(1)} all-reduce(f32[256]{0:T(256)S(1)} %multiply_dynamic-update-slice_fusion), channel_id=1, replica_groups=mesh['grp'=4,'wsh'=8] {'grp'}, use_global_device_ids=true, to_apply=%add | all-reduce | flops 256 | bytes 2048
  93.6 0.0 copy-done
  93.7 9.4 %all_gather.23 = f32[256,896]{1,0:T(8,128)S(1)} all-gather(f32[64,896]{1,0:T(8,128)S(1)} %copy-done.2), channel_id=1, replica_groups=mesh['grp'=4,'wsh'=8] {'grp'}, dimensions={0}, use_global_device_ids=true | all-gather | bytes 1146880 | tf_op jit(solution)/shard_map/all_gather | solution.py:69
  103.1 9.6 %all_gather.21 = f32[256,896]{1,0:T(8,128)S(1)} all-gather(f32[64,896]{1,0:T(8,128)S(1)} %copy-done.3), channel_id=1, replica_groups=mesh['grp'=4,'wsh'=8] {'grp'}, dimensions={0}, use_global_device_ids=true | all-gather | bytes 1146880 | tf_op jit(solution)/shard_map/all_gather | solution.py:68
  112.7 0.0 all-gather.8.cloned.1.call-done
  112.7 3.8 %multiply_convert_fusion = bf16[512,896]{1,0:T(8,128)(2,1)} fusion(f32[256,896]{1,0:T(8,128)S(1)} %all_gather.23, bf16[256,2048]{1,0:T(8,128)(2,1)} %all-gather.8.cloned.1.call-done, s32[]{:T(128)S(6)} %select_n.8, f32[256]{0:T(256)S(1)} %all-reduce), kind=kOutput, calls=%fused_computation.12 | convolution fusion | flops 1410465792 | bytes 2098180 | tf_op jit(solution)/shard_map/dot_general | solution.py:86
  116.5 3.8 %multiply_convert_fusion.1 = bf16[512,896]{1,0:T(8,128)(2,1)} fusion(f32[256,896]{1,0:T(8,128)S(1)} %all_gather.21, bf16[256,2048]{1,0:T(8,128)(2,1)} %all-gather.6.cloned.1.call-done, s32[]{:T(128)S(6)} %select_n.8, f32[256]{0:T(256)S(1)} %all-reduce), kind=kOutput, calls=%fused_computation.13 | convolution fusion | flops 1410465792 | bytes 2098180 | tf_op jit(solution)/shard_map/dot_general | solution.py:86
  120.3 0.0 copy-done.6
  120.3 1.9 fusion.10
  122.2 0.1 mul.114
  122.3 22.2 %psum.7 = f32[512]{0:T(512)S(1)} all-reduce(f32[512]{0:T(512)S(1)} %mul.114), channel_id=1, replica_groups=mesh['grp'=4,'wsh'=8] {'wsh'}, use_global_device_ids=true, to_apply=%region_1.0 | all-reduce | flops 512 | bytes 4096 | tf_op jit(solution)/shard_map/psum | solution.py:56
  144.5 49.7 %reduce-scatter.2.cloned.1.call-done = f32[512,256]{1,0:T(8,128)} async-done(((f32[512,2048]{1,0:T(8,128)}), f32[512,256]{1,0:T(8,128)}) %reduce-scatter.2.cloned.1.call-update) | async-done | bytes 524304 | tf_op jit(solution)/shard_map/reduce_scatter | solution.py:55
  194.2 1.9 fusion.14
  (4 shorter events, 0.0 us)
Async XLA Ops:
  7.2 86.5 %copy-start = (f32[64,2048]{1,0:T(8,128)S(1)}, f32[64,2048]{1,0:T(8,128)}, u32[]{:S(2)}) copy-start(f32[64,2048]{1,0:T(8,128)} %param.20) | copy-start | bytes 1572868
  7.2 56.7 %all-gather.4.cloned.1.call-start = ((), (), s32[]{:S(2)}) async-start(), calls=%async_computation.1 | async-start | bytes 2359296 | tf_op jit(solution)/shard_map/all_gather | solution.py:33
  7.9 104.8 %all-gather.8.cloned.1.call-start = ((), (), s32[]{:S(2)}) async-start(), calls=%async_computation.4 | async-start | bytes 1310720 | tf_op jit(solution)/shard_map/all_gather | solution.py:75
  8.7 107.9 %all-gather.6.cloned.1.call-start = ((), (), s32[]{:S(2)}) async-start(), calls=%async_computation.3 | async-start | bytes 1310720 | tf_op jit(solution)/shard_map/all_gather | solution.py:74
  9.4 184.8 %reduce-scatter.2.cloned.1.call-start = ((), (), s32[]{:S(2)}) async-start(), calls=%async_computation.2 | async-start | bytes 4718592 | tf_op jit(solution)/shard_map/reduce_scatter | solution.py:55
  63.9 3.2 %copy-start.5 = (bf16[512,2048]{1,0:T(8,128)(2,1)S(1)}, bf16[512,2048]{1,0:T(8,128)(2,1)}, u32[]{:S(2)}) copy-start(bf16[512,2048]{1,0:T(8,128)(2,1)} %all-gather.4.cloned.1.call-done) | copy-start | bytes 6291460
  67.1 5.7 %copy-start.1 = (bf16[64,2048]{1,0:T(8,128)(2,1)S(1)}, bf16[64,2048]{1,0:T(8,128)(2,1)}, u32[]{:S(2)}) copy-start(bf16[64,2048]{1,0:T(8,128)(2,1)} %param.17) | copy-start | bytes 786436
  72.8 1.5 copy-start.2
  72.8 1.5 copy-start.3
  74.3 6.5 %copy-start.4 = (bf16[896,2048]{1,0:T(8,128)(2,1)S(1)}, bf16[896,2048]{1,0:T(8,128)(2,1)}, u32[]{:S(2)}) copy-start(bf16[896,2048]{1,0:T(8,128)(2,1)} %param.14) | copy-start | bytes 11010052
  79.8 1.0 copy-start.9
  85.1 0.7 copy-start.8
  85.1 1.9 copy-start.7
  112.7 7.7 %copy-start.6 = (bf16[64,896]{1,0:T(8,128)(2,1)S(1)}, bf16[64,896]{1,0:T(8,128)(2,1)}, u32[]{:S(2)}) copy-start(bf16[64,896]{1,0:T(8,128)(2,1)} %param.19) | copy-start | bytes 344068
Sparse Core Ops, SparseCore 0:
  10.1 53.7 all-gather.3
  65.4 14.9 all-gather.7
  81.9 17.2 all-gather.5
  102.7 91.4 reduce-scatter.1
where the time goes:
time: 203 us
  waiting for transfers between devices  106 us (52%)
  blocking collectives  47.8 us (24%)
  matrix products  29.5 us (15%)
  between operations  14.5 us (7%)
  local copies, waits for them, and re-layouts  2.49 us (1%)
    all_gather x1, waiting for transfers between devices, per_device(): piece = lax.all_gather(tokens, 'wsh', axis=1, tiled=True)  54.4 us
    reduce_scatter x1, waiting for transfers between devices, per_device(): mixed = lax.psum_scatter(product, 'wsh', scatter_dimension=1, tiled=True)  49.7 us
    psum x1, blocking collectives, per_device(): total_score = lax.psum(down_score, 'wsh')  22.2 us
    all_gather x1, blocking collectives, per_device(): lax.all_gather(gate_right, 'grp', axis=0, tiled=True)  9.6 us
    all_gather x1, blocking collectives, per_device(): lax.all_gather(up_right, 'grp', axis=0, tiled=True)  9.42 us
    dot_general x2, matrix products, outer(): jnp.dot(weighted.T, right, precision=lax.Precision.HIGHEST, preferred_ele...  7.65 us
    unnamed x1, blocking collectives  6.55 us
    dot_general x1, matrix products, per_device(): gate_sum = jnp.dot(piece, gate_weight, preferred_element_type=jnp.float32)  5.68 us
  transfers between devices with their start and end apart: 4, of which 2 were waited for; matrix products, arithmetic and copies ran while one was open for 15% of the time, Pallas kernels for 0%

commit v1 on v0

v1 whole, which is shorter than its diff:
```python
import math

import jax
import jax.numpy as jnp
from jax import lax
from jax.sharding import PartitionSpec as P

noise_scale = 0.5


def silu(value):
    return value / (1.0 + jnp.exp(-value))


def ring_place(index, n):
    return jnp.where(index % 2 == 0, index // 2, n - 1 - index // 2)


def ring_owner(place, n):
    place = place % n
    return jnp.where(place < n // 2, 2 * place, 2 * (n - 1 - place) + 1)


def per_device(
    tokens,
    gate_weight,
    up_weight,
    down_weight,
    gate_left,
    gate_right,
    up_left,
    up_right,
    down_left,
    down_right,
    fitness_rank,
):
    members, width = gate_left.shape
    rows, span = tokens.shape
    per_member = rows // members
    hidden_cols = gate_weight.shape[1]
    n = lax.axis_size("wsh")
    groups = lax.axis_size("grp")
    total_members = members * groups
    hops = n // 2
    half = rows // 2
    wire = jnp.bfloat16 if n <= 8 else jnp.float32

    order = [2 * q for q in range(hops)] + [2 * (n - 1 - q) + 1 for q in range(hops, n)]
    onward = [(order[q], order[(q + 1) % n]) for q in range(n)]
    back = [(b, a) for a, b in onward]
    place = ring_place(lax.axis_index("wsh"), n)

    weight_fit = (2.0 * fitness_rank.astype(jnp.float32) - (total_members - 1)) / (
        total_members - 1
    )
    rights = jnp.concatenate([gate_right, up_right], axis=1)
    fitted = (weight_fit[:, None] * rights).astype(jnp.bfloat16)
    block = width // groups
    grp = lax.axis_index("grp")
    if groups == 4:
        pair = [(g, g ^ 2) for g in range(4)]
        mate = [(g, g ^ 1) for g in range(4)]
        lefts = jnp.stack([gate_left, up_left])
        far = (1 - grp // 2) * 2 * block
        near = (grp // 2) * 2 * block
        away = lax.dynamic_slice_in_dim(lefts, far, 2 * block, 2)
        here = lax.dynamic_slice_in_dim(lefts, near, 2 * block, 2)
        fitted_far = lax.ppermute(fitted, "grp", pair)
        left_far = lax.ppermute(away, "grp", pair)
        fitted_two = jnp.concatenate([fitted, fitted_far], axis=0)
        left_two = jnp.concatenate([here, left_far], axis=1)
        other = (1 - grp % 2) * block
        mine = (grp % 2) * block
        left_out = lax.dynamic_slice_in_dim(left_two, other, block, 2)
        left_own = lax.dynamic_slice_in_dim(left_two, mine, block, 2)
        fitted_in = lax.ppermute(fitted_two, "grp", mate)
        left_in = lax.ppermute(left_out, "grp", mate)
        fitted_all = jnp.concatenate([fitted_two, fitted_in], axis=0)
        left_all = jnp.concatenate([left_own, left_in], axis=1)
        gate_block, up_block = left_all[0], left_all[1]
    else:
        fitted_all = lax.all_gather(fitted, "grp", axis=0, tiled=True)
        gate_all = lax.all_gather(gate_left, "grp", axis=0, tiled=True)
        up_all = lax.all_gather(up_left, "grp", axis=0, tiled=True)
        gate_block = lax.dynamic_slice_in_dim(gate_all, grp * block, block, 1)
        up_block = lax.dynamic_slice_in_dim(up_all, grp * block, block, 1)
    scale = math.sqrt(width / total_members)

    def outer(left, right):
        total = lax.dot_general(
            left, right, (((0,), (0,)), ((), ())), preferred_element_type=jnp.float32
        )
        return (scale * total).astype(jnp.bfloat16)

    gate_step = outer(gate_block, fitted_all[:, :hidden_cols])
    up_step = outer(up_block, fitted_all[:, hidden_cols:])

    left_both = jnp.concatenate([gate_left, up_left], axis=0)

    def grow(total, piece, owner):
        at = owner * span
        gate_w = lax.dynamic_slice_in_dim(gate_weight, at, span, 0)
        up_w = lax.dynamic_slice_in_dim(up_weight, at, span, 0)
        left_w = lax.dynamic_slice_in_dim(left_both, at, span, 1)
        new = (
            jnp.dot(piece, gate_w, preferred_element_type=jnp.float32),
            jnp.dot(piece, up_w, preferred_element_type=jnp.float32),
            lax.dot_general(
                piece, left_w, (((1,), (1,)), ((), ())), preferred_element_type=jnp.float32
            ),
        )
        return new if total is None else tuple(a + b for a, b in zip(total, new))

    from_back, from_front = tokens, tokens
    total = None
    for hop in range(1, hops):
        sent_on, sent_back = from_back, from_front
        from_back = lax.ppermute(sent_on, "wsh", onward)
        from_front = lax.ppermute(sent_back, "wsh", back)
        if hop == 1:
            total = grow(total, tokens, ring_owner(place, n))
        else:
            total = grow(total, sent_on, ring_owner(place - hop + 1, n))
            total = grow(total, sent_back, ring_owner(place + hop - 1, n))
    top = lax.ppermute(from_back[:half], "wsh", onward)
    bottom = lax.ppermute(from_front[half:], "wsh", back)
    total = grow(total, from_back, ring_owner(place - hops + 1, n))
    total = grow(total, from_front, ring_owner(place + hops - 1, n))
    total = grow(total, jnp.concatenate([top, bottom], axis=0), ring_owner(place + hops, n))
    gate_sum, up_sum, scores = total

    own_member = (
        lax.broadcasted_iota(jnp.int32, (rows, members), 0) // per_member
        == lax.broadcasted_iota(jnp.int32, (rows, members), 1)
    )

    def pick(values):
        return jnp.sum(jnp.where(own_member, values, 0.0), axis=1)

    def spread(score, right):
        return (
            score.reshape(members, per_member)[:, :, None] * (noise_scale * right)[:, None, :]
        ).reshape(rows, right.shape[1])

    gate = gate_sum + spread(pick(scores[:, :members]), gate_right)
    up = up_sum + spread(pick(scores[:, members:]), up_right)
    hidden = (silu(gate) * up).astype(jnp.bfloat16)
    down_score = pick(
        lax.dot_general(
            hidden, down_left, (((1,), (1,)), ((), ())), preferred_element_type=jnp.float32
        )
    )

    def share(owner):
        at = owner * span
        down_w = lax.dynamic_slice_in_dim(down_weight, at, span, 1)
        right = lax.dynamic_slice_in_dim(down_right, at, span, 1)
        return jnp.dot(hidden, down_w, preferred_element_type=jnp.float32) + spread(
            down_score, right
        )

    opposite = share(ring_owner(place + hops, n)).astype(wire)
    got_on = lax.ppermute(opposite[:half], "wsh", onward)
    got_back = lax.ppermute(opposite[half:], "wsh", back)
    for hop in range(hops - 1, 0, -1):
        ahead = share(ring_owner(place + hop, n))
        behind = share(ring_owner(place - hop, n))
        if hop == hops - 1:
            ahead = jnp.concatenate([ahead[:half] + got_on.astype(jnp.float32), ahead[half:]], axis=0)
            behind = jnp.concatenate([behind[:half], behind[half:] + got_back.astype(jnp.float32)], axis=0)
        else:
            ahead = ahead + got_on.astype(jnp.float32)
            behind = behind + got_back.astype(jnp.float32)
        got_on = lax.ppermute(ahead.astype(wire), "wsh", onward)
        got_back = lax.ppermute(behind.astype(wire), "wsh", back)
    own = share(ring_owner(place, n))
    mixed = own + got_on.astype(jnp.float32) + got_back.astype(jnp.float32)
    return mixed.astype(jnp.bfloat16), gate_step, up_step


def solution(mesh):
    in_specs = (
        P("grp", "wsh"),
        P(None, "wsh"),
        P(None, "wsh"),
        P("wsh", None),
        P("grp", None),
        P("grp", "wsh"),
        P("grp", None),
        P("grp", "wsh"),
        P("grp", "wsh"),
        P("grp", None),
        P("grp"),
    )
    out_specs = (P("grp", "wsh"), P("grp", "wsh"), P("grp", "wsh"))
    return jax.shard_map(
        per_device, mesh=mesh, in_specs=in_specs, out_specs=out_specs, check_vma=False
    )
```

time: 203 us -> 104 us (0.51)
  waiting for transfers between devices: 106 us -> 20.7 us
  blocking collectives: 47.8 us -> 0 us
  starting transfers between devices: 0.15 us -> 21.9 us
  between operations: 14.5 us -> 1.45 us
  other arithmetic: 1.99 us -> 13 us
  matrix products: 29.5 us -> 40.1 us
  local copies, waits for them, and re-layouts: 2.49 us -> 6.02 us
    all_gather x3 -> x0, waiting for transfers between devices: 54.4 us -> none  [the longest x1 54.4 us: per_device(): piece = lax.all_gather(tokens, 'wsh', axis=1, tiled=True)]
    reduce_scatter x1 -> x0, waiting for transfers between devices: 49.7 us -> none  [per_device(): mixed = lax.psum_scatter(product, 'wsh', scatter_dimension=1, tiled=True)]
    psum x1 -> x0, blocking collectives: 22.2 us -> none  [per_device(): total_score = lax.psum(down_score, 'wsh')]
    ppermute x0 -> x20, starting transfers between devices: none -> 21.9 us  [the longest x3 6.73 us: per_device(): from_back = lax.ppermute(sent_on, 'wsh', onward)]
    ppermute x0 -> x20, waiting for transfers between devices: none -> 20.7 us  [the longest x3 12.6 us: per_device(): got_on = lax.ppermute(ahead.astype(wire), 'wsh', onward)]
    all_gather x2 -> x0, blocking collectives: 19 us -> none  [the longest x1 9.6 us: per_device(): lax.all_gather(gate_right, 'grp', axis=0, tiled=True)]
    dot_general x8 -> x35, matrix products: 29.5 us -> 40.1 us  [the longest x8 15.5 us: grow(): jnp.dot(piece, up_w, preferred_element_type=jnp.float32)]
    unnamed x1 -> x0, blocking collectives: 6.55 us -> none
  transfers between devices with their start and end apart: 4 -> 20, of which waited for: 2 -> 9; matrix products, arithmetic and copies ran while one was open for 15% -> 43% of each run, Pallas kernels for 0% -> 0%
where the time goes in v1:
time: 104 us; the launch traced here: 103 us
  matrix products  40.1 us (39%)
  starting transfers between devices  21.9 us (21%)
  waiting for transfers between devices  20.7 us (20%)
  other arithmetic  13 us (12%)
  local copies, waits for them, and re-layouts  6.02 us (6%)
  between operations  1.45 us (1%)
    dot_general x8, matrix products, grow(): jnp.dot(piece, up_w, preferred_element_type=jnp.float32)  15.5 us
    dot_general x8, matrix products, grow(): jnp.dot(piece, gate_w, preferred_element_type=jnp.float32)  13.1 us
    ppermute x3, waiting for transfers between devices, per_device(): got_on = lax.ppermute(ahead.astype(wire), 'wsh', onward)  12.6 us
    ppermute x3, starting transfers between devices, per_device(): from_back = lax.ppermute(sent_on, 'wsh', onward)  6.73 us
    ppermute x3, starting transfers between devices, per_device(): got_on = lax.ppermute(ahead.astype(wire), 'wsh', onward)  6.48 us
    dot_general x8, matrix products, share(): jnp.dot(hidden, down_w, preferred_element_type=jnp.float32)  6.04 us
    mul x4, local copies, waits for them, and re-layouts, spread(): score.reshape(members, per_member)[:, :, None]  5.09 us
    mul x3, other arithmetic, spread(): noise_scale * right  3.33 us
  transfers between devices with their start and end apart: 20, of which 9 were waited for; matrix products, arithmetic and copies ran while one was open for 43% of the time, Pallas kernels for 0%

profile of v1, /device:TPU:0, one launch (start us, length us, event | category | flops | bytes accessed | tf_op | source)
XLA Modules:
  0.0 103.2 jit_solution(3704918723163280933)
XLA Ops:
  0.7 3.1 %collective-permute-start = (bf16[512,256]{1,0:T(8,128)(2,1)}, bf16[512,256]{1,0:T(8,128)(2,1)S(1)}, u32[]{:S(2)}, u32[]{:S(2)}) collective-permute-start(bf16[512,256]{1,0:T(8,128)(2,1)} %param.11), channel_id=1, source_target_pairs={{0,2},{2,4},{4,6},{6,7},{7,5},{5,3},{3,1},{1,0},{8,10},{10,12},{12... | collective-permute-start | bytes 786440 | tf_op jit(solution)/shard_map/ppermute | solution.py:118
  3.8 2.0 %fusion.64 = (bf16[2,64,1024]{2,1,0:T(8,128)(2,1)}, bf16[2,64,1024]{2,1,0:T(8,128)(2,1)}) fusion(s32[]{:T(128)S(6)} %select_n.225, bf16[1,64,2048]{2,1,0:T(8,128)(2,1)} %bitcast.100, bf16[1,64,2048]{2,1,0:T(8,128)(2,1)} %bitcast.101, s32[]{:T(128)S(6)} %select_n.224), kind=kLoop, calls=%fused_computation.102 | loop fusion | flops 1048576 | bytes 1048584 | tf_op jit(solution)/shard_map/stack | solution.py:63
  5.7 2.0 %collective-permute-start.16 = (bf16[2,64,1024]{2,1,0:T(8,128)(2,1)}, bf16[2,64,1024]{2,1,0:T(8,128)(2,1)}, u32[]{:S(2)}, u32[]{:S(2)}) collective-permute-start(bf16[2,64,1024]{2,1,0:T(8,128)(2,1)} %get-tuple-element.7), channel_id=1, source_target_pairs={{0,16},{8,24},{16,0},{24,8},{1,17},{9,25},{17,1},{25,9},{2,18},{10... | collective-permute-start | bytes 786440 | tf_op jit(solution)/shard_map/ppermute | solution.py:69
  7.7 0.7 add_multiply_fusion
  8.4 1.1 %fusion.12 = bf16[64,1792]{1,0:T(8,128)(2,1)S(1)} fusion(f32[64,896]{1,0:T(8,128)} %param.18, f32[64,896]{1,0:T(8,128)} %param.16, f32[64]{0:T(128)S(1)} %add_multiply_fusion), kind=kLoop, calls=%fused_computation.56 | loop fusion | flops 344064 | bytes 688384 | tf_op jit(solution)/shard_map/convert_element_type | solution.py:57
  9.9 0.7 broadcast_multiply_fusion.1
  10.6 0.7 broadcast_multiply_fusion
  11.4 0.9 fusion.83
  12.3 2.7 %fusion.41 = f32[896,512]{1,0:T(8,128)} fusion(bf16[512,256]{1,0:T(8,128)(2,1)S(1)} %copy-done.6, bf16[2048,896]{1,0:T(8,128)(2,1)} %param.13, s32[]{:T(128)S(6)} %select_n.197), kind=kOutput, calls=%fused_computation.80 | convolution fusion | flops 234881024 | bytes 2555908 | tf_op jit(solution)/shard_map/dot_general | solution.py:107
  15.0 2.8 %fusion.57 = f32[896,512]{1,0:T(8,128)} fusion(bf16[512,256]{1,0:T(8,128)(2,1)S(1)} %copy-done.6, bf16[2048,896]{1,0:T(8,128)(2,1)} %param.12, s32[]{:T(128)S(6)} %select_n.197), kind=kOutput, calls=%fused_computation.96 | convolution fusion | flops 234881024 | bytes 2555908 | tf_op jit(solution)/shard_map/dot_general | solution.py:106
  17.9 1.4 %broadcast_bitcast_fusion = f32[512,896]{1,0:T(8,128)} fusion(f32[64,896]{1,0:T(8,128)S(1)} %copy-done.13), kind=kLoop, calls=%fused_computation.28 | loop fusion | bytes 2064384 | tf_op jit(solution)/shard_map/mul | solution.py:142
  19.3 1.9 %dynamic-slice_multiply_fusion.5 = (f32[64,256]{1,0:T(8,128)}, f32[64,256]{1,0:T(8,128)}, f32[64,256]{1,0:T(8,128)}, f32[64,256]{1,0:T(8,128)}, f32[64,256]{1,0:...) fusion(f32[64,2048]{1,0:T(8,128)} %param.20, s32[]{:T(128)S(6)} %select_n.209, ...), kind=kLoop, calls=%fused_computation.127 | loop fusion | flops 131072 | bytes 1048608 | tf_op jit(solution)/shard_map/mul | solution.py:142
  21.7 0.6 iota_shift-right-logical_fusion
  22.9 1.8 %copy.19 = f32[512,896]{0,1:T(8,128)} copy(f32[512,896]{1,0:T(8,128)S(1)} %broadcast_bitcast_fusion.1) | data formatting | bytes 3670016 | tf_op jit(solution)/shard_map/mul | solution.py:142
  24.7 1.8 %copy.21 = f32[512,896]{0,1:T(8,128)S(1)} copy(f32[512,896]{1,0:T(8,128)} %broadcast_bitcast_fusion) | data formatting | bytes 3670016 | tf_op jit(solution)/shard_map/mul | solution.py:142
  26.6 1.1 %pad_maximum_fusion.1 = bf16[128,1792]{1,0:T(8,128)(2,1)S(1)} fusion(bf16[64,1792]{1,0:T(8,128)(2,1)} %collective-permute-done.18, bf16[64,1792]{1,0:T(8,128)(2,1)S(1)} %fusion.12), kind=kLoop, calls=%fused_computation.57 | loop fusion | flops 917504 | bytes 917504 | tf_op jit(solution)/shard_map/concatenate | solution.py:70
  27.8 1.0 fusion.62
  29.3 1.8 %collective-permute-start.2 = (bf16[512,256]{1,0:T(8,128)(2,1)S(1)}, bf16[512,256]{1,0:T(8,128)(2,1)S(1)}, u32[]{:S(2)}, u32[]{:S(2)}) collective-permute-start(bf16[512,256]{1,0:T(8,128)(2,1)S(1)} %collective-permute-done), channel_id=1, source_target_pairs={{0,2},{2,4},{4,6},{6,7},{7,5},{5,3},{3,1},{1,0},{8,10},{10,12},{12... | collective-permute-start | bytes 786440 | tf_op jit(solution)/shard_map/ppermute | solution.py:118
  31.2 1.5 %fusion.55 = f32[896,512]{1,0:T(8,128)S(1)} fusion(bf16[512,256]{1,0:T(8,128)(2,1)S(1)} %collective-permute-done, bf16[2048,896]{1,0:T(8,128)(2,1)} %param.12, s32[]{:T(128)S(6)} %select_n.200), kind=kOutput, calls=%fused_computation.94 | convolution fusion | flops 234881024 | bytes 2555908 | tf_op jit(solution)/shard_map/dot_general | solution.py:106
  33.4 1.5 %fusion.53 = f32[896,512]{1,0:T(8,128)S(1)} fusion(bf16[512,256]{1,0:T(8,128)(2,1)S(1)} %collective-permute-done.1, bf16[2048,896]{1,0:T(8,128)(2,1)} %param.12, s32[]{:T(128)S(6)} %select_n.203), kind=kOutput, calls=%fused_computation.92 | convolution fusion | flops 234881024 | bytes 2555908 | tf_op jit(solution)/shard_map/dot_general | solution.py:106
  35.8 1.8 %collective-permute-done.2 = bf16[512,256]{1,0:T(8,128)(2,1)S(1)} collective-permute-done((bf16[512,256]{1,0:T(8,128)(2,1)S(1)}, bf16[512,256]{1,0:T(8,128)(2,1)S(1)}, u32[]{:S(2)}, u32[]{:S(2)}) %collective-permute-start.2) | collective-permute-done | bytes 262176 | tf_op jit(solution)/shard_map/ppermute | solution.py:118
  37.6 1.8 %collective-permute-start.4 = (bf16[512,256]{1,0:T(8,128)(2,1)S(1)}, bf16[512,256]{1,0:T(8,128)(2,1)S(1)}, u32[]{:S(2)}, u32[]{:S(2)}) collective-permute-start(bf16[512,256]{1,0:T(8,128)(2,1)S(1)} %collective-permute-done.2), channel_id=1, source_target_pairs={{0,2},{2,4},{4,6},{6,7},{7,5},{5,3},{3,1},{1,0},{8,10},{10,12},{12... | collective-permute-start | bytes 786440 | tf_op jit(solution)/shard_map/ppermute | solution.py:118
  40.4 0.8 collective-permute-done.3
  41.5 1.8 %fusion.49 = f32[896,512]{1,0:T(8,128)} fusion(bf16[512,256]{1,0:T(8,128)(2,1)S(1)} %collective-permute-done.3, bf16[2048,896]{1,0:T(8,128)(2,1)S(1)} %copy-done.5, s32[]{:T(128)S(6)} %select_n.209), kind=kOutput, calls=%fused_computation.88 | convolution fusion | flops 234881024 | bytes 2555908 | tf_op jit(solution)/shard_map/dot_general | solution.py:106
  43.3 1.7 %fusion.33 = f32[896,512]{1,0:T(8,128)} fusion(bf16[512,256]{1,0:T(8,128)(2,1)S(1)} %collective-permute-done.3, bf16[2048,896]{1,0:T(8,128)(2,1)S(1)} %copy-done.4, s32[]{:T(128)S(6)} %select_n.209), kind=kOutput, calls=%fused_computation.72 | convolution fusion | flops 234881024 | bytes 2555908 | tf_op jit(solution)/shard_map/dot_general | solution.py:107
  45.5 1.0 pad_maximum_fusion
  46.5 1.4 %multiply_convert_fusion = bf16[512,896]{1,0:T(8,128)(2,1)} fusion(bf16[256,1792]{1,0:T(8,128)(2,1)S(1)} %pad_maximum_fusion, bf16[2,128,512]{2,1,0:T(8,128)(2,1)S(1)} %collective-permute-done.17, bf16[2,128,512]{2,1,0:T(8,128)(2,1)S(1)} %get-tuple-element.6), kind=kOutput, calls=%fused_computation.6 | convolution fusion | flops 236322816 | bytes 1900544 | tf_op jit(solution)/shard_map/dot_general | solution.py:90
  47.9 1.4 %multiply_convert_fusion.1 = bf16[512,896]{1,0:T(8,128)(2,1)} fusion(bf16[256,1792]{1,0:T(8,128)(2,1)S(1)} %pad_maximum_fusion, bf16[2,128,512]{2,1,0:T(8,128)(2,1)S(1)} %get-tuple-element.6, bf16[2,128,512]{2,1,0:T(8,128)(2,1)S(1)} %collective-permute-done.17), kind=kOutput, calls=%fused_computation.7 | convolution fusion | flops 236322816 | bytes 1900544 | tf_op jit(solution)/shard_map/dot_general | solution.py:90
  49.3 1.8 %collective-permute-start.6 = (bf16[256,256]{1,0:T(8,128)(2,1)S(1)}, bf16[256,256]{1,0:T(8,128)(2,1)S(1)}, u32[]{:S(2)}, u32[]{:S(2)}) collective-permute-start(bf16[256,256]{1,0:T(8,128)(2,1)S(1)} %slice.58), channel_id=1, source_target_pairs={{0,2},{2,4},{4,6},{6,7},{7,5},{5,3},{3,1},{1,0},{8,10},{10,12},{12... | collective-permute-start | bytes 393224 | tf_op jit(solution)/shard_map/ppermute | solution.py:125
  51.6 1.7 %fusion.45 = f32[896,512]{1,0:T(8,128)} fusion(bf16[512,256]{1,0:T(8,128)(2,1)S(1)} %collective-permute-done.5, bf16[2048,896]{1,0:T(8,128)(2,1)S(1)} %copy-done.5, s32[]{:T(128)S(6)} %select_n.215), kind=kOutput, calls=%fused_computation.84 | convolution fusion | flops 234881024 | bytes 2555908 | tf_op jit(solution)/shard_map/dot_general | solution.py:106
  53.3 1.7 %fusion.47 = f32[896,512]{1,0:T(8,128)} fusion(bf16[512,256]{1,0:T(8,128)(2,1)S(1)} %collective-permute-done.4, bf16[2048,896]{1,0:T(8,128)(2,1)S(1)} %copy-done.5, s32[]{:T(128)S(6)} %select_n.212), kind=kOutput, calls=%fused_computation.86 | convolution fusion | flops 234881024 | bytes 2555908 | tf_op jit(solution)/shard_map/dot_general | solution.py:106
  55.0 1.8 %fusion.31 = f32[896,512]{1,0:T(8,128)} fusion(bf16[512,256]{1,0:T(8,128)(2,1)S(1)} %collective-permute-done.4, bf16[2048,896]{1,0:T(8,128)(2,1)S(1)} %copy-done.4, s32[]{:T(128)S(6)} %select_n.212), kind=kOutput, calls=%fused_computation.70 | convolution fusion | flops 234881024 | bytes 2555908 | tf_op jit(solution)/shard_map/dot_general | solution.py:107
  57.3 1.7 %fusion.43 = f32[512,896]{0,1:T(8,128)} fusion(bf16[512,256]{1,0:T(8,128)(2,1)S(1)} %constant_dynamic-update-slice_fusion, bf16[2048,896]{1,0:T(8,128)(2,1)S(1)} %copy-done.5, s32[]{:T(128)S(6)} %select_n.218), kind=kOutput, calls=%fused_computation.82 | convolution fusion | flops 234881024 | bytes 2555908 | tf_op jit(solution)/shard_map/dot_general | solution.py:106
  59.0 1.7 %fusion.25 = f32[512,896]{0,1:T(8,128)} fusion(bf16[512,256]{1,0:T(8,128)(2,1)S(1)} %constant_dynamic-update-slice_fusion, bf16[2048,896]{1,0:T(8,128)(2,1)S(1)} %copy-done.4, s32[]{:T(128)S(6)} %select_n.218), kind=kOutput, calls=%fused_computation.66 | convolution fusion | flops 234881024 | bytes 2555908 | tf_op jit(solution)/shard_map/dot_general | solution.py:107
  61.1 0.7 copy-done.2
  61.7 6.2 %fusion.2 = bf16[512,896]{0,1:T(8,128)(2,1)S(1)} fusion(f32[512,896]{0,1:T(8,128)} %fusion.25, f32[896,512]{1,0:T(8,128)} %fusion.31, f32[512,896]{0,1:T(8,128)S(1)} %copy.21, f32[896,512]{1,0:T(8,128)} %fusion.33, f32[896,512]{1,0:T(8,128)S(1)} %fusion.35, f32[896,512]{1,0:T(8,128)S(1)} %fusion.37, f32[896,512]{1,0:T(8,128)S(1)} %copy-done.2, ...), kind=kOutput, calls=%fused_computation.3 | convolution fusion | flops 245432320 | bytes 32837636 | tf_op jit(solution)/shard_map/dot_general | solution.py:107
  68.3 1.6 %convolution_add_fusion.4 = f32[512,256]{1,0:T(8,128)S(1)} fusion(bf16[512,896]{0,1:T(8,128)(2,1)S(1)} %fusion.2, bf16[896,2048]{1,0:T(8,128)(2,1)} %param.14, s32[]{:T(128)S(6)} %select_n.215, f32[64,256]{1,0:T(8,128)S(1)} %copy-done.21, f32[512]{0:T(512)S(1)} %fusion.9), kind=kOutput, calls=%fused_computation.12 | convolution fusion | flops 235143168 | bytes 1968132 | tf_op jit(solution)/shard_map/dot_general | solution.py:158
  69.9 1.5 %fusion.4 = bf16[512,256]{1,0:T(8,128)(2,1)S(1)} fusion(bf16[512,896]{0,1:T(8,128)(2,1)S(1)} %fusion.2, bf16[896,2048]{1,0:T(8,128)(2,1)} %param.14, s32[]{:T(128)S(6)} %select_n.218, f32[64,256]{1,0:T(8,128)S(1)} %copy-done.20, f32[512]{0:T(512)S(1)} %fusion.9), kind=kOutput, calls=%fused_computation.16 | convolution fusion | flops 235274240 | bytes 1705988 | tf_op jit(solution)/shard_map/dot_general | solution.py:158
  71.5 1.8 %collective-permute-start.8 = (bf16[256,256]{1,0:T(8,128)(2,1)S(1)}, bf16[256,256]{1,0:T(8,128)(2,1)S(1)}, u32[]{:S(2)}, u32[]{:S(2)}) collective-permute-start(bf16[256,256]{1,0:T(8,128)(2,1)S(1)} %get-tuple-element.17), channel_id=1, source_target_pairs={{0,2},{2,4},{4,6},{6,7},{7,5},{5,3},{3,1},{1,0},{8,10},{10,12},{12... | collective-permute-start | bytes 393224 | tf_op jit(solution)/shard_map/ppermute | solution.py:163
  74.7 2.1 %collective-permute-done.8 = bf16[256,256]{1,0:T(8,128)(2,1)S(1)} collective-permute-done((bf16[256,256]{1,0:T(8,128)(2,1)S(1)}, bf16[256,256]{1,0:T(8,128)(2,1)S(1)}, u32[]{:S(2)}, u32[]{:S(2)}) %collective-permute-start.8) | collective-permute-done | bytes 131104 | tf_op jit(solution)/shard_map/ppermute | solution.py:163
  76.8 1.9 %collective-permute-start.9 = (bf16[512,256]{1,0:T(8,128)(2,1)S(1)}, bf16[512,256]{1,0:T(8,128)(2,1)S(1)}, u32[]{:S(2)}, u32[]{:S(2)}) collective-permute-start(bf16[512,256]{1,0:T(8,128)(2,1)S(1)} %pad_maximum_fusion.3), channel_id=1, source_target_pairs={{0,2},{2,4},{4,6},{6,7},{7,5},{5,3},{3,1},{1,0},{8,10},{10,12},{12... | collective-permute-start | bytes 786440 | tf_op jit(solution)/shard_map/ppermute | solution.py:174
  79.6 4.4 %collective-permute-done.9 = bf16[512,256]{1,0:T(8,128)(2,1)S(1)} collective-permute-done((bf16[512,256]{1,0:T(8,128)(2,1)S(1)}, bf16[512,256]{1,0:T(8,128)(2,1)S(1)}, u32[]{:S(2)}, u32[]{:S(2)}) %collective-permute-start.9) | collective-permute-done | bytes 262176 | tf_op jit(solution)/shard_map/ppermute | solution.py:174
  84.5 2.2 %collective-permute-start.10 = (bf16[512,256]{1,0:T(8,128)(2,1)S(1)}, bf16[512,256]{1,0:T(8,128)(2,1)S(1)}, u32[]{:S(2)}, u32[]{:S(2)}) collective-permute-start(bf16[512,256]{1,0:T(8,128)(2,1)S(1)} %add_convert_fusion.4), channel_id=1, source_target_pairs={{0,2},{2,4},{4,6},{6,7},{7,5},{5,3},{3,1},{1,0},{8,10},{10,12},{12... | collective-permute-start | bytes 786440 | tf_op jit(solution)/shard_map/ppermute | solution.py:174
  87.8 5.2 %collective-permute-done.10 = bf16[512,256]{1,0:T(8,128)(2,1)S(1)} collective-permute-done((bf16[512,256]{1,0:T(8,128)(2,1)S(1)}, bf16[512,256]{1,0:T(8,128)(2,1)S(1)}, u32[]{:S(2)}, u32[]{:S(2)}) %collective-permute-start.10) | collective-permute-done | bytes 262176 | tf_op jit(solution)/shard_map/ppermute | solution.py:174
  93.1 2.4 %collective-permute-start.11 = (bf16[512,256]{1,0:T(8,128)(2,1)S(1)}, bf16[512,256]{1,0:T(8,128)(2,1)S(1)}, u32[]{:S(2)}, u32[]{:S(2)}) collective-permute-start(bf16[512,256]{1,0:T(8,128)(2,1)S(1)} %add_convert_fusion.3), channel_id=1, source_target_pairs={{0,2},{2,4},{4,6},{6,7},{7,5},{5,3},{3,1},{1,0},{8,10},{10,12},{12... | collective-permute-start | bytes 786440 | tf_op jit(solution)/shard_map/ppermute | solution.py:174
  97.0 3.0 %collective-permute-done.11 = bf16[512,256]{1,0:T(8,128)(2,1)S(1)} collective-permute-done((bf16[512,256]{1,0:T(8,128)(2,1)S(1)}, bf16[512,256]{1,0:T(8,128)(2,1)S(1)}, u32[]{:S(2)}, u32[]{:S(2)}) %collective-permute-start.11) | collective-permute-done | bytes 262176 | tf_op jit(solution)/shard_map/ppermute | solution.py:174
  100.0 2.4 %collective-permute-done.15 = bf16[512,256]{1,0:T(8,128)(2,1)S(1)} collective-permute-done((bf16[512,256]{1,0:T(8,128)(2,1)S(1)}, bf16[512,256]{1,0:T(8,128)(2,1)S(1)}, u32[]{:S(2)}, u32[]{:S(2)}) %collective-permute-start.15) | collective-permute-done | bytes 262176 | tf_op jit(solution)/shard_map/ppermute | solution.py:175
  102.5 0.8 add_convert_fusion
  (112 shorter events, 12.4 us)
Async XLA Ops:
  0.6 67.3 %copy-start = (bf16[64,896]{1,0:T(8,128)(2,1)S(1)}, bf16[64,896]{1,0:T(8,128)(2,1)}, u32[]{:S(2)}) copy-start(bf16[64,896]{1,0:T(8,128)(2,1)} %param.19) | copy-start | bytes 344068
  0.6 9.2 %copy-start.8 = (bf16[64,2048]{1,0:T(8,128)(2,1)S(1)}, bf16[64,2048]{1,0:T(8,128)(2,1)}, u32[]{:S(2)}) copy-start(bf16[64,2048]{1,0:T(8,128)(2,1)} %param.15) | copy-start | bytes 786436
  0.7 10.7 %copy-start.9 = (bf16[64,2048]{1,0:T(8,128)(2,1)S(1)}, bf16[64,2048]{1,0:T(8,128)(2,1)}, u32[]{:S(2)}) copy-start(bf16[64,2048]{1,0:T(8,128)(2,1)} %param.17) | copy-start | bytes 786436
  0.7 9.2 %copy-start.11 = (f32[64,896]{1,0:T(8,128)S(1)}, f32[64,896]{1,0:T(8,128)}, u32[]{:S(2)}) copy-start(f32[64,896]{1,0:T(8,128)} %param.16) | copy-start | bytes 688132
  0.7 9.9 %copy-start.12 = (f32[64,896]{1,0:T(8,128)S(1)}, f32[64,896]{1,0:T(8,128)}, u32[]{:S(2)}) copy-start(f32[64,896]{1,0:T(8,128)} %param.18) | copy-start | bytes 688132
  0.7 28.7 %collective-permute-start = (bf16[512,256]{1,0:T(8,128)(2,1)}, bf16[512,256]{1,0:T(8,128)(2,1)S(1)}, u32[]{:S(2)}, u32[]{:S(2)}) collective-permute-start(bf16[512,256]{1,0:T(8,128)(2,1)} %param.11), channel_id=1, source_target_pairs={{0,2},{2,4},{4,6},{6,7},{7,5},{5,3},{3,1},{1,0},{8,10},{10,12},{12... | collective-permute-start | bytes 786440 | tf_op jit(solution)/shard_map/ppermute | solution.py:118
  3.8 29.4 %collective-permute-start.1 = (bf16[512,256]{1,0:T(8,128)(2,1)}, bf16[512,256]{1,0:T(8,128)(2,1)S(1)}, u32[]{:S(2)}, u32[]{:S(2)}) collective-permute-start(bf16[512,256]{1,0:T(8,128)(2,1)} %param.11), channel_id=1, source_target_pairs={{2,0},{4,2},{6,4},{7,6},{5,7},{3,5},{1,3},{0,1},{10,8},{12,10},{14... | collective-permute-start | bytes 786440 | tf_op jit(solution)/shard_map/ppermute | solution.py:119
  3.8 7.6 %copy-start.6 = (bf16[512,256]{1,0:T(8,128)(2,1)S(1)}, bf16[512,256]{1,0:T(8,128)(2,1)}, u32[]{:S(2)}) copy-start(bf16[512,256]{1,0:T(8,128)(2,1)} %param.11) | copy-start | bytes 786436
  5.7 22.0 %collective-permute-start.16 = (bf16[2,64,1024]{2,1,0:T(8,128)(2,1)}, bf16[2,64,1024]{2,1,0:T(8,128)(2,1)}, u32[]{:S(2)}, u32[]{:S(2)}) collective-permute-start(bf16[2,64,1024]{2,1,0:T(8,128)(2,1)} %get-tuple-element.7), channel_id=1, source_target_pairs={{0,16},{8,24},{16,0},{24,8},{1,17},{9,25},{17,1},{25,9},{2,18},{10... | collective-permute-start | bytes 786440 | tf_op jit(solution)/shard_map/ppermute | solution.py:69
  9.5 17.0 %collective-permute-start.18 = (bf16[64,1792]{1,0:T(8,128)(2,1)S(1)}, bf16[64,1792]{1,0:T(8,128)(2,1)}, u32[]{:S(2)}, u32[]{:S(2)}) collective-permute-start(bf16[64,1792]{1,0:T(8,128)(2,1)S(1)} %fusion.12), channel_id=1, source_target_pairs={{0,16},{8,24},{16,0},{24,8},{1,17},{9,25},{17,1},{25,9},{2,18},{10... | collective-permute-start | bytes 688136 | tf_op jit(solution)/shard_map/ppermute | solution.py:68
  15.0 2.8 %copy-start.14 = (f32[64,896]{1,0:T(8,128)S(1)}, f32[64,896]{1,0:T(8,128)}, u32[]{:S(2)}) copy-start(f32[64,896]{1,0:T(8,128)} %broadcast_multiply_fusion.1) | copy-start | bytes 688132
  15.0 2.9 %copy-start.13 = (f32[64,896]{1,0:T(8,128)S(1)}, f32[64,896]{1,0:T(8,128)}, u32[]{:S(2)}) copy-start(f32[64,896]{1,0:T(8,128)} %broadcast_multiply_fusion) | copy-start | bytes 688132
  24.7 3.1 %copy-start.7 = (bf16[2,64,1024]{2,1,0:T(8,128)(2,1)S(1)}, bf16[2,64,1024]{2,1,0:T(8,128)(2,1)}, u32[]{:S(2)}) copy-start(bf16[2,64,1024]{2,1,0:T(8,128)(2,1)} %get-tuple-element.8) | copy-start | bytes 786436
  26.5 6.1 %copy-start.4 = (bf16[2048,896]{1,0:T(8,128)(2,1)S(1)}, bf16[2048,896]{1,0:T(8,128)(2,1)}, u32[]{:S(2)}) copy-start(bf16[2048,896]{1,0:T(8,128)(2,1)} %param.13) | copy-start | bytes 11010052
  27.7 17.8 %collective-permute-start.19 = (bf16[128,1792]{1,0:T(8,128)(2,1)S(1)}, bf16[128,1792]{1,0:T(8,128)(2,1)S(1)}, u32[]{:S(2)}, u32[]{:S(2)}) collective-permute-start(bf16[128,1792]{1,0:T(8,128)(2,1)S(1)} %pad_maximum_fusion.1), channel_id=1, source_target_pairs={{0,8},{8,0},{16,24},{24,16},{1,9},{9,1},{17,25},{25,17},{2,10},{10... | collective-permute-start | bytes 1376264 | tf_op jit(solution)/shard_map/ppermute | solution.py:76
  28.8 17.7 %collective-permute-start.17 = (bf16[2,128,512]{2,1,0:T(8,128)(2,1)S(1)}, bf16[2,128,512]{2,1,0:T(8,128)(2,1)S(1)}, u32[]{:S(2)}, u32[]{:S(2)}) collective-permute-start(bf16[2,128,512]{2,1,0:T(8,128)(2,1)S(1)} %get-tuple-element.5), channel_id=1, source_target_pairs={{0,8},{8,0},{16,24},{24,16},{1,9},{9,1},{17,25},{25,17},{2,10},{10... | collective-permute-start | bytes 786440 | tf_op jit(solution)/shard_map/ppermute | solution.py:77
  29.3 8.3 %collective-permute-start.2 = (bf16[512,256]{1,0:T(8,128)(2,1)S(1)}, bf16[512,256]{1,0:T(8,128)(2,1)S(1)}, u32[]{:S(2)}, u32[]{:S(2)}) collective-permute-start(bf16[512,256]{1,0:T(8,128)(2,1)S(1)} %collective-permute-done), channel_id=1, source_target_pairs={{0,2},{2,4},{4,6},{6,7},{7,5},{5,3},{3,1},{1,0},{8,10},{10,12},{12... | collective-permute-start | bytes 786440 | tf_op jit(solution)/shard_map/ppermute | solution.py:118
  33.1 1.7 %copy-start.10 = (f32[128,512]{1,0:T(8,128)S(1)}, f32[128,512]{1,0:T(8,128)}, u32[]{:S(2)}) copy-start(f32[128,512]{1,0:T(8,128)} %fusion.83) | copy-start | bytes 786436
  33.2 8.1 %collective-permute-start.3 = (bf16[512,256]{1,0:T(8,128)(2,1)S(1)}, bf16[512,256]{1,0:T(8,128)(2,1)S(1)}, u32[]{:S(2)}, u32[]{:S(2)}) collective-permute-start(bf16[512,256]{1,0:T(8,128)(2,1)S(1)} %collective-permute-done.1), channel_id=1, source_target_pairs={{2,0},{4,2},{6,4},{7,6},{5,7},{3,5},{1,3},{0,1},{10,8},{12,10},{14... | collective-permute-start | bytes 786440 | tf_op jit(solution)/shard_map/ppermute | solution.py:119
  34.9 4.6 %copy-start.5 = (bf16[2048,896]{1,0:T(8,128)(2,1)S(1)}, bf16[2048,896]{1,0:T(8,128)(2,1)}, u32[]{:S(2)}) copy-start(bf16[2048,896]{1,0:T(8,128)(2,1)} %param.12) | copy-start | bytes 11010052
  37.6 11.6 %collective-permute-start.4 = (bf16[512,256]{1,0:T(8,128)(2,1)S(1)}, bf16[512,256]{1,0:T(8,128)(2,1)S(1)}, u32[]{:S(2)}, u32[]{:S(2)}) collective-permute-start(bf16[512,256]{1,0:T(8,128)(2,1)S(1)} %collective-permute-done.2), channel_id=1, source_target_pairs={{0,2},{2,4},{4,6},{6,7},{7,5},{5,3},{3,1},{1,0},{8,10},{10,12},{12... | collective-permute-start | bytes 786440 | tf_op jit(solution)/shard_map/ppermute | solution.py:118
  41.2 9.9 %collective-permute-start.5 = (bf16[512,256]{1,0:T(8,128)(2,1)S(1)}, bf16[512,256]{1,0:T(8,128)(2,1)S(1)}, u32[]{:S(2)}, u32[]{:S(2)}) collective-permute-start(bf16[512,256]{1,0:T(8,128)(2,1)S(1)} %collective-permute-done.3), channel_id=1, source_target_pairs={{2,0},{4,2},{6,4},{7,6},{5,7},{3,5},{1,3},{0,1},{10,8},{12,10},{14... | collective-permute-start | bytes 786440 | tf_op jit(solution)/shard_map/ppermute | solution.py:119
  49.3 7.8 %collective-permute-start.6 = (bf16[256,256]{1,0:T(8,128)(2,1)S(1)}, bf16[256,256]{1,0:T(8,128)(2,1)S(1)}, u32[]{:S(2)}, u32[]{:S(2)}) collective-permute-start(bf16[256,256]{1,0:T(8,128)(2,1)S(1)} %slice.58), channel_id=1, source_target_pairs={{0,2},{2,4},{4,6},{6,7},{7,5},{5,3},{3,1},{1,0},{8,10},{10,12},{12... | collective-permute-start | bytes 393224 | tf_op jit(solution)/shard_map/ppermute | solution.py:125
  51.1 6.0 %collective-permute-start.7 = (bf16[256,256]{1,0:T(8,128)(2,1)S(1)}, bf16[256,256]{1,0:T(8,128)(2,1)S(1)}, u32[]{:S(2)}, u32[]{:S(2)}) collective-permute-start(bf16[256,256]{1,0:T(8,128)(2,1)S(1)} %slice.59), channel_id=1, source_target_pairs={{2,0},{4,2},{6,4},{7,6},{5,7},{3,5},{1,3},{0,1},{10,8},{12,10},{14... | collective-permute-start | bytes 393224 | tf_op jit(solution)/shard_map/ppermute | solution.py:126
  57.3 3.7 %copy-start.3 = (f32[896,512]{1,0:T(8,128)S(1)}, f32[896,512]{1,0:T(8,128)}, u32[]{:S(2)}) copy-start(f32[896,512]{1,0:T(8,128)} %fusion.57) | copy-start | bytes 5505028
  59.0 1.9 %copy-start.22 = (s32[512]{0:T(512)S(1)}, s32[512]{0:T(512)}, u32[]{:S(2)}) copy-start(s32[512]{0:T(512)} %broadcast_add_fusion) | copy-start | bytes 6148
  59.0 2.0 %copy-start.23 = (s32[512]{0:T(512)S(1)}, s32[512]{0:T(512)}, u32[]{:S(2)}) copy-start(s32[512]{0:T(512)} %iota_shift-right-logical_fusion) | copy-start | bytes 6148
  59.0 2.0 %copy-start.24 = (pred[512]{0:T(512)(128)(4,1)S(1)}, pred[512]{0:T(512)(128)(4,1)}, u32[]{:S(2)}) copy-start(pred[512]{0:T(512)(128)(4,1)} %fusion.119) | copy-start | bytes 1540
  59.0 2.0 %copy-start.1 = (f32[512,896]{0,1:T(8,128)S(1)}, f32[512,896]{0,1:T(8,128)}, u32[]{:S(2)}) copy-start(f32[512,896]{0,1:T(8,128)} %copy.19) | copy-start | bytes 5505028
  59.0 2.7 %copy-start.2 = (f32[896,512]{1,0:T(8,128)S(1)}, f32[896,512]{1,0:T(8,128)}, u32[]{:S(2)}) copy-start(f32[896,512]{1,0:T(8,128)} %fusion.41) | copy-start | bytes 5505028
  61.7 6.5 %copy-start.21 = (f32[64,256]{1,0:T(8,128)S(1)}, f32[64,256]{1,0:T(8,128)}, u32[]{:S(2)}) copy-start(f32[64,256]{1,0:T(8,128)} %get-tuple-element.12) | copy-start | bytes 196612
  67.9 2.0 %copy-start.20 = (f32[64,256]{1,0:T(8,128)S(1)}, f32[64,256]{1,0:T(8,128)}, u32[]{:S(2)}) copy-start(f32[64,256]{1,0:T(8,128)} %get-tuple-element.11) | copy-start | bytes 196612
  68.2 5.1 %copy-start.25 = (bf16[896,2048]{1,0:T(8,128)(2,1)S(1)}, bf16[896,2048]{1,0:T(8,128)(2,1)}, u32[]{:S(2)}) copy-start(bf16[896,2048]{1,0:T(8,128)(2,1)} %param.14) | copy-start | bytes 11010052
  69.9 3.4 %copy-start.19 = (f32[64,256]{1,0:T(8,128)S(1)}, f32[64,256]{1,0:T(8,128)}, u32[]{:S(2)}) copy-start(f32[64,256]{1,0:T(8,128)} %get-tuple-element.13) | copy-start | bytes 196612
  71.5 2.7 %copy-start.18 = (f32[64,256]{1,0:T(8,128)S(1)}, f32[64,256]{1,0:T(8,128)}, u32[]{:S(2)}) copy-start(f32[64,256]{1,0:T(8,128)} %get-tuple-element.15) | copy-start | bytes 196612
  71.5 5.3 %collective-permute-start.8 = (bf16[256,256]{1,0:T(8,128)(2,1)S(1)}, bf16[256,256]{1,0:T(8,128)(2,1)S(1)}, u32[]{:S(2)}, u32[]{:S(2)}) collective-permute-start(bf16[256,256]{1,0:T(8,128)(2,1)S(1)} %get-tuple-element.17), channel_id=1, source_target_pairs={{0,2},{2,4},{4,6},{6,7},{7,5},{5,3},{3,1},{1,0},{8,10},{10,12},{12... | collective-permute-start | bytes 393224 | tf_op jit(solution)/shard_map/ppermute | solution.py:163
  73.8 5.4 %collective-permute-start.12 = (bf16[256,256]{1,0:T(8,128)(2,1)S(1)}, bf16[256,256]{1,0:T(8,128)(2,1)S(1)}, u32[]{:S(2)}, u32[]{:S(2)}) collective-permute-start(bf16[256,256]{1,0:T(8,128)(2,1)S(1)} %get-tuple-element.18), channel_id=1, source_target_pairs={{2,0},{4,2},{6,4},{7,6},{5,7},{3,5},{1,3},{0,1},{10,8},{12,10},{14... | collective-permute-start | bytes 393224 | tf_op jit(solution)/shard_map/ppermute | solution.py:164
  74.1 9.8 %copy-start.17 = (f32[64,256]{1,0:T(8,128)S(1)}, f32[64,256]{1,0:T(8,128)}, u32[]{:S(2)}) copy-start(f32[64,256]{1,0:T(8,128)} %get-tuple-element.9) | copy-start | bytes 196612
  76.8 9.9 %copy-start.16 = (f32[64,256]{1,0:T(8,128)S(1)}, f32[64,256]{1,0:T(8,128)}, u32[]{:S(2)}) copy-start(f32[64,256]{1,0:T(8,128)} %get-tuple-element.16) | copy-start | bytes 196612
  76.8 7.2 %collective-permute-start.9 = (bf16[512,256]{1,0:T(8,128)(2,1)S(1)}, bf16[512,256]{1,0:T(8,128)(2,1)S(1)}, u32[]{:S(2)}, u32[]{:S(2)}) collective-permute-start(bf16[512,256]{1,0:T(8,128)(2,1)S(1)} %pad_maximum_fusion.3), channel_id=1, source_target_pairs={{0,2},{2,4},{4,6},{6,7},{7,5},{5,3},{3,1},{1,0},{8,10},{10,12},{12... | collective-permute-start | bytes 786440 | tf_op jit(solution)/shard_map/ppermute | solution.py:174
  79.2 7.4 %collective-permute-start.13 = (bf16[512,256]{1,0:T(8,128)(2,1)S(1)}, bf16[512,256]{1,0:T(8,128)(2,1)S(1)}, u32[]{:S(2)}, u32[]{:S(2)}) collective-permute-start(bf16[512,256]{1,0:T(8,128)(2,1)S(1)} %pad_maximum_fusion.4), channel_id=1, source_target_pairs={{2,0},{4,2},{6,4},{7,6},{5,7},{3,5},{1,3},{0,1},{10,8},{12,10},{14... | collective-permute-start | bytes 786440 | tf_op jit(solution)/shard_map/ppermute | solution.py:175
  84.5 2.9 %copy-start.15 = (f32[64,256]{1,0:T(8,128)S(1)}, f32[64,256]{1,0:T(8,128)}, u32[]{:S(2)}) copy-start(f32[64,256]{1,0:T(8,128)} %get-tuple-element.10) | copy-start | bytes 196612
  84.5 8.6 %collective-permute-start.10 = (bf16[512,256]{1,0:T(8,128)(2,1)S(1)}, bf16[512,256]{1,0:T(8,128)(2,1)S(1)}, u32[]{:S(2)}, u32[]{:S(2)}) collective-permute-start(bf16[512,256]{1,0:T(8,128)(2,1)S(1)} %add_convert_fusion.4), channel_id=1, source_target_pairs={{0,2},{2,4},{4,6},{6,7},{7,5},{5,3},{3,1},{1,0},{8,10},{10,12},{12... | collective-permute-start | bytes 786440 | tf_op jit(solution)/shard_map/ppermute | solution.py:174
  87.2 8.8 %collective-permute-start.14 = (bf16[512,256]{1,0:T(8,128)(2,1)S(1)}, bf16[512,256]{1,0:T(8,128)(2,1)S(1)}, u32[]{:S(2)}, u32[]{:S(2)}) collective-permute-start(bf16[512,256]{1,0:T(8,128)(2,1)S(1)} %add_convert_fusion.2), channel_id=1, source_target_pairs={{2,0},{4,2},{6,4},{7,6},{5,7},{3,5},{1,3},{0,1},{10,8},{12,10},{14... | collective-permute-start | bytes 786440 | tf_op jit(solution)/shard_map/ppermute | solution.py:175
  93.1 6.9 %collective-permute-start.11 = (bf16[512,256]{1,0:T(8,128)(2,1)S(1)}, bf16[512,256]{1,0:T(8,128)(2,1)S(1)}, u32[]{:S(2)}, u32[]{:S(2)}) collective-permute-start(bf16[512,256]{1,0:T(8,128)(2,1)S(1)} %add_convert_fusion.3), channel_id=1, source_target_pairs={{0,2},{2,4},{4,6},{6,7},{7,5},{5,3},{3,1},{1,0},{8,10},{10,12},{12... | collective-permute-start | bytes 786440 | tf_op jit(solution)/shard_map/ppermute | solution.py:174
  96.0 6.4 %collective-permute-start.15 = (bf16[512,256]{1,0:T(8,128)(2,1)S(1)}, bf16[512,256]{1,0:T(8,128)(2,1)S(1)}, u32[]{:S(2)}, u32[]{:S(2)}) collective-permute-start(bf16[512,256]{1,0:T(8,128)(2,1)S(1)} %add_convert_fusion.1), channel_id=1, source_target_pairs={{2,0},{4,2},{6,4},{7,6},{5,7},{3,5},{1,3},{0,1},{10,8},{12,10},{14... | collective-permute-start | bytes 786440 | tf_op jit(solution)/shard_map/ppermute | solution.py:175

commit v2 on v1

--- a/solution.py
+++ b/solution.py
@@ -3,6 +3,8 @@
 import jax
 import jax.numpy as jnp
 from jax import lax
+from jax.experimental import pallas as pl
+from jax.experimental.pallas import tpu as pltpu
 from jax.sharding import PartitionSpec as P
 
 noise_scale = 0.5
@@ -21,7 +23,7 @@
     return jnp.where(place < n // 2, 2 * place, 2 * (n - 1 - place) + 1)
 
 
-def per_device(
+def plain_device(
     tokens,
     gate_weight,
     up_weight,
@@ -178,6 +180,350 @@
     return mixed.astype(jnp.bfloat16), gate_step, up_step
 
 
+MIB = 1 << 20
+
+
+def dims(lhs, rhs):
+    return (((lhs,), (rhs,)), ((), ()))
+
+
+def message_kernel(at, fit, gate_r, up_r, gate_far, up_far, gate_near, up_near, far, near):
+    cols = gate_r.shape[1]
+    block = gate_far.shape[1]
+    weight = fit[...]
+    gate_fit = (weight * gate_r[...]).astype(jnp.bfloat16)
+    up_fit = (weight * up_r[...]).astype(jnp.bfloat16)
+    for out, gate_l, up_l in ((far, gate_far, up_far), (near, gate_near, up_near)):
+        out[:, :cols] = gate_fit
+        out[:, cols : 2 * cols] = up_fit
+        out[:, 2 * cols : 2 * cols + block] = gate_l[...]
+        out[:, 2 * cols + block :] = up_l[...]
+
+
+def messages(at, fit, gate_right, up_right, gate_left, up_left, slot_far, slot_near):
+    members, cols = gate_right.shape
+    half_width = gate_left.shape[1] // 2
+    shape = jax.ShapeDtypeStruct((members, 2 * cols + 2 * half_width), jnp.bfloat16)
+    whole = lambda a: pl.BlockSpec(a.shape, lambda i, at: (0, 0))
+    far = pl.BlockSpec((members, half_width), lambda i, at: (0, at[slot_far]))
+    near = pl.BlockSpec((members, half_width), lambda i, at: (0, at[slot_near]))
+    return pl.pallas_call(
+        message_kernel,
+        out_shape=(shape, shape),
+        grid_spec=pltpu.PrefetchScalarGridSpec(
+            num_scalar_prefetch=1,
+            grid=(1,),
+            in_specs=[whole(fit), whole(gate_right), whole(up_right), far, far, near, near],
+            out_specs=[whole(shape), whole(shape)],
+        ),
+        compiler_params=pltpu.CompilerParams(vmem_limit_bytes=16 * MIB),
+        cost_estimate=pl.CostEstimate(flops=10**6, bytes_accessed=2 * 10**6, transcendentals=0),
+        name="messages",
+    )(at, fit, gate_right, up_right, gate_left, up_left, gate_left, up_left)
+
+
+def outer_kernel(slot, scale, at, a, b, c, d, gate_out, up_out):
+    rows = gate_out.shape[0]
+    cols = gate_out.shape[1]
+    parts = (a, b, c, d)
+    start = pl.multiple_of(2 * cols + at[slot] * rows, 128)
+    for out, shift, right_at in ((gate_out, 0, 0), (up_out, 2 * rows, cols)):
+        left = jnp.concatenate([p[:, pl.ds(start + shift, rows)] for p in parts], axis=0)
+        right = jnp.concatenate([p[:, right_at : right_at + cols] for p in parts], axis=0)
+        total = lax.dot_general(left, right, dims(0, 0), preferred_element_type=jnp.float32)
+        out[...] = (scale * total).astype(out.dtype)
+
+
+def outers(at, parts, rows, cols, slot, scale):
+    shape = jax.ShapeDtypeStruct((rows, cols), jnp.bfloat16)
+    whole = lambda a: pl.BlockSpec(a.shape, lambda i, at: (0, 0))
+    return pl.pallas_call(
+        lambda *refs: outer_kernel(slot, scale, *refs),
+        out_shape=(shape, shape),
+        grid_spec=pltpu.PrefetchScalarGridSpec(
+            num_scalar_prefetch=1,
+            grid=(1,),
+            in_specs=[whole(p) for p in parts],
+            out_specs=[whole(shape), whole(shape)],
+        ),
+        compiler_params=pltpu.CompilerParams(vmem_limit_bytes=24 * MIB),
+        cost_estimate=pl.CostEstimate(flops=10**9, bytes_accessed=6 * 10**6, transcendentals=0),
+        name="outers",
+    )(at, *parts)
+
+
+def grow_kernel(count, fresh, at, *refs):
+    pieces = refs[:count]
+    gate_w, up_w, gate_l, up_l = refs[count : count + 4]
+    old = () if fresh else refs[count + 4 : count + 7]
+    gate, up, scores = refs[-3:]
+    step = pl.program_id(0)
+    for j, piece_ref in enumerate(pieces):
+
+        @pl.when(step == j)
+        def _(j=j, piece_ref=piece_ref):
+            piece = piece_ref[...]
+            left = jnp.concatenate([gate_l[...], up_l[...]], axis=0)
+            new_g = jnp.dot(piece, gate_w[...], preferred_element_type=jnp.float32)
+            new_u = jnp.dot(piece, up_w[...], preferred_element_type=jnp.float32)
+            new_s = lax.dot_general(piece, left, dims(1, 1), preferred_element_type=jnp.float32)
+            if j == 0 and fresh:
+                gate[...], up[...], scores[...] = new_g, new_u, new_s
+            elif j == 0:
+                gate[...] = old[0][...] + new_g
+                up[...] = old[1][...] + new_u
+                scores[...] = old[2][...] + new_s
+            else:
+                gate[...] += new_g
+                up[...] += new_u
+                scores[...] += new_s
+
+
+def grow(at, pieces, slots, gate_weight, up_weight, gate_left, up_left, total):
+    rows, span = pieces[0].shape
+    cols = gate_weight.shape[1]
+    members = gate_left.shape[0]
+    count = len(pieces)
+
+    def pick(i, at):
+        slot = jnp.int32(slots[0])
+        for j in range(1, count):
+            slot = jnp.where(i == j, slots[j], slot)
+        return at[slot]
+
+    whole = lambda a: pl.BlockSpec(a.shape, lambda i, at: (0, 0))
+    weight = pl.BlockSpec((span, cols), lambda i, at: (pick(i, at), 0))
+    left = pl.BlockSpec((members, span), lambda i, at: (0, pick(i, at)))
+    shapes = (
+        jax.ShapeDtypeStruct((rows, cols), jnp.float32),
+        jax.ShapeDtypeStruct((rows, cols), jnp.float32),
+        jax.ShapeDtypeStruct((rows, 2 * members), jnp.float32),
+    )
+    old = [] if total is None else list(total)
+    return pl.pallas_call(
+        lambda *refs: grow_kernel(count, total is None, *refs),
+        out_shape=shapes,
+        grid_spec=pltpu.PrefetchScalarGridSpec(
+            num_scalar_prefetch=1,
+            grid=(count,),
+            in_specs=[whole(p) for p in pieces] + [weight, weight, left, left] + [whole(o) for o in old],
+            out_specs=[whole(s) for s in shapes],
+        ),
+        compiler_params=pltpu.CompilerParams(vmem_limit_bytes=32 * MIB),
+        cost_estimate=pl.CostEstimate(
+            flops=count * 2 * rows * span * 2 * cols,
+            bytes_accessed=count * span * cols * 4 + 4 * rows * cols * 2 * (1 + len(old) // 3),
+            transcendentals=0,
+        ),
+        name="grow",
+    )(at, *pieces, gate_weight, up_weight, gate_left, up_left, *old)
+
+
+def spread_rows(score, right, per_member):
+    members, cols = right.shape
+    wide = jnp.broadcast_to(right[:, None, :], (members, per_member, cols))
+    return score * wide.reshape(members * per_member, cols)
+
+
+def hidden_kernel(
+    per_member, at, gate_sum, up_sum, scores, top, bottom, gate_w, up_w, gate_l, up_l,
+    gate_r, up_r, down_l, down_w, down_r, hidden_out, score_out, share_out,
+):
+    step = pl.program_id(0)
+    steps = pl.num_programs(0)
+    rows = gate_sum.shape[0]
+    members = gate_l.shape[0]
+    local = gate_r.shape[0]
+    piece = jnp.where(step < steps // 2, top[...], bottom[...])
+    left = jnp.concatenate([gate_l[...], up_l[...]], axis=0)
+    score = scores[...] + lax.dot_general(piece, left, dims(1, 1), preferred_element_type=jnp.float32)
+    member = lax.broadcasted_iota(jnp.int32, (rows, 2 * members), 0) // per_member + step * local
+    column = lax.broadcasted_iota(jnp.int32, (rows, 2 * members), 1)
+    gate_score = jnp.sum(jnp.where(column == member, score, 0.0), axis=1, keepdims=True)
+    up_score = jnp.sum(jnp.where(column == member + members, score, 0.0), axis=1, keepdims=True)
+    gate = gate_sum[...] + jnp.dot(piece, gate_w[...], preferred_element_type=jnp.float32)
+    up = up_sum[...] + jnp.dot(piece, up_w[...], preferred_element_type=jnp.float32)
+    gate = gate + spread_rows(noise_scale * gate_score, gate_r[...], per_member)
+    up = up + spread_rows(noise_scale * up_score, up_r[...], per_member)
+    hidden = (silu(gate) * up).astype(jnp.bfloat16)
+    hidden_out[...] = hidden
+    down = lax.dot_general(hidden, down_l[...], dims(1, 1), preferred_element_type=jnp.float32)
+    down = jnp.where(column[:, :members] == member[:, :members], down, 0.0)
+    down_score = noise_scale * jnp.sum(down, axis=1, keepdims=True)
+    score_out[...] = jnp.broadcast_to(down_score, score_out.shape)
+    share = jnp.dot(hidden, down_w[...], preferred_element_type=jnp.float32)
+    share_out[...] = (share + spread_rows(down_score, down_r[...], per_member)).astype(share_out.dtype)
+
+
+def finish(at, total, top, bottom, gate_weight, up_weight, gate_left, up_left, gate_right, up_right,
+           down_left, down_weight, down_right, slot, wire):
+    rows, cols = total[0].shape
+    span = top.shape[1]
+    members = gate_left.shape[0]
+    per_member = rows // members
+    steps = 4
+    tall = rows // steps
+    local = members // steps
+    row = lambda width: pl.BlockSpec((tall, width), lambda i, at: (i, 0))
+    whole = lambda a: pl.BlockSpec(a.shape, lambda i, at: (0, 0))
+    weight = pl.BlockSpec((span, cols), lambda i, at: (at[slot], 0))
+    left = pl.BlockSpec((members, span), lambda i, at: (0, at[slot]))
+    return pl.pallas_call(
+        lambda *refs: hidden_kernel(per_member, *refs),
+        out_shape=(
+            jax.ShapeDtypeStruct((rows, cols), jnp.bfloat16),
+            jax.ShapeDtypeStruct((rows, 128), jnp.float32),
+            jax.ShapeDtypeStruct((rows, span), wire),
+        ),
+        grid_spec=pltpu.PrefetchScalarGridSpec(
+            num_scalar_prefetch=1,
+            grid=(steps,),
+            in_specs=[
+                row(cols), row(cols), row(2 * members),
+                pl.BlockSpec((tall, span), lambda i, at: (jnp.minimum(i, steps // 2 - 1), 0)),
+                pl.BlockSpec((tall, span), lambda i, at: (jnp.maximum(i - steps // 2, 0), 0)),
+                weight, weight, left, left,
+                pl.BlockSpec((local, cols), lambda i, at: (i, 0)),
+                pl.BlockSpec((local, cols), lambda i, at: (i, 0)),
+                whole(down_left),
+                pl.BlockSpec((cols, span), lambda i, at: (0, at[slot])),
+                pl.BlockSpec((local, span), lambda i, at: (i, at[slot])),
+            ],
+            out_specs=[row(cols), row(128), row(span)],
+        ),
+        compiler_params=pltpu.CompilerParams(vmem_limit_bytes=24 * MIB),
+        cost_estimate=pl.CostEstimate(
+            flops=2 * rows * span * cols * 3, bytes_accessed=6 * 10**6, transcendentals=rows * cols
+        ),
+        name="finish",
+    )(at, *total, top, bottom, gate_weight, up_weight, gate_left, up_left, gate_right, up_right,
+      down_left, down_weight, down_right)
+
+
+def share_kernel(per_member, at, hidden, score, down_w, down_r, out):
+    total = jnp.dot(hidden[...], down_w[...], preferred_element_type=jnp.float32)
+    out[...] = total + spread_rows(score[...][:, :1], down_r[...], per_member)
+
+
+def shares(at, hidden, score, down_weight, down_right, slots, span):
+    rows, cols = hidden.shape
+    members = down_right.shape[0]
+    count = len(slots)
+
+    def pick(j, at):
+        slot = jnp.int32(slots[0])
+        for i in range(1, count):
+            slot = jnp.where(j == i, slots[i], slot)
+        return at[slot]
+
+    whole = lambda a: pl.BlockSpec(a.shape, lambda j, at: (0, 0))
+    return pl.pallas_call(
+        lambda *refs: share_kernel(rows // members, *refs),
+        out_shape=jax.ShapeDtypeStruct((count, rows, span), jnp.float32),
+        grid_spec=pltpu.PrefetchScalarGridSpec(
+            num_scalar_prefetch=1,
+            grid=(count,),
+            in_specs=[
+                whole(hidden), whole(score),
+                pl.BlockSpec((cols, span), lambda j, at: (0, pick(j, at))),
+                pl.BlockSpec((members, span), lambda j, at: (0, pick(j, at))),
+            ],
+            out_specs=pl.BlockSpec((None, rows, span), lambda j, at: (j, 0, 0)),
+        ),
+        compiler_params=pltpu.CompilerParams(vmem_limit_bytes=16 * MIB),
+        cost_estimate=pl.CostEstimate(
+            flops=2 * rows * span * cols * count,
+            bytes_accessed=count * span * (2 * cols + 4 * rows),
+            transcendentals=0,
+        ),
+        name="shares",
+    )(at, hidden, score, down_weight, down_right)
+
+
+def per_device(
+    tokens,
+    gate_weight,
+    up_weight,
+    down_weight,
+    gate_left,
+    gate_right,
+    up_left,
+    up_right,
+    down_left,
+    down_right,
+    fitness_rank,
+):
+    arguments = (tokens, gate_weight, up_weight, down_weight, gate_left, gate_right, up_left,
+                 up_right, down_left, down_right, fitness_rank)
+    members, width = gate_left.shape
+    rows, span = tokens.shape
+    hidden_cols = gate_weight.shape[1]
+    n = lax.axis_size("wsh")
+    groups = lax.axis_size("grp")
+    if n != 8 or groups != 4 or span % 128 or hidden_cols % 128:
+        return plain_device(*arguments)
+    total_members = members * groups
+    hops = n // 2
+    half = rows // 2
+    wire = jnp.bfloat16
+
+    order = [2 * q for q in range(hops)] + [2 * (n - 1 - q) + 1 for q in range(hops, n)]
+    onward = [(order[q], order[(q + 1) % n]) for q in range(n)]
+    back = [(b, a) for a, b in onward]
+    place = ring_place(lax.axis_index("wsh"), n)
+    grp = lax.axis_index("grp")
+    at = jnp.concatenate([
+        ring_owner(place + jnp.arange(n, dtype=jnp.int32), n),
+        jnp.stack([grp // 2, 1 - grp // 2, grp % 2]),
+    ]).astype(jnp.int32)
+    slot_near, slot_far, slot_core = n, n + 1, n + 2
+
+    pair = [(g, g ^ 2) for g in range(4)]
+    mate = [(g, g ^ 1) for g in range(4)]
+
+    one_a = lax.ppermute(tokens, "wsh", onward)
+    one_b = lax.ppermute(tokens, "wsh", back)
+    weight_fit = (2.0 * fitness_rank.astype(jnp.float32) - (total_members - 1)) / (
+        total_members - 1
+    )
+    far, near = messages(at, weight_fit[:, None], gate_right, up_right, gate_left, up_left, slot_far, slot_near)
+    far_in = lax.ppermute(far, "grp", pair)
+    near_in = lax.ppermute(near, "grp", mate)
+    far_mate = lax.ppermute(far_in, "grp", mate)
+
+    two_a = lax.ppermute(one_a, "wsh", onward)
+    two_b = lax.ppermute(one_b, "wsh", back)
+    three_a = lax.ppermute(two_a, "wsh", onward)
+    three_b = lax.ppermute(two_b, "wsh", back)
+    weights = (gate_weight, up_weight, gate_left, up_left)
+    total = grow(at, [tokens, one_a, one_b, two_a, two_b], [0, n - 1, 1, n - 2, 2], *weights, None)
+    top = lax.ppermute(three_a[:half], "wsh", onward)
+    bottom = lax.ppermute(three_b[half:], "wsh", back)
+    total = grow(at, [three_a, three_b], [n - 3, 3], *weights, total)
+    hidden, score, opposite = finish(
+        at, total, top, bottom, *weights, gate_right, up_right, down_left, down_weight, down_right, hops, wire
+    )
+    got_on = lax.ppermute(opposite[:half], "wsh", onward)
+    got_back = lax.ppermute(opposite[half:], "wsh", back)
+    rest = shares(at, hidden, score, down_weight, down_right, [3, n - 3, 2, n - 2, 1, n - 1, 0], span)
+    wide = lambda a: a.astype(jnp.float32)
+    for hop in range(hops - 1, 0, -1):
+        ahead = rest[2 * (hops - 1 - hop)]
+        behind = rest[2 * (hops - 1 - hop) + 1]
+        if hop == hops - 1:
+            ahead = jnp.concatenate([ahead[:half] + wide(got_on), ahead[half:]], axis=0)
+            behind = jnp.concatenate([behind[:half], behind[half:] + wide(got_back)], axis=0)
+        else:
+            ahead = ahead + wide(got_on)
+            behind = behind + wide(got_back)
+        got_on = lax.ppermute(ahead.astype(wire), "wsh", onward)
+        got_back = lax.ppermute(behind.astype(wire), "wsh", back)
+    mixed = (rest[n - 2] + wide(got_on) + wide(got_back)).astype(jnp.bfloat16)
+    scale = math.sqrt(width / total_members)
+    gate_step, up_step = outers(at, [near, near_in, far_in, far_mate], width // groups, hidden_cols, slot_core, scale)
+    return mixed, gate_step, up_step
+
+
 def solution(mesh):
     in_specs = (
         P("grp", "wsh"),

time: 104 us -> 85.5 us (0.82)
  matrix products: 40.1 us -> 0 us
  Pallas kernels: 0 us -> 18.3 us
  waiting for transfers between devices: 20.7 us -> 32.1 us
  other arithmetic: 13 us -> 4.73 us
  local copies, waits for them, and re-layouts: 6.02 us -> 7.14 us
    dot_general x35 -> x0, matrix products: 40.1 us -> none  [the longest x8 15.5 us: grow(): jnp.dot(piece, up_w, preferred_element_type=jnp.float32)]
    pallas_call x0 -> x6, Pallas kernels: none -> 18.3 us  [the longest x2 7.15 us: grow(): pl.pallas_call(lambda *refs: grow_kernel(count, total is None, *refs), ou...]
    ppermute x12 -> x11, waiting for transfers between devices: 2.67 us -> 16.8 us  [the longest x1 6.43 us: per_device(): one_a = lax.ppermute(tokens, 'wsh', onward)]
    unnamed x54 -> x32, local copies, waits for them, and re-layouts: 0.83 us -> 6.98 us
    mul x4 -> x0, local copies, waits for them, and re-layouts: 5.09 us -> none  [spread(): score.reshape(members, per_member)[:, :, None]]
    ppermute x3, starting transfers between devices: 1.02 us -> 5.44 us  [per_device(): got_back = lax.ppermute(behind.astype(wire), 'wsh', back)]
    mul x3 -> x0, other arithmetic: 3.33 us -> none  [spread(): noise_scale * right]
    concatenate x5 -> x3, other arithmetic: 3.18 us -> 0.12 us  [the longest x1 0.08 us: per_device(): jnp.concatenate([ring_owner(place + jnp.arange(n, dtype=jnp.int32), n), j...]
  transfers between devices with their start and end apart: 20 -> 19, of which waited for: 9 -> 9; matrix products, arithmetic and copies ran while one was open for 43% -> 3% of each run, Pallas kernels for 0% -> 17%
where the time goes in v2:
time: 85.5 us; the launch traced here: 85.1 us
  waiting for transfers between devices  32.1 us (38%)
  starting transfers between devices  21.9 us (26%)
  Pallas kernels  18.3 us (21%)
  local copies, waits for them, and re-layouts  7.14 us (8%)
  other arithmetic  4.73 us (6%)
  between operations  0.9 us (1%)
    ppermute x3, waiting for transfers between devices, per_device(): got_on = lax.ppermute(ahead.astype(wire), 'wsh', onward)  9.9 us
    pallas_call x2, Pallas kernels, grow(): pl.pallas_call(lambda *refs: grow_kernel(count, total is None, *refs), ou...  7.15 us
    unnamed x32, local copies, waits for them, and re-layouts  6.98 us
    ppermute x1, waiting for transfers between devices, per_device(): one_a = lax.ppermute(tokens, 'wsh', onward)  6.43 us
    ppermute x1, waiting for transfers between devices, per_device(): two_a = lax.ppermute(one_a, 'wsh', onward)  5.46 us
    ppermute x3, starting transfers between devices, per_device(): got_back = lax.ppermute(behind.astype(wire), 'wsh', back)  5.44 us
    ppermute x3, waiting for transfers between devices, per_device(): got_back = lax.ppermute(behind.astype(wire), 'wsh', back)  4.47 us
    ppermute x1, waiting for transfers between devices, per_device(): three_a = lax.ppermute(two_a, 'wsh', onward)  4.45 us
  transfers between devices with their start and end apart: 19, of which 9 were waited for; matrix products, arithmetic and copies ran while one was open for 3% of the time, Pallas kernels for 17%

profile of v2, /device:TPU:0, one launch (start us, length us, event | category | flops | bytes accessed | tf_op | source)
XLA Modules:
  0.0 85.1 jit_solution(18113072460074823518)
XLA Ops:
  0.6 3.1 %collective-permute-start = (bf16[512,256]{1,0:T(8,128)(2,1)}, bf16[512,256]{1,0:T(8,128)(2,1)S(1)}, u32[]{:S(2)}, u32[]{:S(2)}) collective-permute-start(bf16[512,256]{1,0:T(8,128)(2,1)} %refs_1_.1), channel_id=1, source_target_pairs={{0,2},{2,4},{4,6},{6,7},{7,5},{5,3},{3,1},{1,0},{8,10},{10,12},{12... | collective-permute-start | bytes 786440 | tf_op jit(solution)/shard_map/ppermute | solution.py:484
  3.7 6.4 %collective-permute-done.refs_2_ = bf16[512,256]{1,0:T(8,128)(2,1)S(1)} collective-permute-done((bf16[512,256]{1,0:T(8,128)(2,1)}, bf16[512,256]{1,0:T(8,128)(2,1)S(1)}, u32[]{:S(2)}, u32[]{:S(2)}) %collective-permute-start) | collective-permute-done | bytes 262176 | tf_op jit(solution)/shard_map/ppermute | solution.py:484
  10.1 1.8 %collective-permute-start.1 = (bf16[512,256]{1,0:T(8,128)(2,1)S(1)}, bf16[512,256]{1,0:T(8,128)(2,1)S(1)}, u32[]{:S(2)}, u32[]{:S(2)}) collective-permute-start(bf16[512,256]{1,0:T(8,128)(2,1)S(1)} %collective-permute-done.refs_2_), channel_id=1, source_target_pairs={{0,2},{2,4},{4,6},{6,7},{7,5},{5,3},{3,1},{1,0},{8,10},{10,12},{12... | collective-permute-start | bytes 786440 | tf_op jit(solution)/shard_map/ppermute | solution.py:494
  12.0 0.2 collective-permute-start.4
  12.2 5.5 %collective-permute-done.1.refs_4_ = bf16[512,256]{1,0:T(8,128)(2,1)S(1)} collective-permute-done((bf16[512,256]{1,0:T(8,128)(2,1)S(1)}, bf16[512,256]{1,0:T(8,128)(2,1)S(1)}, u32[]{:S(2)}, u32[]{:S(2)}) %collective-permute-start.1) | collective-permute-done | bytes 262176 | tf_op jit(solution)/shard_map/ppermute | solution.py:494
  17.6 1.5 %collective-permute-start.2 = (bf16[512,256]{1,0:T(8,128)(2,1)S(1)}, bf16[512,256]{1,0:T(8,128)(2,1)S(1)}, u32[]{:S(2)}, u32[]{:S(2)}) collective-permute-start(bf16[512,256]{1,0:T(8,128)(2,1)S(1)} %collective-permute-done.1.refs_4_), channel_id=1, source_target_pairs={{0,2},{2,4},{4,6},{6,7},{7,5},{5,3},{3,1},{1,0},{8,10},{10,12},{12... | collective-permute-start | bytes 786440 | tf_op jit(solution)/shard_map/ppermute | solution.py:496
  19.1 0.5 collective-permute-start.5
  19.7 0.1 pad_add_fusion.refs_0_.at
  19.8 4.4 %collective-permute-done.2.refs_1_ = bf16[512,256]{1,0:T(8,128)(2,1)S(1)} collective-permute-done((bf16[512,256]{1,0:T(8,128)(2,1)S(1)}, bf16[512,256]{1,0:T(8,128)(2,1)S(1)}, u32[]{:S(2)}, u32[]{:S(2)}) %collective-permute-start.2) | collective-permute-done | bytes 262176 | tf_op jit(solution)/shard_map/ppermute | solution.py:496
  24.2 1.7 %collective-permute-start.6 = (bf16[256,256]{1,0:T(8,128)(2,1)S(1)}, bf16[256,256]{1,0:T(8,128)(2,1)S(1)}, u32[]{:S(2)}, u32[]{:S(2)}) collective-permute-start(bf16[256,256]{1,0:T(8,128)(2,1)S(1)} %slice.76), channel_id=1, source_target_pairs={{0,2},{2,4},{4,6},{6,7},{7,5},{5,3},{3,1},{1,0},{8,10},{10,12},{12... | collective-permute-start | bytes 393224 | tf_op jit(solution)/shard_map/ppermute | solution.py:500
  26.0 0.4 collective-permute-start.7
  26.4 2.0 %copy-done = bf16[2048,896]{1,0:T(8,128)(2,1)S(1)} copy-done((bf16[2048,896]{1,0:T(8,128)(2,1)S(1)}, bf16[2048,896]{1,0:T(8,128)(2,1)}, u32[]{:S(2)}) %copy-start) | copy-done | bytes 3670040
  28.4 2.0 %copy-done.2 = bf16[2048,896]{1,0:T(8,128)(2,1)S(1)} copy-done((bf16[2048,896]{1,0:T(8,128)(2,1)S(1)}, bf16[2048,896]{1,0:T(8,128)(2,1)}, u32[]{:S(2)}) %copy-start.2) | copy-done | bytes 3670040
  30.4 0.9 %copy-done.6 = bf16[64,2048]{1,0:T(8,128)(2,1)S(1)} copy-done((bf16[64,2048]{1,0:T(8,128)(2,1)S(1)}, bf16[64,2048]{1,0:T(8,128)(2,1)}, u32[]{:S(2)}) %copy-start.6) | copy-done | bytes 262168
  31.4 0.9 %copy-done.8 = bf16[64,2048]{1,0:T(8,128)(2,1)S(1)} copy-done((bf16[64,2048]{1,0:T(8,128)(2,1)S(1)}, bf16[64,2048]{1,0:T(8,128)(2,1)}, u32[]{:S(2)}) %copy-start.8) | copy-done | bytes 262168
  32.3 0.9 %copy-done.13 = bf16[512,256]{1,0:T(8,128)(2,1)S(1)} copy-done((bf16[512,256]{1,0:T(8,128)(2,1)S(1)}, bf16[512,256]{1,0:T(8,128)(2,1)}, u32[]{:S(2)}) %copy-start.13) | copy-done | bytes 262168
  33.3 4.9 %grow.2 = (f32[512,896]{1,0:T(8,128)S(1)}, f32[512,896]{1,0:T(8,128)S(1)}, f32[512,128]{1,0:T(8,128)S(1)}) custom-call(s32[11]{0:T(128)S(1)} %pad_add_fusion.refs_0_.at, bf16[512,256]{1,0:T(8,128)(2,1)S(1)} %copy-done.13, bf16[512,256]{1,0:T(8,128)(2,1)S(1)} %collective-permute-done.refs_2_, bf16[512,256]{1,0:T(8,128)(2,1)S(1)} %collective-permute-done.3.refs_3_, ...), custom_call_target="tpu_custom_call" | custom-call | flops 2348810240 | bytes 8257536 | tf_op jit(solution)/shard_map/grow/pallas_call | solution.py:303
  38.3 0.0 copy-start.10
  38.3 0.0 copy-start.11
  38.3 2.3 %grow.3 = (f32[512,896]{1,0:T(8,128)S(1)}, f32[512,896]{1,0:T(8,128)S(1)}, f32[512,128]{1,0:T(8,128)S(1)}) custom-call(s32[11]{0:T(128)S(1)} %pad_add_fusion.refs_0_.at, bf16[512,256]{1,0:T(8,128)(2,1)S(1)} %collective-permute-done.2.refs_1_, bf16[512,256]{1,0:T(8,128)(2,1)S(1)} %collective-permute-done.5.refs_2_, bf16[2048,896]{1,0:T(8,128)(2,1)S(1)} %copy-done.1, ...), custom_call_target="tpu_custom_call" | custom-call | flops 939524096 | bytes 9175040 | tf_op jit(solution)/shard_map/grow/pallas_call | solution.py:303
  40.6 4.0 %finish.1 = (bf16[512,896]{1,0:T(8,128)(2,1)S(1)}, f32[512,128]{1,0:T(8,128)S(1)}, bf16[512,256]{1,0:T(8,128)(2,1)S(1)}) custom-call(s32[11]{0:T(128)S(1)} %pad_add_fusion.refs_0_.at, f32[512,896]{1,0:T(8,128)S(1)} %get-tuple-element.19.refs_1_, f32[512,896]{1,0:T(8,128)S(1)} %get-tuple-element.20.refs_2_, f32[512,128]{1,0:T(8,128)S(1)} %get-tuple-element.21.refs_3_, ...), custom_call_target="tpu_custom_call" | custom-call | flops 704643072 | bytes 6000000 | tf_op jit(solution)/shard_map/finish/pallas_call | solution.py:371
  44.6 1.7 %collective-permute-start.12 = (bf16[256,256]{1,0:T(8,128)(2,1)S(1)}, bf16[256,256]{1,0:T(8,128)(2,1)S(1)}, u32[]{:S(2)}, u32[]{:S(2)}) collective-permute-start(bf16[256,256]{1,0:T(8,128)(2,1)S(1)} %get-tuple-element.36), channel_id=1, source_target_pairs={{2,0},{4,2},{6,4},{7,6},{5,7},{3,5},{1,3},{0,1},{10,8},{12,10},{14... | collective-permute-start | bytes 393224 | tf_op jit(solution)/shard_map/ppermute | solution.py:507
  46.3 0.4 collective-permute-start.8
  46.7 4.3 %shares.1 = f32[7,512,256]{2,1,0:T(8,128)S(1)} custom-call(s32[11]{0:T(128)S(1)} %pad_add_fusion.refs_0_.at, bf16[512,896]{1,0:T(8,128)(2,1)S(1)} %get-tuple-element.22.refs_1_, f32[512,128]{1,0:T(8,128)S(1)} %get-tuple-element.23.refs_2_, bf16[896,2048]{1,0:T(8,128)(2,1)S(1)} %copy-done.5, f32[64,2048]{1,0:T(8,128)S(1)} %copy-done.10), custom_call_target="tpu_custom_call" | custom-call | flops 1644167168 | bytes 6881280 | tf_op jit(solution)/shard_map/shares/pallas_call | solution.py:420
  51.1 0.0 copy-start.15
  51.1 0.2 convert.15
  51.3 0.9 %collective-permute-done.8 = bf16[256,256]{1,0:T(8,128)(2,1)S(1)} collective-permute-done((bf16[256,256]{1,0:T(8,128)(2,1)S(1)}, bf16[256,256]{1,0:T(8,128)(2,1)S(1)}, u32[]{:S(2)}, u32[]{:S(2)}) %collective-permute-start.8) | collective-permute-done | bytes 131104 | tf_op jit(solution)/shard_map/ppermute | solution.py:506
  52.2 0.1 fusion.14
  52.3 0.8 collective-permute-start.9
  53.2 1.3 %collective-permute-start.13 = (bf16[512,256]{1,0:T(8,128)(2,1)S(1)}, bf16[512,256]{1,0:T(8,128)(2,1)S(1)}, u32[]{:S(2)}, u32[]{:S(2)}) collective-permute-start(bf16[512,256]{1,0:T(8,128)(2,1)S(1)} %pad_maximum_fusion.1), channel_id=1, source_target_pairs={{2,0},{4,2},{6,4},{7,6},{5,7},{3,5},{1,3},{0,1},{10,8},{12,10},{14... | collective-permute-start | bytes 786440 | tf_op jit(solution)/shard_map/ppermute | solution.py:520
  54.5 6.4 %collective-permute-done.9 = bf16[512,256]{1,0:T(8,128)(2,1)S(1)} collective-permute-done((bf16[512,256]{1,0:T(8,128)(2,1)S(1)}, bf16[512,256]{1,0:T(8,128)(2,1)S(1)}, u32[]{:S(2)}, u32[]{:S(2)}) %collective-permute-start.9) | collective-permute-done | bytes 262176 | tf_op jit(solution)/shard_map/ppermute | solution.py:519
  60.9 0.1 fusion.5
  61.0 1.2 %collective-permute-start.10 = (bf16[512,256]{1,0:T(8,128)(2,1)S(1)}, bf16[512,256]{1,0:T(8,128)(2,1)S(1)}, u32[]{:S(2)}, u32[]{:S(2)}) collective-permute-start(bf16[512,256]{1,0:T(8,128)(2,1)S(1)} %fusion.5), channel_id=1, source_target_pairs={{0,2},{2,4},{4,6},{6,7},{7,5},{5,3},{3,1},{1,0},{8,10},{10,12},{12... | collective-permute-start | bytes 786440 | tf_op jit(solution)/shard_map/ppermute | solution.py:519
  62.1 0.1 copy.14.fit
  62.2 0.6 messages.1
  62.9 1.6 %collective-permute-start.17 = (bf16[64,3840]{1,0:T(8,128)(2,1)S(1)}, bf16[64,3840]{1,0:T(8,128)(2,1)S(1)}, u32[]{:S(2)}, u32[]{:S(2)}) collective-permute-start(bf16[64,3840]{1,0:T(8,128)(2,1)S(1)} %get-tuple-element.26), channel_id=1, source_target_pairs={{0,16},{8,24},{16,0},{24,8},{1,17},{9,25},{17,1},{25,9},{2,18},{10... | collective-permute-start | bytes 1474568 | tf_op jit(solution)/shard_map/ppermute | solution.py:490
  64.5 3.5 %collective-permute-done.10 = bf16[512,256]{1,0:T(8,128)(2,1)S(1)} collective-permute-done((bf16[512,256]{1,0:T(8,128)(2,1)S(1)}, bf16[512,256]{1,0:T(8,128)(2,1)S(1)}, u32[]{:S(2)}, u32[]{:S(2)}) %collective-permute-start.10) | collective-permute-done | bytes 262176 | tf_op jit(solution)/shard_map/ppermute | solution.py:519
  67.9 1.4 %fusion.7 = (bf16[512,256]{1,0:T(8,128)(2,1)S(1)}, bf16[512,256]{1,0:T(8,128)(2,1)S(1)}) fusion(f32[7,512,256]{2,1,0:T(8,128)} %copy-done.4, bf16[512,256]{1,0:T(8,128)(2,1)S(1)} %collective-permute-done.10, bf16[512,256]{1,0:T(8,128)(2,1)S(1)} %collective-permute-done.13), kind=kLoop, calls=%fused_computation.11 | loop fusion | flops 786432 | bytes 2097152 | tf_op jit(solution)/shard_map/convert_element_type | solution.py:519
  69.3 2.1 %collective-permute-start.14 = (bf16[512,256]{1,0:T(8,128)(2,1)S(1)}, bf16[512,256]{1,0:T(8,128)(2,1)S(1)}, u32[]{:S(2)}, u32[]{:S(2)}) collective-permute-start(bf16[512,256]{1,0:T(8,128)(2,1)S(1)} %get-tuple-element.30), channel_id=1, source_target_pairs={{2,0},{4,2},{6,4},{7,6},{5,7},{3,5},{1,3},{0,1},{10,8},{12,10},{14... | collective-permute-start | bytes 786440 | tf_op jit(solution)/shard_map/ppermute | solution.py:520
  71.4 0.4 collective-permute-done.17.refs_3_
  71.8 0.1 collective-permute-start.18
  71.9 1.5 %collective-permute-start.11 = (bf16[512,256]{1,0:T(8,128)(2,1)S(1)}, bf16[512,256]{1,0:T(8,128)(2,1)S(1)}, u32[]{:S(2)}, u32[]{:S(2)}) collective-permute-start(bf16[512,256]{1,0:T(8,128)(2,1)S(1)} %get-tuple-element.29), channel_id=1, source_target_pairs={{0,2},{2,4},{4,6},{6,7},{7,5},{5,3},{3,1},{1,0},{8,10},{10,12},{12... | collective-permute-start | bytes 786440 | tf_op jit(solution)/shard_map/ppermute | solution.py:519
  73.3 2.4 %collective-permute-done.14 = bf16[512,256]{1,0:T(8,128)(2,1)S(1)} collective-permute-done((bf16[512,256]{1,0:T(8,128)(2,1)S(1)}, bf16[512,256]{1,0:T(8,128)(2,1)S(1)}, u32[]{:S(2)}, u32[]{:S(2)}) %collective-permute-start.14) | collective-permute-done | bytes 262176 | tf_op jit(solution)/shard_map/ppermute | solution.py:520
  75.7 1.1 %fusion.3 = bf16[512,256]{1,0:T(8,128)(2,1)S(1)} fusion(f32[7,512,256]{2,1,0:T(8,128)} %copy-done.4, bf16[512,256]{1,0:T(8,128)(2,1)S(1)} %collective-permute-done.14), kind=kLoop, calls=%fused_computation.5 | loop fusion | flops 393216 | bytes 1048576 | tf_op jit(solution)/shard_map/convert_element_type | solution.py:520
  76.8 2.1 %collective-permute-start.15 = (bf16[512,256]{1,0:T(8,128)(2,1)S(1)}, bf16[512,256]{1,0:T(8,128)(2,1)S(1)}, u32[]{:S(2)}, u32[]{:S(2)}) collective-permute-start(bf16[512,256]{1,0:T(8,128)(2,1)S(1)} %fusion.3), channel_id=1, source_target_pairs={{2,0},{4,2},{6,4},{7,6},{5,7},{3,5},{1,3},{0,1},{10,8},{12,10},{14... | collective-permute-start | bytes 786440 | tf_op jit(solution)/shard_map/ppermute | solution.py:520
  78.9 2.2 %outers.1 = (bf16[512,896]{1,0:T(8,128)(2,1)}, bf16[512,896]{1,0:T(8,128)(2,1)}) custom-call(s32[11]{0:T(128)S(1)} %pad_add_fusion.refs_0_.at, bf16[64,3840]{1,0:T(8,128)(2,1)S(1)} %get-tuple-element.25.refs_1_, bf16[64,3840]{1,0:T(8,128)(2,1)S(1)} %collective-permute-done.16.refs_2_, bf16[64,3840]{1,0:T(8,128)(2,1)S(1)} %collective-permute-done.17.refs_3_, ...), custom_call_target="tpu_custom_call" | custom-call | flops 1000000000 | bytes 6000000 | tf_op jit(solution)/shard_map/outers/pallas_call | solution.py:240
  81.1 2.1 %collective-permute-done.15 = bf16[512,256]{1,0:T(8,128)(2,1)S(1)} collective-permute-done((bf16[512,256]{1,0:T(8,128)(2,1)S(1)}, bf16[512,256]{1,0:T(8,128)(2,1)S(1)}, u32[]{:S(2)}, u32[]{:S(2)}) %collective-permute-start.15) | collective-permute-done | bytes 262176 | tf_op jit(solution)/shard_map/ppermute | solution.py:520
  83.2 1.8 %fusion.10 = bf16[512,256]{1,0:T(8,128)(2,1)} fusion(f32[7,512,256]{2,1,0:T(8,128)} %copy-done.4, bf16[512,256]{1,0:T(8,128)(2,1)S(1)} %collective-permute-done.15, bf16[512,256]{1,0:T(8,128)(2,1)S(1)} %collective-permute-done.11), kind=kLoop, calls=%fused_computation.15 | loop fusion | flops 655360 | bytes 1310720 | tf_op jit(solution)/shard_map/convert_element_type | solution.py:521
  (44 shorter events, 0.2 us)
Async XLA Ops:
  0.6 9.5 %collective-permute-start = (bf16[512,256]{1,0:T(8,128)(2,1)}, bf16[512,256]{1,0:T(8,128)(2,1)S(1)}, u32[]{:S(2)}, u32[]{:S(2)}) collective-permute-start(bf16[512,256]{1,0:T(8,128)(2,1)} %refs_1_.1), channel_id=1, source_target_pairs={{0,2},{2,4},{4,6},{6,7},{7,5},{5,3},{3,1},{1,0},{8,10},{10,12},{12... | collective-permute-start | bytes 786440 | tf_op jit(solution)/shard_map/ppermute | solution.py:484
  3.7 8.3 %collective-permute-start.3 = (bf16[512,256]{1,0:T(8,128)(2,1)}, bf16[512,256]{1,0:T(8,128)(2,1)S(1)}, u32[]{:S(2)}, u32[]{:S(2)}) collective-permute-start(bf16[512,256]{1,0:T(8,128)(2,1)} %refs_1_.1), channel_id=1, source_target_pairs={{2,0},{4,2},{6,4},{7,6},{5,7},{3,5},{1,3},{0,1},{10,8},{12,10},{14... | collective-permute-start | bytes 786440 | tf_op jit(solution)/shard_map/ppermute | solution.py:485
  10.1 7.5 %collective-permute-start.1 = (bf16[512,256]{1,0:T(8,128)(2,1)S(1)}, bf16[512,256]{1,0:T(8,128)(2,1)S(1)}, u32[]{:S(2)}, u32[]{:S(2)}) collective-permute-start(bf16[512,256]{1,0:T(8,128)(2,1)S(1)} %collective-permute-done.refs_2_), channel_id=1, source_target_pairs={{0,2},{2,4},{4,6},{6,7},{7,5},{5,3},{3,1},{1,0},{8,10},{10,12},{12... | collective-permute-start | bytes 786440 | tf_op jit(solution)/shard_map/ppermute | solution.py:494
  12.0 7.2 %collective-permute-start.4 = (bf16[512,256]{1,0:T(8,128)(2,1)S(1)}, bf16[512,256]{1,0:T(8,128)(2,1)S(1)}, u32[]{:S(2)}, u32[]{:S(2)}) collective-permute-start(bf16[512,256]{1,0:T(8,128)(2,1)S(1)} %collective-permute-done.3.refs_3_), channel_id=1, source_target_pairs={{2,0},{4,2},{6,4},{7,6},{5,7},{3,5},{1,3},{0,1},{10,8},{12,10},{14... | collective-permute-start | bytes 786440 | tf_op jit(solution)/shard_map/ppermute | solution.py:495
  17.6 6.6 %collective-permute-start.2 = (bf16[512,256]{1,0:T(8,128)(2,1)S(1)}, bf16[512,256]{1,0:T(8,128)(2,1)S(1)}, u32[]{:S(2)}, u32[]{:S(2)}) collective-permute-start(bf16[512,256]{1,0:T(8,128)(2,1)S(1)} %collective-permute-done.1.refs_4_), channel_id=1, source_target_pairs={{0,2},{2,4},{4,6},{6,7},{7,5},{5,3},{3,1},{1,0},{8,10},{10,12},{12... | collective-permute-start | bytes 786440 | tf_op jit(solution)/shard_map/ppermute | solution.py:496
  19.1 6.8 %collective-permute-start.5 = (bf16[512,256]{1,0:T(8,128)(2,1)S(1)}, bf16[512,256]{1,0:T(8,128)(2,1)S(1)}, u32[]{:S(2)}, u32[]{:S(2)}) collective-permute-start(bf16[512,256]{1,0:T(8,128)(2,1)S(1)} %collective-permute-done.4.refs_5_), channel_id=1, source_target_pairs={{2,0},{4,2},{6,4},{7,6},{5,7},{3,5},{1,3},{0,1},{10,8},{12,10},{14... | collective-permute-start | bytes 786440 | tf_op jit(solution)/shard_map/ppermute | solution.py:497
  24.2 16.4 %collective-permute-start.6 = (bf16[256,256]{1,0:T(8,128)(2,1)S(1)}, bf16[256,256]{1,0:T(8,128)(2,1)S(1)}, u32[]{:S(2)}, u32[]{:S(2)}) collective-permute-start(bf16[256,256]{1,0:T(8,128)(2,1)S(1)} %slice.76), channel_id=1, source_target_pairs={{0,2},{2,4},{4,6},{6,7},{7,5},{5,3},{3,1},{1,0},{8,10},{10,12},{12... | collective-permute-start | bytes 393224 | tf_op jit(solution)/shard_map/ppermute | solution.py:500
  26.0 14.6 %collective-permute-start.7 = (bf16[256,256]{1,0:T(8,128)(2,1)S(1)}, bf16[256,256]{1,0:T(8,128)(2,1)S(1)}, u32[]{:S(2)}, u32[]{:S(2)}) collective-permute-start(bf16[256,256]{1,0:T(8,128)(2,1)S(1)} %slice.77), channel_id=1, source_target_pairs={{2,0},{4,2},{6,4},{7,6},{5,7},{3,5},{1,3},{0,1},{10,8},{12,10},{14... | collective-permute-start | bytes 393224 | tf_op jit(solution)/shard_map/ppermute | solution.py:501
  26.4 2.0 %copy-start = (bf16[2048,896]{1,0:T(8,128)(2,1)S(1)}, bf16[2048,896]{1,0:T(8,128)(2,1)}, u32[]{:S(2)}) copy-start(bf16[2048,896]{1,0:T(8,128)(2,1)} %refs_6_.5) | copy-start | bytes 11010052
  28.4 2.0 %copy-start.2 = (bf16[2048,896]{1,0:T(8,128)(2,1)S(1)}, bf16[2048,896]{1,0:T(8,128)(2,1)}, u32[]{:S(2)}) copy-start(bf16[2048,896]{1,0:T(8,128)(2,1)} %refs_7_.3) | copy-start | bytes 11010052
  30.4 0.9 %copy-start.6 = (bf16[64,2048]{1,0:T(8,128)(2,1)S(1)}, bf16[64,2048]{1,0:T(8,128)(2,1)}, u32[]{:S(2)}) copy-start(bf16[64,2048]{1,0:T(8,128)(2,1)} %gate_near.1) | copy-start | bytes 786436
  31.4 0.9 %copy-start.8 = (bf16[64,2048]{1,0:T(8,128)(2,1)S(1)}, bf16[64,2048]{1,0:T(8,128)(2,1)}, u32[]{:S(2)}) copy-start(bf16[64,2048]{1,0:T(8,128)(2,1)} %up_near.1) | copy-start | bytes 786436
  32.3 0.9 %copy-start.13 = (bf16[512,256]{1,0:T(8,128)(2,1)S(1)}, bf16[512,256]{1,0:T(8,128)(2,1)}, u32[]{:S(2)}) copy-start(bf16[512,256]{1,0:T(8,128)(2,1)} %refs_1_.1) | copy-start | bytes 786436
  33.3 4.9 %copy-start.1 = (bf16[2048,896]{1,0:T(8,128)(2,1)S(1)}, bf16[2048,896]{1,0:T(8,128)(2,1)}, u32[]{:S(2)}) copy-start(bf16[2048,896]{1,0:T(8,128)(2,1)} %refs_6_.5) | copy-start | bytes 11010052
  33.3 4.9 %copy-start.3 = (bf16[2048,896]{1,0:T(8,128)(2,1)S(1)}, bf16[2048,896]{1,0:T(8,128)(2,1)}, u32[]{:S(2)}) copy-start(bf16[2048,896]{1,0:T(8,128)(2,1)} %refs_7_.3) | copy-start | bytes 11010052
  33.3 4.9 %copy-start.7 = (bf16[64,2048]{1,0:T(8,128)(2,1)S(1)}, bf16[64,2048]{1,0:T(8,128)(2,1)}, u32[]{:S(2)}) copy-start(bf16[64,2048]{1,0:T(8,128)(2,1)} %gate_near.1) | copy-start | bytes 786436
  33.3 4.9 %copy-start.9 = (bf16[64,2048]{1,0:T(8,128)(2,1)S(1)}, bf16[64,2048]{1,0:T(8,128)(2,1)}, u32[]{:S(2)}) copy-start(bf16[64,2048]{1,0:T(8,128)(2,1)} %up_near.1) | copy-start | bytes 786436
  38.2 2.4 %copy-start.5 = (bf16[896,2048]{1,0:T(8,128)(2,1)S(1)}, bf16[896,2048]{1,0:T(8,128)(2,1)}, u32[]{:S(2)}) copy-start(bf16[896,2048]{1,0:T(8,128)(2,1)} %refs_3_.3) | copy-start | bytes 11010052
  38.3 2.4 %copy-start.10 = (f32[64,2048]{1,0:T(8,128)S(1)}, f32[64,2048]{1,0:T(8,128)}, u32[]{:S(2)}) copy-start(f32[64,2048]{1,0:T(8,128)} %refs_4_.3) | copy-start | bytes 1572868
  38.3 2.3 %copy-start.11 = (f32[64,896]{1,0:T(8,128)S(1)}, f32[64,896]{1,0:T(8,128)}, u32[]{:S(2)}) copy-start(f32[64,896]{1,0:T(8,128)} %gate_r.1) | copy-start | bytes 688132
  38.3 2.3 %copy-start.12 = (f32[64,896]{1,0:T(8,128)S(1)}, f32[64,896]{1,0:T(8,128)}, u32[]{:S(2)}) copy-start(f32[64,896]{1,0:T(8,128)} %up_r.1) | copy-start | bytes 688132
  38.3 2.3 %copy-start.14 = (bf16[64,896]{1,0:T(8,128)(2,1)S(1)}, bf16[64,896]{1,0:T(8,128)(2,1)}, u32[]{:S(2)}) copy-start(bf16[64,896]{1,0:T(8,128)(2,1)} %refs_12_.1) | copy-start | bytes 344068
  44.6 6.7 %collective-permute-start.12 = (bf16[256,256]{1,0:T(8,128)(2,1)S(1)}, bf16[256,256]{1,0:T(8,128)(2,1)S(1)}, u32[]{:S(2)}, u32[]{:S(2)}) collective-permute-start(bf16[256,256]{1,0:T(8,128)(2,1)S(1)} %get-tuple-element.36), channel_id=1, source_target_pairs={{2,0},{4,2},{6,4},{7,6},{5,7},{3,5},{1,3},{0,1},{10,8},{12,10},{14... | collective-permute-start | bytes 393224 | tf_op jit(solution)/shard_map/ppermute | solution.py:507
  46.3 5.9 %collective-permute-start.8 = (bf16[256,256]{1,0:T(8,128)(2,1)S(1)}, bf16[256,256]{1,0:T(8,128)(2,1)S(1)}, u32[]{:S(2)}, u32[]{:S(2)}) collective-permute-start(bf16[256,256]{1,0:T(8,128)(2,1)S(1)} %get-tuple-element.35), channel_id=1, source_target_pairs={{0,2},{2,4},{4,6},{6,7},{7,5},{5,3},{3,1},{1,0},{8,10},{10,12},{12... | collective-permute-start | bytes 393224 | tf_op jit(solution)/shard_map/ppermute | solution.py:506
  51.1 9.8 %copy-start.4 = (f32[7,512,256]{2,1,0:T(8,128)}, f32[7,512,256]{2,1,0:T(8,128)S(1)}, u32[]{:S(2)}) copy-start(f32[7,512,256]{2,1,0:T(8,128)S(1)} %shares.1) | copy-start | bytes 11010052
  51.1 11.1 %copy-start.15 = (s32[64]{0:T(128)S(1)}, s32[64]{0:T(128)}, u32[]{:S(2)}) copy-start(s32[64]{0:T(128)} %param.21) | copy-start | bytes 772
  52.3 8.6 %collective-permute-start.9 = (bf16[512,256]{1,0:T(8,128)(2,1)S(1)}, bf16[512,256]{1,0:T(8,128)(2,1)S(1)}, u32[]{:S(2)}, u32[]{:S(2)}) collective-permute-start(bf16[512,256]{1,0:T(8,128)(2,1)S(1)} %pad_maximum_fusion), channel_id=1, source_target_pairs={{0,2},{2,4},{4,6},{6,7},{7,5},{5,3},{3,1},{1,0},{8,10},{10,12},{12... | collective-permute-start | bytes 786440 | tf_op jit(solution)/shard_map/ppermute | solution.py:519
  53.2 11.3 %collective-permute-start.13 = (bf16[512,256]{1,0:T(8,128)(2,1)S(1)}, bf16[512,256]{1,0:T(8,128)(2,1)S(1)}, u32[]{:S(2)}, u32[]{:S(2)}) collective-permute-start(bf16[512,256]{1,0:T(8,128)(2,1)S(1)} %pad_maximum_fusion.1), channel_id=1, source_target_pairs={{2,0},{4,2},{6,4},{7,6},{5,7},{3,5},{1,3},{0,1},{10,8},{12,10},{14... | collective-permute-start | bytes 786440 | tf_op jit(solution)/shard_map/ppermute | solution.py:520
  61.0 7.0 %collective-permute-start.10 = (bf16[512,256]{1,0:T(8,128)(2,1)S(1)}, bf16[512,256]{1,0:T(8,128)(2,1)S(1)}, u32[]{:S(2)}, u32[]{:S(2)}) collective-permute-start(bf16[512,256]{1,0:T(8,128)(2,1)S(1)} %fusion.5), channel_id=1, source_target_pairs={{0,2},{2,4},{4,6},{6,7},{7,5},{5,3},{3,1},{1,0},{8,10},{10,12},{12... | collective-permute-start | bytes 786440 | tf_op jit(solution)/shard_map/ppermute | solution.py:519
  62.9 8.9 %collective-permute-start.17 = (bf16[64,3840]{1,0:T(8,128)(2,1)S(1)}, bf16[64,3840]{1,0:T(8,128)(2,1)S(1)}, u32[]{:S(2)}, u32[]{:S(2)}) collective-permute-start(bf16[64,3840]{1,0:T(8,128)(2,1)S(1)} %get-tuple-element.26), channel_id=1, source_target_pairs={{0,16},{8,24},{16,0},{24,8},{1,17},{9,25},{17,1},{25,9},{2,18},{10... | collective-permute-start | bytes 1474568 | tf_op jit(solution)/shard_map/ppermute | solution.py:490
  69.3 6.4 %collective-permute-start.14 = (bf16[512,256]{1,0:T(8,128)(2,1)S(1)}, bf16[512,256]{1,0:T(8,128)(2,1)S(1)}, u32[]{:S(2)}, u32[]{:S(2)}) collective-permute-start(bf16[512,256]{1,0:T(8,128)(2,1)S(1)} %get-tuple-element.30), channel_id=1, source_target_pairs={{2,0},{4,2},{6,4},{7,6},{5,7},{3,5},{1,3},{0,1},{10,8},{12,10},{14... | collective-permute-start | bytes 786440 | tf_op jit(solution)/shard_map/ppermute | solution.py:520
  71.4 7.5 %collective-permute-start.16 = (bf16[64,3840]{1,0:T(8,128)(2,1)S(1)}, bf16[64,3840]{1,0:T(8,128)(2,1)S(1)}, u32[]{:S(2)}, u32[]{:S(2)}) collective-permute-start(bf16[64,3840]{1,0:T(8,128)(2,1)S(1)} %get-tuple-element.25.refs_1_), channel_id=1, source_target_pairs={{0,8},{8,0},{16,24},{24,16},{1,9},{9,1},{17,25},{25,17},{2,10},{10... | collective-permute-start | bytes 1474568 | tf_op jit(solution)/shard_map/ppermute | solution.py:491
  71.8 7.1 %collective-permute-start.18 = (bf16[64,3840]{1,0:T(8,128)(2,1)S(1)}, bf16[64,3840]{1,0:T(8,128)(2,1)S(1)}, u32[]{:S(2)}, u32[]{:S(2)}) collective-permute-start(bf16[64,3840]{1,0:T(8,128)(2,1)S(1)} %collective-permute-done.17.refs_3_), channel_id=1, source_target_pairs={{0,8},{8,0},{16,24},{24,16},{1,9},{9,1},{17,25},{25,17},{2,10},{10... | collective-permute-start | bytes 1474568 | tf_op jit(solution)/shard_map/ppermute | solution.py:492
  71.9 9.3 %collective-permute-start.11 = (bf16[512,256]{1,0:T(8,128)(2,1)S(1)}, bf16[512,256]{1,0:T(8,128)(2,1)S(1)}, u32[]{:S(2)}, u32[]{:S(2)}) collective-permute-start(bf16[512,256]{1,0:T(8,128)(2,1)S(1)} %get-tuple-element.29), channel_id=1, source_target_pairs={{0,2},{2,4},{4,6},{6,7},{7,5},{5,3},{3,1},{1,0},{8,10},{10,12},{12... | collective-permute-start | bytes 786440 | tf_op jit(solution)/shard_map/ppermute | solution.py:519
  76.8 6.4 %collective-permute-start.15 = (bf16[512,256]{1,0:T(8,128)(2,1)S(1)}, bf16[512,256]{1,0:T(8,128)(2,1)S(1)}, u32[]{:S(2)}, u32[]{:S(2)}) collective-permute-start(bf16[512,256]{1,0:T(8,128)(2,1)S(1)} %fusion.3), channel_id=1, source_target_pairs={{2,0},{4,2},{6,4},{7,6},{5,7},{3,5},{1,3},{0,1},{10,8},{12,10},{14... | collective-permute-start | bytes 786440 | tf_op jit(solution)/shard_map/ppermute | solution.py:520

commit v3 on v1

--- a/solution.py
+++ b/solution.py
@@ -3,6 +3,8 @@
 import jax
 import jax.numpy as jnp
 from jax import lax
+from jax.experimental import pallas as pl
+from jax.experimental.pallas import tpu as pltpu
 from jax.sharding import PartitionSpec as P
 
 noise_scale = 0.5
@@ -21,7 +23,7 @@
     return jnp.where(place < n // 2, 2 * place, 2 * (n - 1 - place) + 1)
 
 
-def per_device(
+def plain_device(
     tokens,
     gate_weight,
     up_weight,
@@ -178,6 +180,370 @@
     return mixed.astype(jnp.bfloat16), gate_step, up_step
 
 
+MIB = 1 << 20
+VMEM = pl.BlockSpec(memory_space=pltpu.VMEM)
+SMEM = pl.BlockSpec(memory_space=pltpu.SMEM)
+ANY = pl.BlockSpec(memory_space=pl.ANY)
+HBM = pl.BlockSpec(memory_space=pltpu.HBM)
+
+
+def dims(lhs, rhs):
+    return (((lhs,), (rhs,)), ((), ()))
+
+
+def call(body, operands, out_shape, micros, name, in_specs=None, out_specs=None, scratch=(), limit=24, aliases=None):
+    count = len(out_shape)
+    return pl.pallas_call(
+        body,
+        out_shape=out_shape,
+        in_specs=in_specs or [SMEM] + [VMEM] * (len(operands) - 1),
+        out_specs=out_specs or (VMEM,) * count,
+        scratch_shapes=list(scratch),
+        input_output_aliases=aliases or {},
+        compiler_params=pltpu.CompilerParams(vmem_limit_bytes=limit * MIB),
+        cost_estimate=pl.CostEstimate(flops=int(micros * 10**9), bytes_accessed=10**6, transcendentals=0),
+        name=name,
+    )(*operands)
+
+
+def stage_kernel(plan, count, *refs):
+    sources, targets, sems = refs[:count], refs[count:-1], refs[-1]
+    copies = []
+    for i, (target, row) in enumerate(plan):
+        height = sources[i].shape[0]
+        copies.append(pltpu.make_async_copy(sources[i], targets[target].at[pl.ds(row, height)], sems.at[i]))
+    for copy in copies:
+        copy.start()
+    for copy in copies:
+        copy.wait()
+
+
+def stage(groups, micros, name, earlier=()):
+    arrays, plan, shapes = [], [], []
+    for target, group in enumerate(groups):
+        row = 0
+        for array in group:
+            arrays.append(pltpu.with_memory_space_constraint(array, pltpu.HBM))
+            plan.append((target, row))
+            row += array.shape[0]
+        shapes.append(pltpu.VMEM((row, group[0].shape[1]), group[0].dtype))
+    count = len(arrays)
+    staged = call(
+        lambda *refs: stage_kernel(plan, count, *refs[:count], *refs[count + len(earlier) :]),
+        (*arrays, *earlier),
+        tuple(shapes),
+        micros,
+        name,
+        in_specs=[HBM] * count + [ANY] * len(earlier),
+        scratch=[pltpu.SemaphoreType.DMA((count,))],
+    )
+    return [pltpu.with_memory_space_constraint(array, pltpu.VMEM) for array in staged]
+
+
+def lane_block(ref, index, width, rows=slice(None), base=0):
+    return ref[rows, pl.ds(pl.multiple_of(base + index * width, 128), width)]
+
+
+def message_kernel(slot_far, slot_near, at, fit, rights, lefts, earlier, far, near):
+    members = fit.shape[0]
+    cols = rights.shape[1]
+    block = lefts.shape[1] // 2
+    weight = fit[...]
+    gate_fit = (weight * rights[:members, :]).astype(jnp.bfloat16)
+    up_fit = (weight * rights[members:, :]).astype(jnp.bfloat16)
+    for out, slot in ((far, slot_far), (near, slot_near)):
+        out[:, :cols] = gate_fit
+        out[:, cols : 2 * cols] = up_fit
+        out[:, 2 * cols : 2 * cols + block] = lane_block(lefts, at[slot], block, slice(0, members))
+        out[:, 2 * cols + block :] = lane_block(lefts, at[slot], block, slice(members, 2 * members))
+
+
+def messages(at, fit, rights, lefts, earlier, slot_far, slot_near):
+    members = fit.shape[0]
+    shape = jax.ShapeDtypeStruct((members, 2 * rights.shape[1] + lefts.shape[1]), jnp.bfloat16)
+    return call(
+        lambda *refs: message_kernel(slot_far, slot_near, *refs),
+        (at, fit, rights, lefts, earlier),
+        (shape, shape),
+        2,
+        "messages",
+        in_specs=[SMEM] + [VMEM] * 3 + [ANY],
+    )
+
+
+def outer_kernel(slot, scale, at, a, b, c, d, gate_out, up_out):
+    rows, cols = gate_out.shape
+    parts = (a, b, c, d)
+    for out, shift, right_at in ((gate_out, 0, 0), (up_out, 2 * rows, cols)):
+        left = jnp.concatenate([lane_block(p, at[slot], rows, base=2 * cols + shift) for p in parts], axis=0)
+        right = jnp.concatenate([p[:, right_at : right_at + cols] for p in parts], axis=0)
+        total = lax.dot_general(left, right, dims(0, 0), preferred_element_type=jnp.float32)
+        out[...] = (scale * total).astype(out.dtype)
+
+
+def outers(at, parts, rows, cols, slot, scale):
+    shape = jax.ShapeDtypeStruct((rows, cols), jnp.bfloat16)
+    return call(
+        lambda *refs: outer_kernel(slot, scale, *refs), (at, *parts), (shape, shape), 5, "outers"
+    )
+
+
+def row_block(ref, index, height):
+    return ref[pl.ds(pl.multiple_of(index * height, height), height), :]
+
+
+def grow_kernel(slots, first, fresh, tall, at, *refs):
+    count = len(slots)
+    pieces = refs[:count]
+    gate_w, up_w, lefts = refs[count : count + 3]
+    old = (None,) * 3 if fresh else refs[count + 3 : count + 6]
+    gate, up, scores = refs[-3:]
+    rows, span = pieces[0].shape
+    members = scores.shape[1] // 2
+    owns = [slice(at_row, at_row + members) for at_row in (first, lefts.shape[0] // 2 + first)]
+    for start in range(0, rows, tall):
+        part = slice(start, start + tall)
+        piece = jnp.concatenate([p[part, :] for p in pieces], axis=1)
+        for out, was, weight in ((gate, old[0], gate_w), (up, old[1], up_w)):
+            rhs = jnp.concatenate([row_block(weight, at[s], span) for s in slots], axis=0)
+            new = jnp.dot(piece, rhs, preferred_element_type=jnp.float32)
+            out[part, :] = new if fresh else was[part, :] + new
+        left = jnp.concatenate(
+            [
+                jnp.concatenate([lane_block(lefts, at[s], span, own) for s in slots], axis=1)
+                for own in owns
+            ],
+            axis=0,
+        )
+        new = lax.dot_general(piece, left, dims(1, 1), preferred_element_type=jnp.float32)
+        scores[part, :] = new if fresh else old[2][part, :] + new
+
+
+def grow(at, pieces, slots, weights, total, first, members, micros):
+    rows = pieces[0].shape[0]
+    cols = weights[0].shape[1]
+    count = len(pieces)
+    old = () if total is None else tuple(total)
+    base = 1 + count + len(weights)
+    return call(
+        lambda *refs: grow_kernel(slots, first, total is None, min(rows, 256), *refs),
+        (at, *pieces, *weights, *old),
+        (
+            jax.ShapeDtypeStruct((rows, cols), jnp.float32),
+            jax.ShapeDtypeStruct((rows, cols), jnp.float32),
+            jax.ShapeDtypeStruct((rows, 2 * members), jnp.float32),
+        ),
+        micros,
+        "grow",
+        aliases={base + i: i for i in range(len(old))},
+    )
+
+
+def spread_rows(score, right, per_member):
+    members, cols = right.shape
+    wide = jnp.broadcast_to(right[:, None, :], (members, per_member, cols))
+    return score * wide.reshape(members * per_member, cols)
+
+
+def finish_kernel(
+    slot, first, per_member, tall, at, gate_sum, up_sum, scores, top, bottom, gate_w, up_w, lefts,
+    rights, down_l, down_w, down_r, hidden_out, score_out, on_out, back_out,
+):
+    rows = gate_sum.shape[0]
+    span = top.shape[1]
+    half = rows // 2
+    members = rows // per_member
+    own = slice(first, first + members)
+    gate_rhs, up_rhs = row_block(gate_w, at[slot], span), row_block(up_w, at[slot], span)
+    group = lefts.shape[0] // 2
+    own_up = slice(group + first, group + first + members)
+    left = jnp.concatenate([lane_block(lefts, at[slot], span, own), lane_block(lefts, at[slot], span, own_up)], axis=0)
+    down_rhs = lane_block(down_w, at[slot], span)
+    down_left = down_l[own, :]
+    for start in range(0, rows, tall):
+        part = slice(start, start + tall)
+        source, shift, out = (top, 0, on_out) if start < half else (bottom, half, back_out)
+        inner = slice(start - shift, start - shift + tall)
+        mine = slice(first + start // per_member, first + (start + tall) // per_member)
+        mine_up = slice(group + mine.start, group + mine.stop)
+        piece = source[inner, :]
+        score = scores[part, :] + lax.dot_general(piece, left, dims(1, 1), preferred_element_type=jnp.float32)
+        member = (lax.broadcasted_iota(jnp.int32, (tall, 2 * members), 0) + start) // per_member
+        column = lax.broadcasted_iota(jnp.int32, (tall, 2 * members), 1)
+        gate_score = jnp.sum(jnp.where(column == member, score, 0.0), axis=1, keepdims=True)
+        up_score = jnp.sum(jnp.where(column == member + members, score, 0.0), axis=1, keepdims=True)
+        gate = gate_sum[part, :] + jnp.dot(piece, gate_rhs, preferred_element_type=jnp.float32)
+        up = up_sum[part, :] + jnp.dot(piece, up_rhs, preferred_element_type=jnp.float32)
+        gate = gate + spread_rows(noise_scale * gate_score, rights[mine, :], per_member)
+        up = up + spread_rows(noise_scale * up_score, rights[mine_up, :], per_member)
+        hidden = (silu(gate) * up).astype(jnp.bfloat16)
+        hidden_out[part, :] = hidden
+        down = lax.dot_general(hidden, down_left, dims(1, 1), preferred_element_type=jnp.float32)
+        down = jnp.where(column[:, :members] == member[:, :members], down, 0.0)
+        down_score = noise_scale * jnp.sum(down, axis=1, keepdims=True)
+        score_out[part, :] = jnp.broadcast_to(down_score, (tall, 128))
+        share = jnp.dot(hidden, down_rhs, preferred_element_type=jnp.float32)
+        share = share + spread_rows(down_score, lane_block(down_r, at[slot], span, mine), per_member)
+        out[inner, :] = share.astype(out.dtype)
+
+
+def finish(at, total, top, bottom, weights, others, slot, first, per_member, wire):
+    rows, cols = total[0].shape
+    span = top.shape[1]
+    return call(
+        lambda *refs: finish_kernel(slot, first, per_member, rows // 2, *refs),
+        (at, *total, top, bottom, *weights, *others),
+        (
+            jax.ShapeDtypeStruct((rows, cols), jnp.bfloat16),
+            jax.ShapeDtypeStruct((rows, 128), jnp.float32),
+            jax.ShapeDtypeStruct((rows // 2, span), wire),
+            jax.ShapeDtypeStruct((rows // 2, span), wire),
+        ),
+        4,
+        "finish",
+    )
+
+
+def share_kernel(slots, first, per_member, at, hidden, score, down_w, down_r, *outs):
+    rows = hidden.shape[0]
+    own = slice(first, first + rows // per_member)
+    for slot, out in zip(slots, outs):
+        span = out.shape[1]
+        total = jnp.dot(hidden[...], lane_block(down_w, at[slot], span), preferred_element_type=jnp.float32)
+        out[...] = total + spread_rows(score[:, :1], lane_block(down_r, at[slot], span, own), per_member)
+
+
+def shares(at, hidden, score, down_weight, down_right, slots, span, first, per_member, micros, passing=()):
+    count = len(slots)
+    shape = jax.ShapeDtypeStruct((hidden.shape[0], span), jnp.float32)
+    return call(
+        lambda *refs: share_kernel(slots, first, per_member, *refs[:5], *refs[5 + len(passing) :][:count]),
+        (at, hidden, score, down_weight, down_right, *passing),
+        (shape,) * count + tuple(jax.ShapeDtypeStruct(p.shape, p.dtype) for p in passing),
+        micros,
+        "shares",
+        in_specs=[SMEM] + [VMEM] * 4 + [ANY] * len(passing),
+        out_specs=(VMEM,) * count + (ANY,) * len(passing),
+        aliases={5 + i: count + i for i in range(len(passing))},
+    )
+
+
+CHUNKS = 1
+
+
+def per_device(
+    tokens,
+    gate_weight,
+    up_weight,
+    down_weight,
+    gate_left,
+    gate_right,
+    up_left,
+    up_right,
+    down_left,
+    down_right,
+    fitness_rank,
+):
+    arguments = (tokens, gate_weight, up_weight, down_weight, gate_left, gate_right, up_left,
+                 up_right, down_left, down_right, fitness_rank)
+    members, width = gate_left.shape
+    all_rows, span = tokens.shape
+    hidden_cols = gate_weight.shape[1]
+    n = lax.axis_size("wsh")
+    groups = lax.axis_size("grp")
+    if n != 8 or groups != 4 or span % 128 or hidden_cols % 128:
+        return plain_device(*arguments)
+    total_members = members * groups
+    per_member = all_rows // members
+    hops = n // 2
+    rows = all_rows // CHUNKS
+    half = rows // 2
+    wire = jnp.bfloat16
+
+    order = [2 * q for q in range(hops)] + [2 * (n - 1 - q) + 1 for q in range(hops, n)]
+    onward = [(order[q], order[(q + 1) % n]) for q in range(n)]
+    back = [(b, a) for a, b in onward]
+    place = ring_place(lax.axis_index("wsh"), n)
+    grp = lax.axis_index("grp")
+    at = jnp.concatenate([
+        ring_owner(place + jnp.arange(n, dtype=jnp.int32), n),
+        jnp.stack([grp // 2, 1 - grp // 2, grp % 2]),
+    ]).astype(jnp.int32)
+    slot_near, slot_far, slot_core = n, n + 1, n + 2
+
+    pair = [(g, g ^ 2) for g in range(4)]
+    mate = [(g, g ^ 1) for g in range(4)]
+    on = lambda a: lax.ppermute(a, "wsh", onward)
+    back_to = lambda a: lax.ppermute(a, "wsh", back)
+
+    weight_fit = (2.0 * fitness_rank.astype(jnp.float32) - (total_members - 1)) / (
+        total_members - 1
+    )
+    lefts, gate_w, up_w = stage([(gate_left, up_left), (gate_weight,), (up_weight,)], 4, "stage_one")
+    weights = (gate_w, up_w, lefts)
+
+    wide = lambda a: a.astype(jnp.float32)
+
+    def gather(piece, first):
+        count = rows // per_member
+        micros = 5 / CHUNKS
+        a = b = piece
+        total, early = None, []
+        pieces, slots = [piece], [0]
+        for hop in range(1, hops):
+            a, b = on(a), back_to(b)
+            if hop > 1:
+                total = grow(at, pieces, slots, weights, total, first, count, micros)
+                pieces, slots = [], []
+                early.append(total[2])
+            pieces, slots = pieces + [a, b], slots + [n - hop, hop]
+        top, bottom = on(a[:half]), back_to(b[half:])
+        total = grow(at, pieces, slots, weights, total, first, count, micros)
+        return total, top, bottom, early
+
+    def scatter(hidden, score, opposite_on, opposite_back, first, passed):
+        got_on, got_back = on(opposite_on), back_to(opposite_back)
+        micros = 4 / CHUNKS
+        rest = []
+        for hop in range(hops - 1, 0, -1):
+            slots = [hop, n - hop] if hop > 1 else [hop, n - hop, 0]
+            passing = () if hop > 1 else (passed,)
+            rest.append(shares(at, hidden, score, down_w, down_r, slots, span, first, per_member, micros, passing))
+            ahead, behind = rest[-1][:2]
+            if hop == hops - 1:
+                ahead = jnp.concatenate([ahead[:half] + wide(got_on), ahead[half:]], axis=0)
+                behind = jnp.concatenate([behind[:half], behind[half:] + wide(got_back)], axis=0)
+            else:
+                ahead = ahead + wide(got_on)
+                behind = behind + wide(got_back)
+            got_on, got_back = on(ahead.astype(wire)), back_to(behind.astype(wire))
+        return (rest[-1][2] + wide(got_on) + wide(got_back)).astype(jnp.bfloat16), rest[-1][3]
+
+    outs = []
+    for chunk in range(CHUNKS):
+        first = chunk * members // CHUNKS
+        total, top, bottom, early = gather(tokens[chunk * rows : (chunk + 1) * rows], first)
+        if chunk == 0:
+            rights, down_l, down_r, down_w = stage(
+                [(gate_right, up_right), (down_left,), (down_right,), (down_weight,)], 2, "stage_two", early[:1]
+            )
+            others = (rights, down_l, down_w, down_r)
+            far, near = messages(at, weight_fit[:, None], rights, lefts, early[1], slot_far, slot_near)
+            far_in = lax.ppermute(far, "grp", pair)
+            near_in = lax.ppermute(near, "grp", mate)
+        made = finish(at, total, top, bottom, weights, others, hops, first, per_member, wire)
+        outs.append((made, first))
+    mixed = []
+    for made, first in outs:
+        done, far_in = scatter(*made, first, far_in)
+        mixed.append(done)
+    far_mate = lax.ppermute(far_in, "grp", mate)
+    mixed = mixed[0] if CHUNKS == 1 else jnp.concatenate(mixed, axis=0)
+    scale = math.sqrt(width / total_members)
+    gate_step, up_step = outers(at, [near, near_in, far_in, far_mate], width // groups, hidden_cols, slot_core, scale)
+    return mixed, gate_step, up_step
+
+
 def solution(mesh):
     in_specs = (
         P("grp", "wsh"),

time: 104 us -> 62.9 us (0.60)
  matrix products: 40.1 us -> 0 us
  Pallas kernels: 0 us -> 23.1 us
  other arithmetic: 13 us -> 1.88 us
  local copies, waits for them, and re-layouts: 6.02 us -> 0.15 us
  waiting for transfers between devices: 20.7 us -> 17.3 us
  starting transfers between devices: 21.9 us -> 19.5 us
    dot_general x35 -> x0, matrix products: 40.1 us -> none  [the longest x8 15.5 us: grow(): jnp.dot(piece, up_w, preferred_element_type=jnp.float32)]
    pallas_call x0 -> x11, Pallas kernels: none -> 23.1 us  [call(): pl.pallas_call(body, out_shape=out_shape, in_specs=in_specs or [SMEM] + [...]
    mul x4 -> x0, local copies, waits for them, and re-layouts: 5.09 us -> none  [spread(): score.reshape(members, per_member)[:, :, None]]
    ppermute x20 -> x19, waiting for transfers between devices: 20.7 us -> 17.3 us  [the longest x8 10.3 us: per_device(): on = lambda a: lax.ppermute(a, 'wsh', onward)]
    mul x3 -> x0, other arithmetic: 3.33 us -> none  [spread(): noise_scale * right]
    concatenate x5 -> x3, other arithmetic: 3.18 us -> 0.12 us  [the longest x1 0.08 us: per_device(): jnp.concatenate([ring_owner(place + jnp.arange(n, dtype=jnp.int32), n), j...]
    ppermute x20 -> x19, starting transfers between devices: 21.9 us -> 19.5 us  [the longest x8 14.6 us: per_device(): on = lambda a: lax.ppermute(a, 'wsh', onward)]
    another operation x3 -> x2, other arithmetic: 2.01 us -> 0.06 us  [the longest x1 1.96 us: per_device(): lefts = jnp.stack([gate_left, up_left])]
  transfers between devices with their start and end apart: 20 -> 19, of which waited for: 9 -> 12; matrix products, arithmetic and copies ran while one was open for 43% -> 2% of each run, Pallas kernels for 0% -> 37%
where the time goes in v3:
time: 62.9 us; the launch traced here: 62.8 us
  Pallas kernels  23.1 us (37%)
  starting transfers between devices  19.5 us (31%)
  waiting for transfers between devices  17.3 us (28%)
  other arithmetic  1.88 us (3%)
  between operations  0.79 us (1%)
    pallas_call x11, Pallas kernels, call(): pl.pallas_call(body, out_shape=out_shape, in_specs=in_specs or [SMEM] + [...  23.1 us
    ppermute x8, starting transfers between devices, per_device(): on = lambda a: lax.ppermute(a, 'wsh', onward)  14.6 us
    ppermute x8, waiting for transfers between devices, per_device(): on = lambda a: lax.ppermute(a, 'wsh', onward)  10.3 us
    ppermute x8, waiting for transfers between devices, per_device(): back_to = lambda a: lax.ppermute(a, 'wsh', back)  7 us
    ppermute x8, starting transfers between devices, per_device(): back_to = lambda a: lax.ppermute(a, 'wsh', back)  3.21 us
    ppermute x1, starting transfers between devices, per_device(): far_in = lax.ppermute(far, 'grp', pair)  1.58 us
  transfers between devices with their start and end apart: 19, of which 12 were waited for; matrix products, arithmetic and copies ran while one was open for 2% of the time, Pallas kernels for 37%

profile of v3, /device:TPU:0, one launch (start us, length us, event | category | flops | bytes accessed | tf_op | source)
XLA Modules:
  0.0 62.8 jit_solution(5074635529258341140)
XLA Ops:
  0.6 3.1 %collective-permute-start = (bf16[512,256]{1,0:T(8,128)(2,1)}, bf16[512,256]{1,0:T(8,128)(2,1)S(1)}, u32[]{:S(2)}, u32[]{:S(2)}) collective-permute-start(bf16[512,256]{1,0:T(8,128)(2,1)} %refs_1_.4), channel_id=1, source_target_pairs={{0,2},{2,4},{4,6},{6,7},{7,5},{5,3},{3,1},{1,0},{8,10},{10,12},{12... | collective-permute-start | bytes 786440 | tf_op jit(solution)/shard_map/ppermute | solution.py:476
  3.7 0.7 %multiply_bitcast_fusion = f32[64,1]{0,1:T(1,128)S(1)} fusion(s32[64]{0:T(128)} %param.21), kind=kLoop, calls=%fused_computation.17 | loop fusion | flops 256 | bytes 512 | tf_op jit(solution)/shard_map/broadcast_in_dim | solution.py:531
  4.4 0.1 copy.21.refs_1_
  4.5 0.1 pad_add_fusion.refs_0_
  4.6 3.4 %stage_one.1 = (bf16[128,2048]{1,0:T(8,128)(2,1)S(1)}, bf16[2048,896]{1,0:T(8,128)(2,1)S(1)}, bf16[2048,896]{1,0:T(8,128)(2,1)S(1)}) custom-call(bf16[64,2048]{1,0:T(8,128)(2,1)} %refs_0_.2, bf16[64,2048]{1,0:T(8,128)(2,1)} %refs_1_.3, bf16[2048,896]{1,0:T(8,128)(2,1)} %refs_2_.2, bf16[2048,896]{1,0:T(8,128)(2,1)} %refs_3_.2), custom_call_target="tpu_custom_call" | custom-call | flops 4000000000 | bytes 1000000 | tf_op jit(solution)/shard_map/stage_one/pallas_call | solution.py:196
  8.0 2.2 %collective-permute-done.refs_2_ = bf16[512,256]{1,0:T(8,128)(2,1)S(1)} collective-permute-done((bf16[512,256]{1,0:T(8,128)(2,1)}, bf16[512,256]{1,0:T(8,128)(2,1)S(1)}, u32[]{:S(2)}, u32[]{:S(2)}) %collective-permute-start) | collective-permute-done | bytes 262176 | tf_op jit(solution)/shard_map/ppermute | solution.py:476
  10.1 1.8 %collective-permute-start.1 = (bf16[512,256]{1,0:T(8,128)(2,1)S(1)}, bf16[512,256]{1,0:T(8,128)(2,1)S(1)}, u32[]{:S(2)}, u32[]{:S(2)}) collective-permute-start(bf16[512,256]{1,0:T(8,128)(2,1)S(1)} %collective-permute-done.refs_2_), channel_id=1, source_target_pairs={{0,2},{2,4},{4,6},{6,7},{7,5},{5,3},{3,1},{1,0},{8,10},{10,12},{12... | collective-permute-start | bytes 786440 | tf_op jit(solution)/shard_map/ppermute | solution.py:476
  12.0 0.2 collective-permute-start.4
  12.2 2.6 %grow.3 = (f32[512,896]{1,0:T(8,128)S(1)}, f32[512,896]{1,0:T(8,128)S(1)}, f32[512,128]{1,0:T(8,128)S(1)}) custom-call(s32[11]{0:T(128)S(1)} %pad_add_fusion.refs_0_, bf16[512,256]{1,0:T(8,128)(2,1)S(1)} %copy-done, bf16[512,256]{1,0:T(8,128)(2,1)S(1)} %collective-permute-done.refs_2_, bf16[512,256]{1,0:T(8,128)(2,1)S(1)} %collective-permute-done.3.refs_3_, ...), custom_call_target="tpu_custom_call" | custom-call | flops 5000000000 | bytes 1000000 | tf_op jit(solution)/shard_map/grow/pallas_call | solution.py:196
  14.8 2.5 %stage_two.1 = (f32[128,896]{1,0:T(8,128)S(1)}, bf16[64,896]{1,0:T(8,128)(2,1)S(1)}, f32[64,2048]{1,0:T(8,128)S(1)}, bf16[896,2048]{1,0:T(8,128)(2,1)S(1)}) custom-call(f32[64,896]{1,0:T(8,128)} %refs_0_.3, f32[64,896]{1,0:T(8,128)} %refs_1_.5, bf16[64,896]{1,0:T(8,128)(2,1)} %refs_2_.3, f32[64,2048]{1,0:T(8,128)} %refs_3_.3, bf16[896,2048]{1,0:T(8,128)(2,1)} %refs_4_.1, ...), custom_call_target="tpu_custom_call" | custom-call | flops 2000000000 | bytes 1000000 | tf_op jit(solution)/shard_map/stage_two/pallas_call | solution.py:196
  17.3 0.3 collective-permute-done.1.refs_1_
  17.6 1.6 %collective-permute-start.2 = (bf16[512,256]{1,0:T(8,128)(2,1)S(1)}, bf16[512,256]{1,0:T(8,128)(2,1)S(1)}, u32[]{:S(2)}, u32[]{:S(2)}) collective-permute-start(bf16[512,256]{1,0:T(8,128)(2,1)S(1)} %collective-permute-done.1.refs_1_), channel_id=1, source_target_pairs={{0,2},{2,4},{4,6},{6,7},{7,5},{5,3},{3,1},{1,0},{8,10},{10,12},{12... | collective-permute-start | bytes 786440 | tf_op jit(solution)/shard_map/ppermute | solution.py:476
  19.2 0.5 collective-permute-start.5
  19.7 2.4 %grow.4 = (f32[512,896]{1,0:T(8,128)S(1)}, f32[512,896]{1,0:T(8,128)S(1)}, f32[512,128]{1,0:T(8,128)S(1)}) custom-call(s32[11]{0:T(128)S(1)} %pad_add_fusion.refs_0_, bf16[512,256]{1,0:T(8,128)(2,1)S(1)} %collective-permute-done.1.refs_1_, ...), custom_call_target="tpu_custom_call", output_to_operand_aliasing={{0}: (6, {}), {1}: (7, {}), {2}: (8, {})} | custom-call | flops 5000000000 | bytes 1000000 | tf_op jit(solution)/shard_map/grow/pallas_call | solution.py:196
  22.1 0.6 %messages.1 = (bf16[64,3840]{1,0:T(8,128)(2,1)S(1)}, bf16[64,3840]{1,0:T(8,128)(2,1)S(1)}) custom-call(s32[11]{0:T(128)S(1)} %pad_add_fusion.refs_0_, f32[64,1]{1,0:T(8,128)S(1)} %copy.21.refs_1_, f32[128,896]{1,0:T(8,128)S(1)} %get-tuple-element.47.refs_9_.refs_2_, bf16[128,2048]{1,0:T(8,128)(2,1)S(1)} %get-tuple-element.37.refs_6_.refs_5_.refs_8_.refs_3_, ...), custom_call_target="tpu_custom_call" | custom-call | flops 2000000000 | bytes 1000000 | tf_op jit(solution)/shard_map/messages/pallas_call | solution.py:196
  22.7 1.6 %collective-permute-start.8 = (bf16[64,3840]{1,0:T(8,128)(2,1)S(1)}, bf16[64,3840]{1,0:T(8,128)(2,1)S(1)}, u32[]{:S(2)}, u32[]{:S(2)}) collective-permute-start(bf16[64,3840]{1,0:T(8,128)(2,1)S(1)} %get-tuple-element.53), channel_id=1, source_target_pairs={{0,16},{8,24},{16,0},{24,8},{1,17},{9,25},{17,1},{25,9},{2,18},{10... | collective-permute-start | bytes 1474568 | tf_op jit(solution)/shard_map/ppermute | solution.py:532
  24.3 1.6 %collective-permute-start.6 = (bf16[256,256]{1,0:T(8,128)(2,1)S(1)}, bf16[256,256]{1,0:T(8,128)(2,1)S(1)}, u32[]{:S(2)}, u32[]{:S(2)}) collective-permute-start(bf16[256,256]{1,0:T(8,128)(2,1)S(1)} %slice.26), channel_id=1, source_target_pairs={{0,2},{2,4},{4,6},{6,7},{7,5},{5,3},{3,1},{1,0},{8,10},{10,12},{12... | collective-permute-start | bytes 393224 | tf_op jit(solution)/shard_map/ppermute | solution.py:476
  26.0 0.5 collective-permute-start.7
  26.5 2.4 %grow.5 = (f32[512,896]{1,0:T(8,128)S(1)}, f32[512,896]{1,0:T(8,128)S(1)}, f32[512,128]{1,0:T(8,128)S(1)}) custom-call(s32[11]{0:T(128)S(1)} %pad_add_fusion.refs_0_, bf16[512,256]{1,0:T(8,128)(2,1)S(1)} %collective-permute-done.2.refs_1_, ...), custom_call_target="tpu_custom_call", output_to_operand_aliasing={{0}: (6, {}), {1}: (7, {}), {2}: (8, {})} | custom-call | flops 5000000000 | bytes 1000000 | tf_op jit(solution)/shard_map/grow/pallas_call | solution.py:196
  28.9 1.4 %collective-permute-done.6.refs_4_ = bf16[256,256]{1,0:T(8,128)(2,1)S(1)} collective-permute-done((bf16[256,256]{1,0:T(8,128)(2,1)S(1)}, bf16[256,256]{1,0:T(8,128)(2,1)S(1)}, u32[]{:S(2)}, u32[]{:S(2)}) %collective-permute-start.6) | collective-permute-done | bytes 131104 | tf_op jit(solution)/shard_map/ppermute | solution.py:476
  30.3 1.4 %collective-permute-done.7.refs_5_ = bf16[256,256]{1,0:T(8,128)(2,1)S(1)} collective-permute-done((bf16[256,256]{1,0:T(8,128)(2,1)S(1)}, bf16[256,256]{1,0:T(8,128)(2,1)S(1)}, u32[]{:S(2)}, u32[]{:S(2)}) %collective-permute-start.7) | collective-permute-done | bytes 131104 | tf_op jit(solution)/shard_map/ppermute | solution.py:477
  31.7 2.8 %finish.1 = (bf16[512,896]{1,0:T(8,128)(2,1)S(1)}, f32[512,128]{1,0:T(8,128)S(1)}, bf16[256,256]{1,0:T(8,128)(2,1)S(1)}, bf16[256,256]{1,0:T(8,128)(2,1)S(1)}) custom-call(s32[11]{0:T(128)S(1)} %pad_add_fusion.refs_0_, f32[512,896]{1,0:T(8,128)S(1)} %get-tuple-element.44.refs_1_, f32[512,896]{1,0:T(8,128)S(1)} %get-tuple-element.45.refs_2_, ...), custom_call_target="tpu_custom_call" | custom-call | flops 4000000000 | bytes 1000000 | tf_op jit(solution)/shard_map/finish/pallas_call | solution.py:196
  34.5 1.6 %collective-permute-start.9 = (bf16[256,256]{1,0:T(8,128)(2,1)S(1)}, bf16[256,256]{1,0:T(8,128)(2,1)S(1)}, u32[]{:S(2)}, u32[]{:S(2)}) collective-permute-start(bf16[256,256]{1,0:T(8,128)(2,1)S(1)} %get-tuple-element.58), channel_id=1, source_target_pairs={{0,2},{2,4},{4,6},{6,7},{7,5},{5,3},{3,1},{1,0},{8,10},{10,12},{12... | collective-permute-start | bytes 393224 | tf_op jit(solution)/shard_map/ppermute | solution.py:476
  36.1 1.3 %shares.5 = (f32[512,256]{1,0:T(8,128)S(1)}, f32[512,256]{1,0:T(8,128)S(1)}) custom-call(s32[11]{0:T(128)S(1)} %pad_add_fusion.refs_0_, bf16[512,896]{1,0:T(8,128)(2,1)S(1)} %get-tuple-element.51.refs_1_, f32[512,128]{1,0:T(8,128)S(1)} %get-tuple-element.52.refs_2_, bf16[896,2048]{1,0:T(8,128)(2,1)S(1)} %get-tuple-element.49.refs_11_.refs_3_, ...), custom_call_target="tpu_custom_call" | custom-call | flops 4000000000 | bytes 1000000 | tf_op jit(solution)/shard_map/shares/pallas_call | solution.py:196
  37.4 0.5 collective-permute-start.13
  37.9 1.6 %collective-permute-done.9 = bf16[256,256]{1,0:T(8,128)(2,1)S(1)} collective-permute-done((bf16[256,256]{1,0:T(8,128)(2,1)S(1)}, bf16[256,256]{1,0:T(8,128)(2,1)S(1)}, u32[]{:S(2)}, u32[]{:S(2)}) %collective-permute-start.9) | collective-permute-done | bytes 131104 | tf_op jit(solution)/shard_map/ppermute | solution.py:476
  39.6 1.6 %collective-permute-start.10 = (bf16[512,256]{1,0:T(8,128)(2,1)S(1)}, bf16[512,256]{1,0:T(8,128)(2,1)S(1)}, u32[]{:S(2)}, u32[]{:S(2)}) collective-permute-start(bf16[512,256]{1,0:T(8,128)(2,1)S(1)} %pad_maximum_fusion), channel_id=1, source_target_pairs={{0,2},{2,4},{4,6},{6,7},{7,5},{5,3},{3,1},{1,0},{8,10},{10,12},{12... | collective-permute-start | bytes 786440 | tf_op jit(solution)/shard_map/ppermute | solution.py:476
  41.2 1.2 %collective-permute-done.13 = bf16[256,256]{1,0:T(8,128)(2,1)S(1)} collective-permute-done((bf16[256,256]{1,0:T(8,128)(2,1)S(1)}, bf16[256,256]{1,0:T(8,128)(2,1)S(1)}, u32[]{:S(2)}, u32[]{:S(2)}) %collective-permute-start.13) | collective-permute-done | bytes 131104 | tf_op jit(solution)/shard_map/ppermute | solution.py:477
  42.5 0.5 collective-permute-start.14
  43.0 1.3 %shares.4 = (f32[512,256]{1,0:T(8,128)S(1)}, f32[512,256]{1,0:T(8,128)S(1)}) custom-call(s32[11]{0:T(128)S(1)} %pad_add_fusion.refs_0_, bf16[512,896]{1,0:T(8,128)(2,1)S(1)} %get-tuple-element.51.refs_1_, f32[512,128]{1,0:T(8,128)S(1)} %get-tuple-element.52.refs_2_, bf16[896,2048]{1,0:T(8,128)(2,1)S(1)} %get-tuple-element.49.refs_11_.refs_3_, ...), custom_call_target="tpu_custom_call" | custom-call | flops 4000000000 | bytes 1000000 | tf_op jit(solution)/shard_map/shares/pallas_call | solution.py:196
  44.3 1.8 %collective-permute-done.10 = bf16[512,256]{1,0:T(8,128)(2,1)S(1)} collective-permute-done((bf16[512,256]{1,0:T(8,128)(2,1)S(1)}, bf16[512,256]{1,0:T(8,128)(2,1)S(1)}, u32[]{:S(2)}, u32[]{:S(2)}) %collective-permute-start.10) | collective-permute-done | bytes 262176 | tf_op jit(solution)/shard_map/ppermute | solution.py:476
  46.1 0.1 add_convert_fusion.4
  46.1 1.6 %collective-permute-start.11 = (bf16[512,256]{1,0:T(8,128)(2,1)S(1)}, bf16[512,256]{1,0:T(8,128)(2,1)S(1)}, u32[]{:S(2)}, u32[]{:S(2)}) collective-permute-start(bf16[512,256]{1,0:T(8,128)(2,1)S(1)} %add_convert_fusion.4), channel_id=1, source_target_pairs={{0,2},{2,4},{4,6},{6,7},{7,5},{5,3},{3,1},{1,0},{8,10},{10,12},{12... | collective-permute-start | bytes 786440 | tf_op jit(solution)/shard_map/ppermute | solution.py:476
  47.8 1.2 %collective-permute-done.14 = bf16[512,256]{1,0:T(8,128)(2,1)S(1)} collective-permute-done((bf16[512,256]{1,0:T(8,128)(2,1)S(1)}, bf16[512,256]{1,0:T(8,128)(2,1)S(1)}, u32[]{:S(2)}, u32[]{:S(2)}) %collective-permute-start.14) | collective-permute-done | bytes 262176 | tf_op jit(solution)/shard_map/ppermute | solution.py:477
  49.0 0.1 add_convert_fusion.2
  49.1 0.5 collective-permute-start.15
  49.6 1.5 %shares.3 = (f32[512,256]{1,0:T(8,128)S(1)}, f32[512,256]{1,0:T(8,128)S(1)}, f32[512,256]{1,0:T(8,128)S(1)}, bf16[64,3840]{1,0:T(8,128)(2,1)S(1)}) custom-call(s32[11]{0:T(128)S(1)} %pad_add_fusion.refs_0_, bf16[512,896]{1,0:T(8,128)(2,1)S(1)} %get-tuple-element.51.refs_1_, ...), custom_call_target="tpu_custom_call", output_to_operand_aliasing={{3}: (5, {})} | custom-call | flops 4000000000 | bytes 1000000 | tf_op jit(solution)/shard_map/shares/pallas_call | solution.py:196
  51.1 0.1 collective-permute-start.18
  51.2 1.4 %collective-permute-done.11 = bf16[512,256]{1,0:T(8,128)(2,1)S(1)} collective-permute-done((bf16[512,256]{1,0:T(8,128)(2,1)S(1)}, bf16[512,256]{1,0:T(8,128)(2,1)S(1)}, u32[]{:S(2)}, u32[]{:S(2)}) %collective-permute-start.11) | collective-permute-done | bytes 262176 | tf_op jit(solution)/shard_map/ppermute | solution.py:476
  52.6 0.1 add_convert_fusion.3
  52.6 1.6 %collective-permute-start.12 = (bf16[512,256]{1,0:T(8,128)(2,1)S(1)}, bf16[512,256]{1,0:T(8,128)(2,1)S(1)}, u32[]{:S(2)}, u32[]{:S(2)}) collective-permute-start(bf16[512,256]{1,0:T(8,128)(2,1)S(1)} %add_convert_fusion.3), channel_id=1, source_target_pairs={{0,2},{2,4},{4,6},{6,7},{7,5},{5,3},{3,1},{1,0},{8,10},{10,12},{12... | collective-permute-start | bytes 786440 | tf_op jit(solution)/shard_map/ppermute | solution.py:476
  54.3 1.2 %collective-permute-done.15 = bf16[512,256]{1,0:T(8,128)(2,1)S(1)} collective-permute-done((bf16[512,256]{1,0:T(8,128)(2,1)S(1)}, bf16[512,256]{1,0:T(8,128)(2,1)S(1)}, u32[]{:S(2)}, u32[]{:S(2)}) %collective-permute-start.15) | collective-permute-done | bytes 262176 | tf_op jit(solution)/shard_map/ppermute | solution.py:477
  55.5 0.1 add_convert_fusion.1
  55.5 0.5 collective-permute-start.16
  56.1 2.2 %outers.1 = (bf16[512,896]{1,0:T(8,128)(2,1)}, bf16[512,896]{1,0:T(8,128)(2,1)}) custom-call(s32[11]{0:T(128)S(1)} %pad_add_fusion.refs_0_, bf16[64,3840]{1,0:T(8,128)(2,1)S(1)} %get-tuple-element.63.refs_1_, bf16[64,3840]{1,0:T(8,128)(2,1)S(1)} %collective-permute-done.17.refs_2_, bf16[64,3840]{1,0:T(8,128)(2,1)S(1)} %get-tuple-element.64.refs_3_, ...), custom_call_target="tpu_custom_call" | custom-call | flops 5000000000 | bytes 1000000 | tf_op jit(solution)/shard_map/outers/pallas_call | solution.py:196
  58.3 1.7 %collective-permute-done.12 = bf16[512,256]{1,0:T(8,128)(2,1)S(1)} collective-permute-done((bf16[512,256]{1,0:T(8,128)(2,1)S(1)}, bf16[512,256]{1,0:T(8,128)(2,1)S(1)}, u32[]{:S(2)}, u32[]{:S(2)}) %collective-permute-start.12) | collective-permute-done | bytes 262176 | tf_op jit(solution)/shard_map/ppermute | solution.py:476
  60.0 1.9 %collective-permute-done.16 = bf16[512,256]{1,0:T(8,128)(2,1)S(1)} collective-permute-done((bf16[512,256]{1,0:T(8,128)(2,1)S(1)}, bf16[512,256]{1,0:T(8,128)(2,1)S(1)}, u32[]{:S(2)}, u32[]{:S(2)}) %collective-permute-start.16) | collective-permute-done | bytes 262176 | tf_op jit(solution)/shard_map/ppermute | solution.py:477
  62.0 0.8 %add_convert_fusion = bf16[512,256]{1,0:T(8,128)(2,1)} fusion(bf16[512,256]{1,0:T(8,128)(2,1)S(1)} %collective-permute-done.16, f32[512,256]{1,0:T(8,128)S(1)} %get-tuple-element.54, bf16[512,256]{1,0:T(8,128)(2,1)S(1)} %collective-permute-done.12), kind=kLoop, calls=%fused_computation | loop fusion | flops 655360 | bytes 1310720 | tf_op jit(solution)/shard_map/convert_element_type | solution.py:520
  (20 shorter events, 0.2 us)
Async XLA Ops:
  0.6 9.5 %collective-permute-start = (bf16[512,256]{1,0:T(8,128)(2,1)}, bf16[512,256]{1,0:T(8,128)(2,1)S(1)}, u32[]{:S(2)}, u32[]{:S(2)}) collective-permute-start(bf16[512,256]{1,0:T(8,128)(2,1)} %refs_1_.4), channel_id=1, source_target_pairs={{0,2},{2,4},{4,6},{6,7},{7,5},{5,3},{3,1},{1,0},{8,10},{10,12},{12... | collective-permute-start | bytes 786440 | tf_op jit(solution)/shard_map/ppermute | solution.py:476
  3.7 8.3 %collective-permute-start.3 = (bf16[512,256]{1,0:T(8,128)(2,1)}, bf16[512,256]{1,0:T(8,128)(2,1)S(1)}, u32[]{:S(2)}, u32[]{:S(2)}) collective-permute-start(bf16[512,256]{1,0:T(8,128)(2,1)} %refs_1_.4), channel_id=1, source_target_pairs={{2,0},{4,2},{6,4},{7,6},{5,7},{3,5},{1,3},{0,1},{10,8},{12,10},{14... | collective-permute-start | bytes 786440 | tf_op jit(solution)/shard_map/ppermute | solution.py:477
  4.6 7.6 %copy-start = (bf16[512,256]{1,0:T(8,128)(2,1)S(1)}, bf16[512,256]{1,0:T(8,128)(2,1)}, u32[]{:S(2)}) copy-start(bf16[512,256]{1,0:T(8,128)(2,1)} %refs_1_.4) | copy-start | bytes 786436
  10.1 7.5 %collective-permute-start.1 = (bf16[512,256]{1,0:T(8,128)(2,1)S(1)}, bf16[512,256]{1,0:T(8,128)(2,1)S(1)}, u32[]{:S(2)}, u32[]{:S(2)}) collective-permute-start(bf16[512,256]{1,0:T(8,128)(2,1)S(1)} %collective-permute-done.refs_2_), channel_id=1, source_target_pairs={{0,2},{2,4},{4,6},{6,7},{7,5},{5,3},{3,1},{1,0},{8,10},{10,12},{12... | collective-permute-start | bytes 786440 | tf_op jit(solution)/shard_map/ppermute | solution.py:476
  12.0 7.2 %collective-permute-start.4 = (bf16[512,256]{1,0:T(8,128)(2,1)S(1)}, bf16[512,256]{1,0:T(8,128)(2,1)S(1)}, u32[]{:S(2)}, u32[]{:S(2)}) collective-permute-start(bf16[512,256]{1,0:T(8,128)(2,1)S(1)} %collective-permute-done.3.refs_3_), channel_id=1, source_target_pairs={{2,0},{4,2},{6,4},{7,6},{5,7},{3,5},{1,3},{0,1},{10,8},{12,10},{14... | collective-permute-start | bytes 786440 | tf_op jit(solution)/shard_map/ppermute | solution.py:477
  17.6 6.7 %collective-permute-start.2 = (bf16[512,256]{1,0:T(8,128)(2,1)S(1)}, bf16[512,256]{1,0:T(8,128)(2,1)S(1)}, u32[]{:S(2)}, u32[]{:S(2)}) collective-permute-start(bf16[512,256]{1,0:T(8,128)(2,1)S(1)} %collective-permute-done.1.refs_1_), channel_id=1, source_target_pairs={{0,2},{2,4},{4,6},{6,7},{7,5},{5,3},{3,1},{1,0},{8,10},{10,12},{12... | collective-permute-start | bytes 786440 | tf_op jit(solution)/shard_map/ppermute | solution.py:476
  19.2 6.7 %collective-permute-start.5 = (bf16[512,256]{1,0:T(8,128)(2,1)S(1)}, bf16[512,256]{1,0:T(8,128)(2,1)S(1)}, u32[]{:S(2)}, u32[]{:S(2)}) collective-permute-start(bf16[512,256]{1,0:T(8,128)(2,1)S(1)} %collective-permute-done.4.refs_2_), channel_id=1, source_target_pairs={{2,0},{4,2},{6,4},{7,6},{5,7},{3,5},{1,3},{0,1},{10,8},{12,10},{14... | collective-permute-start | bytes 786440 | tf_op jit(solution)/shard_map/ppermute | solution.py:477
  22.7 26.9 %collective-permute-start.8 = (bf16[64,3840]{1,0:T(8,128)(2,1)S(1)}, bf16[64,3840]{1,0:T(8,128)(2,1)S(1)}, u32[]{:S(2)}, u32[]{:S(2)}) collective-permute-start(bf16[64,3840]{1,0:T(8,128)(2,1)S(1)} %get-tuple-element.53), channel_id=1, source_target_pairs={{0,16},{8,24},{16,0},{24,8},{1,17},{9,25},{17,1},{25,9},{2,18},{10... | collective-permute-start | bytes 1474568 | tf_op jit(solution)/shard_map/ppermute | solution.py:532
  24.3 31.8 %collective-permute-start.17 = (bf16[64,3840]{1,0:T(8,128)(2,1)S(1)}, bf16[64,3840]{1,0:T(8,128)(2,1)S(1)}, u32[]{:S(2)}, u32[]{:S(2)}) collective-permute-start(bf16[64,3840]{1,0:T(8,128)(2,1)S(1)} %get-tuple-element.63.refs_1_), channel_id=1, source_target_pairs={{0,8},{8,0},{16,24},{24,16},{1,9},{9,1},{17,25},{25,17},{2,10},{10... | collective-permute-start | bytes 1474568 | tf_op jit(solution)/shard_map/ppermute | solution.py:533
  24.3 6.0 %collective-permute-start.6 = (bf16[256,256]{1,0:T(8,128)(2,1)S(1)}, bf16[256,256]{1,0:T(8,128)(2,1)S(1)}, u32[]{:S(2)}, u32[]{:S(2)}) collective-permute-start(bf16[256,256]{1,0:T(8,128)(2,1)S(1)} %slice.26), channel_id=1, source_target_pairs={{0,2},{2,4},{4,6},{6,7},{7,5},{5,3},{3,1},{1,0},{8,10},{10,12},{12... | collective-permute-start | bytes 393224 | tf_op jit(solution)/shard_map/ppermute | solution.py:476
  26.0 5.7 %collective-permute-start.7 = (bf16[256,256]{1,0:T(8,128)(2,1)S(1)}, bf16[256,256]{1,0:T(8,128)(2,1)S(1)}, u32[]{:S(2)}, u32[]{:S(2)}) collective-permute-start(bf16[256,256]{1,0:T(8,128)(2,1)S(1)} %slice.27), channel_id=1, source_target_pairs={{2,0},{4,2},{6,4},{7,6},{5,7},{3,5},{1,3},{0,1},{10,8},{12,10},{14... | collective-permute-start | bytes 393224 | tf_op jit(solution)/shard_map/ppermute | solution.py:477
  34.5 5.0 %collective-permute-start.9 = (bf16[256,256]{1,0:T(8,128)(2,1)S(1)}, bf16[256,256]{1,0:T(8,128)(2,1)S(1)}, u32[]{:S(2)}, u32[]{:S(2)}) collective-permute-start(bf16[256,256]{1,0:T(8,128)(2,1)S(1)} %get-tuple-element.58), channel_id=1, source_target_pairs={{0,2},{2,4},{4,6},{6,7},{7,5},{5,3},{3,1},{1,0},{8,10},{10,12},{12... | collective-permute-start | bytes 393224 | tf_op jit(solution)/shard_map/ppermute | solution.py:476
  37.4 5.0 %collective-permute-start.13 = (bf16[256,256]{1,0:T(8,128)(2,1)S(1)}, bf16[256,256]{1,0:T(8,128)(2,1)S(1)}, u32[]{:S(2)}, u32[]{:S(2)}) collective-permute-start(bf16[256,256]{1,0:T(8,128)(2,1)S(1)} %get-tuple-element.62), channel_id=1, source_target_pairs={{2,0},{4,2},{6,4},{7,6},{5,7},{3,5},{1,3},{0,1},{10,8},{12,10},{14... | collective-permute-start | bytes 393224 | tf_op jit(solution)/shard_map/ppermute | solution.py:477
  39.6 6.5 %collective-permute-start.10 = (bf16[512,256]{1,0:T(8,128)(2,1)S(1)}, bf16[512,256]{1,0:T(8,128)(2,1)S(1)}, u32[]{:S(2)}, u32[]{:S(2)}) collective-permute-start(bf16[512,256]{1,0:T(8,128)(2,1)S(1)} %pad_maximum_fusion), channel_id=1, source_target_pairs={{0,2},{2,4},{4,6},{6,7},{7,5},{5,3},{3,1},{1,0},{8,10},{10,12},{12... | collective-permute-start | bytes 786440 | tf_op jit(solution)/shard_map/ppermute | solution.py:476
  42.5 6.5 %collective-permute-start.14 = (bf16[512,256]{1,0:T(8,128)(2,1)S(1)}, bf16[512,256]{1,0:T(8,128)(2,1)S(1)}, u32[]{:S(2)}, u32[]{:S(2)}) collective-permute-start(bf16[512,256]{1,0:T(8,128)(2,1)S(1)} %pad_maximum_fusion.1), channel_id=1, source_target_pairs={{2,0},{4,2},{6,4},{7,6},{5,7},{3,5},{1,3},{0,1},{10,8},{12,10},{14... | collective-permute-start | bytes 786440 | tf_op jit(solution)/shard_map/ppermute | solution.py:477
  46.1 6.4 %collective-permute-start.11 = (bf16[512,256]{1,0:T(8,128)(2,1)S(1)}, bf16[512,256]{1,0:T(8,128)(2,1)S(1)}, u32[]{:S(2)}, u32[]{:S(2)}) collective-permute-start(bf16[512,256]{1,0:T(8,128)(2,1)S(1)} %add_convert_fusion.4), channel_id=1, source_target_pairs={{0,2},{2,4},{4,6},{6,7},{7,5},{5,3},{3,1},{1,0},{8,10},{10,12},{12... | collective-permute-start | bytes 786440 | tf_op jit(solution)/shard_map/ppermute | solution.py:476
  49.1 6.4 %collective-permute-start.15 = (bf16[512,256]{1,0:T(8,128)(2,1)S(1)}, bf16[512,256]{1,0:T(8,128)(2,1)S(1)}, u32[]{:S(2)}, u32[]{:S(2)}) collective-permute-start(bf16[512,256]{1,0:T(8,128)(2,1)S(1)} %add_convert_fusion.2), channel_id=1, source_target_pairs={{2,0},{4,2},{6,4},{7,6},{5,7},{3,5},{1,3},{0,1},{10,8},{12,10},{14... | collective-permute-start | bytes 786440 | tf_op jit(solution)/shard_map/ppermute | solution.py:477
  51.1 4.9 %collective-permute-start.18 = (bf16[64,3840]{1,0:T(8,128)(2,1)S(1)}, bf16[64,3840]{1,0:T(8,128)(2,1)S(1)}, u32[]{:S(2)}, u32[]{:S(2)}) collective-permute-start(bf16[64,3840]{1,0:T(8,128)(2,1)S(1)} %get-tuple-element.64.refs_3_), channel_id=1, source_target_pairs={{0,8},{8,0},{16,24},{24,16},{1,9},{9,1},{17,25},{25,17},{2,10},{10... | collective-permute-start | bytes 1474568 | tf_op jit(solution)/shard_map/ppermute | solution.py:540
  52.6 7.4 %collective-permute-start.12 = (bf16[512,256]{1,0:T(8,128)(2,1)S(1)}, bf16[512,256]{1,0:T(8,128)(2,1)S(1)}, u32[]{:S(2)}, u32[]{:S(2)}) collective-permute-start(bf16[512,256]{1,0:T(8,128)(2,1)S(1)} %add_convert_fusion.3), channel_id=1, source_target_pairs={{0,2},{2,4},{4,6},{6,7},{7,5},{5,3},{3,1},{1,0},{8,10},{10,12},{12... | collective-permute-start | bytes 786440 | tf_op jit(solution)/shard_map/ppermute | solution.py:476
  55.5 6.4 %collective-permute-start.16 = (bf16[512,256]{1,0:T(8,128)(2,1)S(1)}, bf16[512,256]{1,0:T(8,128)(2,1)S(1)}, u32[]{:S(2)}, u32[]{:S(2)}) collective-permute-start(bf16[512,256]{1,0:T(8,128)(2,1)S(1)} %add_convert_fusion.1), channel_id=1, source_target_pairs={{2,0},{4,2},{6,4},{7,6},{5,7},{3,5},{1,3},{0,1},{10,8},{12,10},{14... | collective-permute-start | bytes 786440 | tf_op jit(solution)/shard_map/ppermute | solution.py:477

commit v4 on v3

--- a/solution.py
+++ b/solution.py
@@ -507,7 +507,7 @@
         rest = []
         for hop in range(hops - 1, 0, -1):
             slots = [hop, n - hop] if hop > 1 else [hop, n - hop, 0]
-            passing = () if hop > 1 else (passed,)
+            passing = (passed,) if hop == 3 else ()
             rest.append(shares(at, hidden, score, down_w, down_r, slots, span, first, per_member, micros, passing))
             ahead, behind = rest[-1][:2]
             if hop == hops - 1:
@@ -517,7 +517,7 @@
                 ahead = ahead + wide(got_on)
                 behind = behind + wide(got_back)
             got_on, got_back = on(ahead.astype(wire)), back_to(behind.astype(wire))
-        return (rest[-1][2] + wide(got_on) + wide(got_back)).astype(jnp.bfloat16), rest[-1][3]
+        return (rest[-1][2] + wide(got_on) + wide(got_back)).astype(jnp.bfloat16), rest[-3][2]
 
     outs = []
     for chunk in range(CHUNKS):

time: 62.9 us -> 61.7 us (0.981)
  waiting for transfers between devices: 17.3 us -> 16.2 us
    ppermute x8, waiting for transfers between devices: 7 us -> 3.09 us  [per_device(): back_to = lambda a: lax.ppermute(a, 'wsh', back)]
    ppermute x8, waiting for transfers between devices: 10.3 us -> 13.1 us  [per_device(): on = lambda a: lax.ppermute(a, 'wsh', onward)]
  transfers between devices with their start and end apart: 19 -> 19, of which waited for: 12 -> 9; matrix products, arithmetic and copies ran while one was open for 2% -> 2% of each run, Pallas kernels for 37% -> 38%
where the time goes in v4:
time: 61.7 us; the launch traced here: 61.6 us
  Pallas kernels  23.1 us (37%)
  starting transfers between devices  19.4 us (31%)
  waiting for transfers between devices  16.2 us (26%)
  other arithmetic  1.89 us (3%)
  between operations  0.79 us (1%)
    pallas_call x11, Pallas kernels, call(): pl.pallas_call(body, out_shape=out_shape, in_specs=in_specs or [SMEM] + [...  23.1 us
    ppermute x8, starting transfers between devices, per_device(): on = lambda a: lax.ppermute(a, 'wsh', onward)  14.6 us
    ppermute x8, waiting for transfers between devices, per_device(): on = lambda a: lax.ppermute(a, 'wsh', onward)  13.1 us
    ppermute x8, starting transfers between devices, per_device(): back_to = lambda a: lax.ppermute(a, 'wsh', back)  3.1 us
    ppermute x8, waiting for transfers between devices, per_device(): back_to = lambda a: lax.ppermute(a, 'wsh', back)  3.09 us
    ppermute x1, starting transfers between devices, per_device(): far_in = lax.ppermute(far, 'grp', pair)  1.58 us
  transfers between devices with their start and end apart: 19, of which 9 were waited for; matrix products, arithmetic and copies ran while one was open for 2% of the time, Pallas kernels for 38%

profile of v4, /device:TPU:0, one launch (start us, length us, event | category | flops | bytes accessed | tf_op | source)
XLA Modules:
  0.0 61.6 jit_solution(14560963710447289795)
XLA Ops:
  0.6 3.1 %collective-permute-start = (bf16[512,256]{1,0:T(8,128)(2,1)}, bf16[512,256]{1,0:T(8,128)(2,1)S(1)}, u32[]{:S(2)}, u32[]{:S(2)}) collective-permute-start(bf16[512,256]{1,0:T(8,128)(2,1)} %refs_1_.4), channel_id=1, source_target_pairs={{0,2},{2,4},{4,6},{6,7},{7,5},{5,3},{3,1},{1,0},{8,10},{10,12},{12... | collective-permute-start | bytes 786440 | tf_op jit(solution)/shard_map/ppermute | solution.py:476
  3.7 0.0 collective-permute-start.3
  3.7 0.7 %multiply_bitcast_fusion = f32[64,1]{0,1:T(1,128)S(1)} fusion(s32[64]{0:T(128)} %param.21), kind=kLoop, calls=%fused_computation.17 | loop fusion | flops 256 | bytes 512 | tf_op jit(solution)/shard_map/broadcast_in_dim | solution.py:531
  4.4 0.1 copy.21.refs_1_
  4.5 0.1 pad_add_fusion.refs_0_
  4.6 3.4 %stage_one.1 = (bf16[128,2048]{1,0:T(8,128)(2,1)S(1)}, bf16[2048,896]{1,0:T(8,128)(2,1)S(1)}, bf16[2048,896]{1,0:T(8,128)(2,1)S(1)}) custom-call(bf16[64,2048]{1,0:T(8,128)(2,1)} %refs_0_.2, bf16[64,2048]{1,0:T(8,128)(2,1)} %refs_1_.3, bf16[2048,896]{1,0:T(8,128)(2,1)} %refs_2_.2, bf16[2048,896]{1,0:T(8,128)(2,1)} %refs_3_.2), custom_call_target="tpu_custom_call" | custom-call | flops 4000000000 | bytes 1000000 | tf_op jit(solution)/shard_map/stage_one/pallas_call | solution.py:196
  8.0 2.2 %collective-permute-done.refs_2_ = bf16[512,256]{1,0:T(8,128)(2,1)S(1)} collective-permute-done((bf16[512,256]{1,0:T(8,128)(2,1)}, bf16[512,256]{1,0:T(8,128)(2,1)S(1)}, u32[]{:S(2)}, u32[]{:S(2)}) %collective-permute-start) | collective-permute-done | bytes 262176 | tf_op jit(solution)/shard_map/ppermute | solution.py:476
  10.1 1.8 %collective-permute-start.1 = (bf16[512,256]{1,0:T(8,128)(2,1)S(1)}, bf16[512,256]{1,0:T(8,128)(2,1)S(1)}, u32[]{:S(2)}, u32[]{:S(2)}) collective-permute-start(bf16[512,256]{1,0:T(8,128)(2,1)S(1)} %collective-permute-done.refs_2_), channel_id=1, source_target_pairs={{0,2},{2,4},{4,6},{6,7},{7,5},{5,3},{3,1},{1,0},{8,10},{10,12},{12... | collective-permute-start | bytes 786440 | tf_op jit(solution)/shard_map/ppermute | solution.py:476
  12.0 0.2 collective-permute-start.4
  12.2 2.6 %grow.3 = (f32[512,896]{1,0:T(8,128)S(1)}, f32[512,896]{1,0:T(8,128)S(1)}, f32[512,128]{1,0:T(8,128)S(1)}) custom-call(s32[11]{0:T(128)S(1)} %pad_add_fusion.refs_0_, bf16[512,256]{1,0:T(8,128)(2,1)S(1)} %copy-done, bf16[512,256]{1,0:T(8,128)(2,1)S(1)} %collective-permute-done.refs_2_, bf16[512,256]{1,0:T(8,128)(2,1)S(1)} %collective-permute-done.3.refs_3_, ...), custom_call_target="tpu_custom_call" | custom-call | flops 5000000000 | bytes 1000000 | tf_op jit(solution)/shard_map/grow/pallas_call | solution.py:196
  14.8 2.5 %stage_two.1 = (f32[128,896]{1,0:T(8,128)S(1)}, bf16[64,896]{1,0:T(8,128)(2,1)S(1)}, f32[64,2048]{1,0:T(8,128)S(1)}, bf16[896,2048]{1,0:T(8,128)(2,1)S(1)}) custom-call(f32[64,896]{1,0:T(8,128)} %refs_0_.3, f32[64,896]{1,0:T(8,128)} %refs_1_.5, bf16[64,896]{1,0:T(8,128)(2,1)} %refs_2_.3, f32[64,2048]{1,0:T(8,128)} %refs_3_.3, bf16[896,2048]{1,0:T(8,128)(2,1)} %refs_4_.1, ...), custom_call_target="tpu_custom_call" | custom-call | flops 2000000000 | bytes 1000000 | tf_op jit(solution)/shard_map/stage_two/pallas_call | solution.py:196
  17.3 0.3 collective-permute-done.1.refs_1_
  17.6 1.6 %collective-permute-start.2 = (bf16[512,256]{1,0:T(8,128)(2,1)S(1)}, bf16[512,256]{1,0:T(8,128)(2,1)S(1)}, u32[]{:S(2)}, u32[]{:S(2)}) collective-permute-start(bf16[512,256]{1,0:T(8,128)(2,1)S(1)} %collective-permute-done.1.refs_1_), channel_id=1, source_target_pairs={{0,2},{2,4},{4,6},{6,7},{7,5},{5,3},{3,1},{1,0},{8,10},{10,12},{12... | collective-permute-start | bytes 786440 | tf_op jit(solution)/shard_map/ppermute | solution.py:476
  19.2 0.5 collective-permute-start.5
  19.7 2.4 %grow.4 = (f32[512,896]{1,0:T(8,128)S(1)}, f32[512,896]{1,0:T(8,128)S(1)}, f32[512,128]{1,0:T(8,128)S(1)}) custom-call(s32[11]{0:T(128)S(1)} %pad_add_fusion.refs_0_, bf16[512,256]{1,0:T(8,128)(2,1)S(1)} %collective-permute-done.1.refs_1_, ...), custom_call_target="tpu_custom_call", output_to_operand_aliasing={{0}: (6, {}), {1}: (7, {}), {2}: (8, {})} | custom-call | flops 5000000000 | bytes 1000000 | tf_op jit(solution)/shard_map/grow/pallas_call | solution.py:196
  22.1 0.6 %messages.1 = (bf16[64,3840]{1,0:T(8,128)(2,1)S(1)}, bf16[64,3840]{1,0:T(8,128)(2,1)S(1)}) custom-call(s32[11]{0:T(128)S(1)} %pad_add_fusion.refs_0_, f32[64,1]{1,0:T(8,128)S(1)} %copy.21.refs_1_, f32[128,896]{1,0:T(8,128)S(1)} %get-tuple-element.47.refs_9_.refs_2_, bf16[128,2048]{1,0:T(8,128)(2,1)S(1)} %get-tuple-element.37.refs_6_.refs_5_.refs_8_.refs_3_, ...), custom_call_target="tpu_custom_call" | custom-call | flops 2000000000 | bytes 1000000 | tf_op jit(solution)/shard_map/messages/pallas_call | solution.py:196
  22.7 1.6 %collective-permute-start.8 = (bf16[64,3840]{1,0:T(8,128)(2,1)S(1)}, bf16[64,3840]{1,0:T(8,128)(2,1)S(1)}, u32[]{:S(2)}, u32[]{:S(2)}) collective-permute-start(bf16[64,3840]{1,0:T(8,128)(2,1)S(1)} %get-tuple-element.56), channel_id=1, source_target_pairs={{0,16},{8,24},{16,0},{24,8},{1,17},{9,25},{17,1},{25,9},{2,18},{10... | collective-permute-start | bytes 1474568 | tf_op jit(solution)/shard_map/ppermute | solution.py:532
  24.3 0.0 collective-permute-done.2.refs_1_
  24.3 1.6 %collective-permute-start.6 = (bf16[256,256]{1,0:T(8,128)(2,1)S(1)}, bf16[256,256]{1,0:T(8,128)(2,1)S(1)}, u32[]{:S(2)}, u32[]{:S(2)}) collective-permute-start(bf16[256,256]{1,0:T(8,128)(2,1)S(1)} %slice.26), channel_id=1, source_target_pairs={{0,2},{2,4},{4,6},{6,7},{7,5},{5,3},{3,1},{1,0},{8,10},{10,12},{12... | collective-permute-start | bytes 393224 | tf_op jit(solution)/shard_map/ppermute | solution.py:476
  26.0 0.5 collective-permute-start.7
  26.5 2.4 %grow.5 = (f32[512,896]{1,0:T(8,128)S(1)}, f32[512,896]{1,0:T(8,128)S(1)}, f32[512,128]{1,0:T(8,128)S(1)}) custom-call(s32[11]{0:T(128)S(1)} %pad_add_fusion.refs_0_, bf16[512,256]{1,0:T(8,128)(2,1)S(1)} %collective-permute-done.2.refs_1_, ...), custom_call_target="tpu_custom_call", output_to_operand_aliasing={{0}: (6, {}), {1}: (7, {}), {2}: (8, {})} | custom-call | flops 5000000000 | bytes 1000000 | tf_op jit(solution)/shard_map/grow/pallas_call | solution.py:196
  28.9 1.4 %collective-permute-done.6.refs_4_ = bf16[256,256]{1,0:T(8,128)(2,1)S(1)} collective-permute-done((bf16[256,256]{1,0:T(8,128)(2,1)S(1)}, bf16[256,256]{1,0:T(8,128)(2,1)S(1)}, u32[]{:S(2)}, u32[]{:S(2)}) %collective-permute-start.6) | collective-permute-done | bytes 131104 | tf_op jit(solution)/shard_map/ppermute | solution.py:476
  30.3 1.4 %collective-permute-done.7.refs_5_ = bf16[256,256]{1,0:T(8,128)(2,1)S(1)} collective-permute-done((bf16[256,256]{1,0:T(8,128)(2,1)S(1)}, bf16[256,256]{1,0:T(8,128)(2,1)S(1)}, u32[]{:S(2)}, u32[]{:S(2)}) %collective-permute-start.7) | collective-permute-done | bytes 131104 | tf_op jit(solution)/shard_map/ppermute | solution.py:477
  31.7 2.8 %finish.1 = (bf16[512,896]{1,0:T(8,128)(2,1)S(1)}, f32[512,128]{1,0:T(8,128)S(1)}, bf16[256,256]{1,0:T(8,128)(2,1)S(1)}, bf16[256,256]{1,0:T(8,128)(2,1)S(1)}) custom-call(s32[11]{0:T(128)S(1)} %pad_add_fusion.refs_0_, f32[512,896]{1,0:T(8,128)S(1)} %get-tuple-element.44.refs_1_, f32[512,896]{1,0:T(8,128)S(1)} %get-tuple-element.45.refs_2_, ...), custom_call_target="tpu_custom_call" | custom-call | flops 4000000000 | bytes 1000000 | tf_op jit(solution)/shard_map/finish/pallas_call | solution.py:196
  34.5 1.6 %collective-permute-start.9 = (bf16[256,256]{1,0:T(8,128)(2,1)S(1)}, bf16[256,256]{1,0:T(8,128)(2,1)S(1)}, u32[]{:S(2)}, u32[]{:S(2)}) collective-permute-start(bf16[256,256]{1,0:T(8,128)(2,1)S(1)} %get-tuple-element.58), channel_id=1, source_target_pairs={{0,2},{2,4},{4,6},{6,7},{7,5},{5,3},{3,1},{1,0},{8,10},{10,12},{12... | collective-permute-start | bytes 393224 | tf_op jit(solution)/shard_map/ppermute | solution.py:476
  36.1 0.4 collective-permute-start.13
  36.6 1.3 %shares.5 = (f32[512,256]{1,0:T(8,128)S(1)}, f32[512,256]{1,0:T(8,128)S(1)}, bf16[64,3840]{1,0:T(8,128)(2,1)S(1)}) custom-call(s32[11]{0:T(128)S(1)} %pad_add_fusion.refs_0_, bf16[512,896]{1,0:T(8,128)(2,1)S(1)} %get-tuple-element.51.refs_1_, f32[512,128]{1,0:T(8,128)S(1)} %get-tuple-element.52.refs_2_, ...), custom_call_target="tpu_custom_call", output_to_operand_aliasing={{2}: (5, {})} | custom-call | flops 4000000000 | bytes 1000000 | tf_op jit(solution)/shard_map/shares/pallas_call | solution.py:196
  37.9 1.6 %collective-permute-done.9 = bf16[256,256]{1,0:T(8,128)(2,1)S(1)} collective-permute-done((bf16[256,256]{1,0:T(8,128)(2,1)S(1)}, bf16[256,256]{1,0:T(8,128)(2,1)S(1)}, u32[]{:S(2)}, u32[]{:S(2)}) %collective-permute-start.9) | collective-permute-done | bytes 131104 | tf_op jit(solution)/shard_map/ppermute | solution.py:476
  39.6 1.6 %collective-permute-start.10 = (bf16[512,256]{1,0:T(8,128)(2,1)S(1)}, bf16[512,256]{1,0:T(8,128)(2,1)S(1)}, u32[]{:S(2)}, u32[]{:S(2)}) collective-permute-start(bf16[512,256]{1,0:T(8,128)(2,1)S(1)} %pad_maximum_fusion), channel_id=1, source_target_pairs={{0,2},{2,4},{4,6},{6,7},{7,5},{5,3},{3,1},{1,0},{8,10},{10,12},{12... | collective-permute-start | bytes 786440 | tf_op jit(solution)/shard_map/ppermute | solution.py:476
  41.2 0.5 collective-permute-start.14
  41.7 1.3 %shares.4 = (f32[512,256]{1,0:T(8,128)S(1)}, f32[512,256]{1,0:T(8,128)S(1)}) custom-call(s32[11]{0:T(128)S(1)} %pad_add_fusion.refs_0_, bf16[512,896]{1,0:T(8,128)(2,1)S(1)} %get-tuple-element.51.refs_1_, f32[512,128]{1,0:T(8,128)S(1)} %get-tuple-element.52.refs_2_, bf16[896,2048]{1,0:T(8,128)(2,1)S(1)} %get-tuple-element.49.refs_11_.refs_3_, ...), custom_call_target="tpu_custom_call" | custom-call | flops 4000000000 | bytes 1000000 | tf_op jit(solution)/shard_map/shares/pallas_call | solution.py:196
  43.0 3.1 %collective-permute-done.10 = bf16[512,256]{1,0:T(8,128)(2,1)S(1)} collective-permute-done((bf16[512,256]{1,0:T(8,128)(2,1)S(1)}, bf16[512,256]{1,0:T(8,128)(2,1)S(1)}, u32[]{:S(2)}, u32[]{:S(2)}) %collective-permute-start.10) | collective-permute-done | bytes 262176 | tf_op jit(solution)/shard_map/ppermute | solution.py:476
  46.1 0.1 add_convert_fusion.4
  46.1 1.6 %collective-permute-start.11 = (bf16[512,256]{1,0:T(8,128)(2,1)S(1)}, bf16[512,256]{1,0:T(8,128)(2,1)S(1)}, u32[]{:S(2)}, u32[]{:S(2)}) collective-permute-start(bf16[512,256]{1,0:T(8,128)(2,1)S(1)} %add_convert_fusion.4), channel_id=1, source_target_pairs={{0,2},{2,4},{4,6},{6,7},{7,5},{5,3},{3,1},{1,0},{8,10},{10,12},{12... | collective-permute-start | bytes 786440 | tf_op jit(solution)/shard_map/ppermute | solution.py:476
  47.8 0.1 add_convert_fusion.2
  47.8 0.5 collective-permute-start.15
  48.3 1.5 %shares.3 = (f32[512,256]{1,0:T(8,128)S(1)}, f32[512,256]{1,0:T(8,128)S(1)}, f32[512,256]{1,0:T(8,128)S(1)}) custom-call(s32[11]{0:T(128)S(1)} %pad_add_fusion.refs_0_, bf16[512,896]{1,0:T(8,128)(2,1)S(1)} %get-tuple-element.51.refs_1_, f32[512,128]{1,0:T(8,128)S(1)} %get-tuple-element.52.refs_2_, bf16[896,2048]{1,0:T(8,128)(2,1)S(1)} %get-tuple-element.49.refs_11_.refs_3_, ...), custom_call_target="tpu_custom_call" | custom-call | flops 4000000000 | bytes 1000000 | tf_op jit(solution)/shard_map/shares/pallas_call | solution.py:196
  49.9 0.1 collective-permute-start.18
  50.0 2.6 %collective-permute-done.11 = bf16[512,256]{1,0:T(8,128)(2,1)S(1)} collective-permute-done((bf16[512,256]{1,0:T(8,128)(2,1)S(1)}, bf16[512,256]{1,0:T(8,128)(2,1)S(1)}, u32[]{:S(2)}, u32[]{:S(2)}) %collective-permute-start.11) | collective-permute-done | bytes 262176 | tf_op jit(solution)/shard_map/ppermute | solution.py:476
  52.6 0.1 add_convert_fusion.3
  52.6 1.6 %collective-permute-start.12 = (bf16[512,256]{1,0:T(8,128)(2,1)S(1)}, bf16[512,256]{1,0:T(8,128)(2,1)S(1)}, u32[]{:S(2)}, u32[]{:S(2)}) collective-permute-start(bf16[512,256]{1,0:T(8,128)(2,1)S(1)} %add_convert_fusion.3), channel_id=1, source_target_pairs={{0,2},{2,4},{4,6},{6,7},{7,5},{5,3},{3,1},{1,0},{8,10},{10,12},{12... | collective-permute-start | bytes 786440 | tf_op jit(solution)/shard_map/ppermute | solution.py:476
  54.3 0.0 collective-permute-done.15
  54.3 0.1 add_convert_fusion.1
  54.3 0.5 collective-permute-start.16
  54.8 2.2 %outers.1 = (bf16[512,896]{1,0:T(8,128)(2,1)}, bf16[512,896]{1,0:T(8,128)(2,1)}) custom-call(s32[11]{0:T(128)S(1)} %pad_add_fusion.refs_0_, bf16[64,3840]{1,0:T(8,128)(2,1)S(1)} %get-tuple-element.63.refs_1_, bf16[64,3840]{1,0:T(8,128)(2,1)S(1)} %collective-permute-done.17.refs_2_, bf16[64,3840]{1,0:T(8,128)(2,1)S(1)} %get-tuple-element.64.refs_3_, ...), custom_call_target="tpu_custom_call" | custom-call | flops 5000000000 | bytes 1000000 | tf_op jit(solution)/shard_map/outers/pallas_call | solution.py:196
  57.1 2.0 %collective-permute-done.12 = bf16[512,256]{1,0:T(8,128)(2,1)S(1)} collective-permute-done((bf16[512,256]{1,0:T(8,128)(2,1)S(1)}, bf16[512,256]{1,0:T(8,128)(2,1)S(1)}, u32[]{:S(2)}, u32[]{:S(2)}) %collective-permute-start.12) | collective-permute-done | bytes 262176 | tf_op jit(solution)/shard_map/ppermute | solution.py:476
  59.0 1.7 %collective-permute-done.16 = bf16[512,256]{1,0:T(8,128)(2,1)S(1)} collective-permute-done((bf16[512,256]{1,0:T(8,128)(2,1)S(1)}, bf16[512,256]{1,0:T(8,128)(2,1)S(1)}, u32[]{:S(2)}, u32[]{:S(2)}) %collective-permute-start.16) | collective-permute-done | bytes 262176 | tf_op jit(solution)/shard_map/ppermute | solution.py:477
  60.8 0.8 %add_convert_fusion = bf16[512,256]{1,0:T(8,128)(2,1)} fusion(bf16[512,256]{1,0:T(8,128)(2,1)S(1)} %collective-permute-done.16, f32[512,256]{1,0:T(8,128)S(1)} %get-tuple-element.53, bf16[512,256]{1,0:T(8,128)(2,1)S(1)} %collective-permute-done.12), kind=kLoop, calls=%fused_computation | loop fusion | flops 655360 | bytes 1310720 | tf_op jit(solution)/shard_map/convert_element_type | solution.py:520
  (20 shorter events, 0.2 us)
Async XLA Ops:
  0.6 9.5 %collective-permute-start = (bf16[512,256]{1,0:T(8,128)(2,1)}, bf16[512,256]{1,0:T(8,128)(2,1)S(1)}, u32[]{:S(2)}, u32[]{:S(2)}) collective-permute-start(bf16[512,256]{1,0:T(8,128)(2,1)} %refs_1_.4), channel_id=1, source_target_pairs={{0,2},{2,4},{4,6},{6,7},{7,5},{5,3},{3,1},{1,0},{8,10},{10,12},{12... | collective-permute-start | bytes 786440 | tf_op jit(solution)/shard_map/ppermute | solution.py:476
  3.7 8.3 %collective-permute-start.3 = (bf16[512,256]{1,0:T(8,128)(2,1)}, bf16[512,256]{1,0:T(8,128)(2,1)S(1)}, u32[]{:S(2)}, u32[]{:S(2)}) collective-permute-start(bf16[512,256]{1,0:T(8,128)(2,1)} %refs_1_.4), channel_id=1, source_target_pairs={{2,0},{4,2},{6,4},{7,6},{5,7},{3,5},{1,3},{0,1},{10,8},{12,10},{14... | collective-permute-start | bytes 786440 | tf_op jit(solution)/shard_map/ppermute | solution.py:477
  4.6 7.6 %copy-start = (bf16[512,256]{1,0:T(8,128)(2,1)S(1)}, bf16[512,256]{1,0:T(8,128)(2,1)}, u32[]{:S(2)}) copy-start(bf16[512,256]{1,0:T(8,128)(2,1)} %refs_1_.4) | copy-start | bytes 786436
  10.1 7.5 %collective-permute-start.1 = (bf16[512,256]{1,0:T(8,128)(2,1)S(1)}, bf16[512,256]{1,0:T(8,128)(2,1)S(1)}, u32[]{:S(2)}, u32[]{:S(2)}) collective-permute-start(bf16[512,256]{1,0:T(8,128)(2,1)S(1)} %collective-permute-done.refs_2_), channel_id=1, source_target_pairs={{0,2},{2,4},{4,6},{6,7},{7,5},{5,3},{3,1},{1,0},{8,10},{10,12},{12... | collective-permute-start | bytes 786440 | tf_op jit(solution)/shard_map/ppermute | solution.py:476
  12.0 7.2 %collective-permute-start.4 = (bf16[512,256]{1,0:T(8,128)(2,1)S(1)}, bf16[512,256]{1,0:T(8,128)(2,1)S(1)}, u32[]{:S(2)}, u32[]{:S(2)}) collective-permute-start(bf16[512,256]{1,0:T(8,128)(2,1)S(1)} %collective-permute-done.3.refs_3_), channel_id=1, source_target_pairs={{2,0},{4,2},{6,4},{7,6},{5,7},{3,5},{1,3},{0,1},{10,8},{12,10},{14... | collective-permute-start | bytes 786440 | tf_op jit(solution)/shard_map/ppermute | solution.py:477
  17.6 6.7 %collective-permute-start.2 = (bf16[512,256]{1,0:T(8,128)(2,1)S(1)}, bf16[512,256]{1,0:T(8,128)(2,1)S(1)}, u32[]{:S(2)}, u32[]{:S(2)}) collective-permute-start(bf16[512,256]{1,0:T(8,128)(2,1)S(1)} %collective-permute-done.1.refs_1_), channel_id=1, source_target_pairs={{0,2},{2,4},{4,6},{6,7},{7,5},{5,3},{3,1},{1,0},{8,10},{10,12},{12... | collective-permute-start | bytes 786440 | tf_op jit(solution)/shard_map/ppermute | solution.py:476
  19.2 6.7 %collective-permute-start.5 = (bf16[512,256]{1,0:T(8,128)(2,1)S(1)}, bf16[512,256]{1,0:T(8,128)(2,1)S(1)}, u32[]{:S(2)}, u32[]{:S(2)}) collective-permute-start(bf16[512,256]{1,0:T(8,128)(2,1)S(1)} %collective-permute-done.4.refs_2_), channel_id=1, source_target_pairs={{2,0},{4,2},{6,4},{7,6},{5,7},{3,5},{1,3},{0,1},{10,8},{12,10},{14... | collective-permute-start | bytes 786440 | tf_op jit(solution)/shard_map/ppermute | solution.py:477
  22.7 13.8 %collective-permute-start.8 = (bf16[64,3840]{1,0:T(8,128)(2,1)S(1)}, bf16[64,3840]{1,0:T(8,128)(2,1)S(1)}, u32[]{:S(2)}, u32[]{:S(2)}) collective-permute-start(bf16[64,3840]{1,0:T(8,128)(2,1)S(1)} %get-tuple-element.56), channel_id=1, source_target_pairs={{0,16},{8,24},{16,0},{24,8},{1,17},{9,25},{17,1},{25,9},{2,18},{10... | collective-permute-start | bytes 1474568 | tf_op jit(solution)/shard_map/ppermute | solution.py:532
  24.3 30.5 %collective-permute-start.17 = (bf16[64,3840]{1,0:T(8,128)(2,1)S(1)}, bf16[64,3840]{1,0:T(8,128)(2,1)S(1)}, u32[]{:S(2)}, u32[]{:S(2)}) collective-permute-start(bf16[64,3840]{1,0:T(8,128)(2,1)S(1)} %get-tuple-element.63.refs_1_), channel_id=1, source_target_pairs={{0,8},{8,0},{16,24},{24,16},{1,9},{9,1},{17,25},{25,17},{2,10},{10... | collective-permute-start | bytes 1474568 | tf_op jit(solution)/shard_map/ppermute | solution.py:533
  24.3 6.0 %collective-permute-start.6 = (bf16[256,256]{1,0:T(8,128)(2,1)S(1)}, bf16[256,256]{1,0:T(8,128)(2,1)S(1)}, u32[]{:S(2)}, u32[]{:S(2)}) collective-permute-start(bf16[256,256]{1,0:T(8,128)(2,1)S(1)} %slice.26), channel_id=1, source_target_pairs={{0,2},{2,4},{4,6},{6,7},{7,5},{5,3},{3,1},{1,0},{8,10},{10,12},{12... | collective-permute-start | bytes 393224 | tf_op jit(solution)/shard_map/ppermute | solution.py:476
  26.0 5.7 %collective-permute-start.7 = (bf16[256,256]{1,0:T(8,128)(2,1)S(1)}, bf16[256,256]{1,0:T(8,128)(2,1)S(1)}, u32[]{:S(2)}, u32[]{:S(2)}) collective-permute-start(bf16[256,256]{1,0:T(8,128)(2,1)S(1)} %slice.27), channel_id=1, source_target_pairs={{2,0},{4,2},{6,4},{7,6},{5,7},{3,5},{1,3},{0,1},{10,8},{12,10},{14... | collective-permute-start | bytes 393224 | tf_op jit(solution)/shard_map/ppermute | solution.py:477
  34.5 5.0 %collective-permute-start.9 = (bf16[256,256]{1,0:T(8,128)(2,1)S(1)}, bf16[256,256]{1,0:T(8,128)(2,1)S(1)}, u32[]{:S(2)}, u32[]{:S(2)}) collective-permute-start(bf16[256,256]{1,0:T(8,128)(2,1)S(1)} %get-tuple-element.58), channel_id=1, source_target_pairs={{0,2},{2,4},{4,6},{6,7},{7,5},{5,3},{3,1},{1,0},{8,10},{10,12},{12... | collective-permute-start | bytes 393224 | tf_op jit(solution)/shard_map/ppermute | solution.py:476
  36.1 5.1 %collective-permute-start.13 = (bf16[256,256]{1,0:T(8,128)(2,1)S(1)}, bf16[256,256]{1,0:T(8,128)(2,1)S(1)}, u32[]{:S(2)}, u32[]{:S(2)}) collective-permute-start(bf16[256,256]{1,0:T(8,128)(2,1)S(1)} %get-tuple-element.62), channel_id=1, source_target_pairs={{2,0},{4,2},{6,4},{7,6},{5,7},{3,5},{1,3},{0,1},{10,8},{12,10},{14... | collective-permute-start | bytes 393224 | tf_op jit(solution)/shard_map/ppermute | solution.py:477
  39.6 6.5 %collective-permute-start.10 = (bf16[512,256]{1,0:T(8,128)(2,1)S(1)}, bf16[512,256]{1,0:T(8,128)(2,1)S(1)}, u32[]{:S(2)}, u32[]{:S(2)}) collective-permute-start(bf16[512,256]{1,0:T(8,128)(2,1)S(1)} %pad_maximum_fusion), channel_id=1, source_target_pairs={{0,2},{2,4},{4,6},{6,7},{7,5},{5,3},{3,1},{1,0},{8,10},{10,12},{12... | collective-permute-start | bytes 786440 | tf_op jit(solution)/shard_map/ppermute | solution.py:476
  41.2 6.5 %collective-permute-start.14 = (bf16[512,256]{1,0:T(8,128)(2,1)S(1)}, bf16[512,256]{1,0:T(8,128)(2,1)S(1)}, u32[]{:S(2)}, u32[]{:S(2)}) collective-permute-start(bf16[512,256]{1,0:T(8,128)(2,1)S(1)} %pad_maximum_fusion.1), channel_id=1, source_target_pairs={{2,0},{4,2},{6,4},{7,6},{5,7},{3,5},{1,3},{0,1},{10,8},{12,10},{14... | collective-permute-start | bytes 786440 | tf_op jit(solution)/shard_map/ppermute | solution.py:477
  46.1 6.4 %collective-permute-start.11 = (bf16[512,256]{1,0:T(8,128)(2,1)S(1)}, bf16[512,256]{1,0:T(8,128)(2,1)S(1)}, u32[]{:S(2)}, u32[]{:S(2)}) collective-permute-start(bf16[512,256]{1,0:T(8,128)(2,1)S(1)} %add_convert_fusion.4), channel_id=1, source_target_pairs={{0,2},{2,4},{4,6},{6,7},{7,5},{5,3},{3,1},{1,0},{8,10},{10,12},{12... | collective-permute-start | bytes 786440 | tf_op jit(solution)/shard_map/ppermute | solution.py:476
  47.8 6.4 %collective-permute-start.15 = (bf16[512,256]{1,0:T(8,128)(2,1)S(1)}, bf16[512,256]{1,0:T(8,128)(2,1)S(1)}, u32[]{:S(2)}, u32[]{:S(2)}) collective-permute-start(bf16[512,256]{1,0:T(8,128)(2,1)S(1)} %add_convert_fusion.2), channel_id=1, source_target_pairs={{2,0},{4,2},{6,4},{7,6},{5,7},{3,5},{1,3},{0,1},{10,8},{12,10},{14... | collective-permute-start | bytes 786440 | tf_op jit(solution)/shard_map/ppermute | solution.py:477
  49.9 5.0 %collective-permute-start.18 = (bf16[64,3840]{1,0:T(8,128)(2,1)S(1)}, bf16[64,3840]{1,0:T(8,128)(2,1)S(1)}, u32[]{:S(2)}, u32[]{:S(2)}) collective-permute-start(bf16[64,3840]{1,0:T(8,128)(2,1)S(1)} %get-tuple-element.64.refs_3_), channel_id=1, source_target_pairs={{0,8},{8,0},{16,24},{24,16},{1,9},{9,1},{17,25},{25,17},{2,10},{10... | collective-permute-start | bytes 1474568 | tf_op jit(solution)/shard_map/ppermute | solution.py:540
  52.6 6.4 %collective-permute-start.12 = (bf16[512,256]{1,0:T(8,128)(2,1)S(1)}, bf16[512,256]{1,0:T(8,128)(2,1)S(1)}, u32[]{:S(2)}, u32[]{:S(2)}) collective-permute-start(bf16[512,256]{1,0:T(8,128)(2,1)S(1)} %add_convert_fusion.3), channel_id=1, source_target_pairs={{0,2},{2,4},{4,6},{6,7},{7,5},{5,3},{3,1},{1,0},{8,10},{10,12},{12... | collective-permute-start | bytes 786440 | tf_op jit(solution)/shard_map/ppermute | solution.py:476
  54.3 6.4 %collective-permute-start.16 = (bf16[512,256]{1,0:T(8,128)(2,1)S(1)}, bf16[512,256]{1,0:T(8,128)(2,1)S(1)}, u32[]{:S(2)}, u32[]{:S(2)}) collective-permute-start(bf16[512,256]{1,0:T(8,128)(2,1)S(1)} %add_convert_fusion.1), channel_id=1, source_target_pairs={{2,0},{4,2},{6,4},{7,6},{5,7},{3,5},{1,3},{0,1},{10,8},{12,10},{14... | collective-permute-start | bytes 786440 | tf_op jit(solution)/shard_map/ppermute | solution.py:477

commit v5 on v4

--- a/solution.py
+++ b/solution.py
@@ -191,7 +191,7 @@
     return (((lhs,), (rhs,)), ((), ()))
 
 
-def call(body, operands, out_shape, micros, name, in_specs=None, out_specs=None, scratch=(), limit=24, aliases=None):
+def call(body, operands, out_shape, micros, name, in_specs=None, out_specs=None, scratch=(), limit=36, aliases=None):
     count = len(out_shape)
     return pl.pallas_call(
         body,
@@ -326,7 +326,7 @@
     old = () if total is None else tuple(total)
     base = 1 + count + len(weights)
     return call(
-        lambda *refs: grow_kernel(slots, first, total is None, min(rows, 256), *refs),
+        lambda *refs: grow_kernel(slots, first, total is None, rows, *refs),
         (at, *pieces, *weights, *old),
         (
             jax.ShapeDtypeStruct((rows, cols), jnp.float32),

time: 61.7 us -> 61.6 us (level)
  transfers between devices with their start and end apart: 19 -> 19, of which waited for: 9 -> 10; matrix products, arithmetic and copies ran while one was open for 2% -> 2% of each run, Pallas kernels for 38% -> 37%
where the time goes in v5:
time: 61.6 us; the launch traced here: 61.5 us
  Pallas kernels  22.6 us (37%)
  starting transfers between devices  19.4 us (31%)
  waiting for transfers between devices  16.8 us (27%)
  other arithmetic  1.89 us (3%)
  between operations  0.79 us (1%)
    pallas_call x11, Pallas kernels, call(): pl.pallas_call(body, out_shape=out_shape, in_specs=in_specs or [SMEM] + [...  22.6 us
    ppermute x8, starting transfers between devices, per_device(): on = lambda a: lax.ppermute(a, 'wsh', onward)  14.5 us
    ppermute x8, waiting for transfers between devices, per_device(): on = lambda a: lax.ppermute(a, 'wsh', onward)  13.7 us
    ppermute x8, starting transfers between devices, per_device(): back_to = lambda a: lax.ppermute(a, 'wsh', back)  3.19 us
    ppermute x8, waiting for transfers between devices, per_device(): back_to = lambda a: lax.ppermute(a, 'wsh', back)  3.1 us
    ppermute x1, starting transfers between devices, per_device(): far_in = lax.ppermute(far, 'grp', pair)  1.55 us
  transfers between devices with their start and end apart: 19, of which 10 were waited for; matrix products, arithmetic and copies ran while one was open for 2% of the time, Pallas kernels for 37%

profile of v5, /device:TPU:0, one launch (start us, length us, event | category | flops | bytes accessed | tf_op | source)
XLA Modules:
  0.0 61.5 jit_solution(7219705949787937358)
XLA Ops:
  0.6 3.1 %collective-permute-start = (bf16[512,256]{1,0:T(8,128)(2,1)}, bf16[512,256]{1,0:T(8,128)(2,1)S(1)}, u32[]{:S(2)}, u32[]{:S(2)}) collective-permute-start(bf16[512,256]{1,0:T(8,128)(2,1)} %refs_1_.4), channel_id=1, source_target_pairs={{0,2},{2,4},{4,6},{6,7},{7,5},{5,3},{3,1},{1,0},{8,10},{10,12},{12... | collective-permute-start | bytes 786440 | tf_op jit(solution)/shard_map/ppermute | solution.py:476
  3.7 0.0 collective-permute-start.3
  3.7 0.7 %multiply_bitcast_fusion = f32[64,1]{0,1:T(1,128)S(1)} fusion(s32[64]{0:T(128)} %param.21), kind=kLoop, calls=%fused_computation.17 | loop fusion | flops 256 | bytes 512 | tf_op jit(solution)/shard_map/broadcast_in_dim | solution.py:531
  4.4 0.1 copy.21.refs_1_
  4.5 0.1 pad_add_fusion.refs_0_
  4.6 3.4 %stage_one.1 = (bf16[128,2048]{1,0:T(8,128)(2,1)S(1)}, bf16[2048,896]{1,0:T(8,128)(2,1)S(1)}, bf16[2048,896]{1,0:T(8,128)(2,1)S(1)}) custom-call(bf16[64,2048]{1,0:T(8,128)(2,1)} %refs_0_.2, bf16[64,2048]{1,0:T(8,128)(2,1)} %refs_1_.3, bf16[2048,896]{1,0:T(8,128)(2,1)} %refs_2_.2, bf16[2048,896]{1,0:T(8,128)(2,1)} %refs_3_.2), custom_call_target="tpu_custom_call" | custom-call | flops 4000000000 | bytes 1000000 | tf_op jit(solution)/shard_map/stage_one/pallas_call | solution.py:196
  8.0 2.2 %collective-permute-done.refs_2_ = bf16[512,256]{1,0:T(8,128)(2,1)S(1)} collective-permute-done((bf16[512,256]{1,0:T(8,128)(2,1)}, bf16[512,256]{1,0:T(8,128)(2,1)S(1)}, u32[]{:S(2)}, u32[]{:S(2)}) %collective-permute-start) | collective-permute-done | bytes 262176 | tf_op jit(solution)/shard_map/ppermute | solution.py:476
  10.1 1.8 %collective-permute-start.1 = (bf16[512,256]{1,0:T(8,128)(2,1)S(1)}, bf16[512,256]{1,0:T(8,128)(2,1)S(1)}, u32[]{:S(2)}, u32[]{:S(2)}) collective-permute-start(bf16[512,256]{1,0:T(8,128)(2,1)S(1)} %collective-permute-done.refs_2_), channel_id=1, source_target_pairs={{0,2},{2,4},{4,6},{6,7},{7,5},{5,3},{3,1},{1,0},{8,10},{10,12},{12... | collective-permute-start | bytes 786440 | tf_op jit(solution)/shard_map/ppermute | solution.py:476
  12.0 0.2 collective-permute-start.4
  12.2 2.6 %grow.3 = (f32[512,896]{1,0:T(8,128)S(1)}, f32[512,896]{1,0:T(8,128)S(1)}, f32[512,128]{1,0:T(8,128)S(1)}) custom-call(s32[11]{0:T(128)S(1)} %pad_add_fusion.refs_0_, bf16[512,256]{1,0:T(8,128)(2,1)S(1)} %copy-done, bf16[512,256]{1,0:T(8,128)(2,1)S(1)} %collective-permute-done.refs_2_, bf16[512,256]{1,0:T(8,128)(2,1)S(1)} %collective-permute-done.3.refs_3_, ...), custom_call_target="tpu_custom_call" | custom-call | flops 5000000000 | bytes 1000000 | tf_op jit(solution)/shard_map/grow/pallas_call | solution.py:196
  14.7 2.5 %stage_two.1 = (f32[128,896]{1,0:T(8,128)S(1)}, bf16[64,896]{1,0:T(8,128)(2,1)S(1)}, f32[64,2048]{1,0:T(8,128)S(1)}, bf16[896,2048]{1,0:T(8,128)(2,1)S(1)}) custom-call(f32[64,896]{1,0:T(8,128)} %refs_0_.3, f32[64,896]{1,0:T(8,128)} %refs_1_.5, bf16[64,896]{1,0:T(8,128)(2,1)} %refs_2_.3, f32[64,2048]{1,0:T(8,128)} %refs_3_.3, bf16[896,2048]{1,0:T(8,128)(2,1)} %refs_4_.1, ...), custom_call_target="tpu_custom_call" | custom-call | flops 2000000000 | bytes 1000000 | tf_op jit(solution)/shard_map/stage_two/pallas_call | solution.py:196
  17.3 0.3 collective-permute-done.1.refs_1_
  17.6 1.5 %collective-permute-start.2 = (bf16[512,256]{1,0:T(8,128)(2,1)S(1)}, bf16[512,256]{1,0:T(8,128)(2,1)S(1)}, u32[]{:S(2)}, u32[]{:S(2)}) collective-permute-start(bf16[512,256]{1,0:T(8,128)(2,1)S(1)} %collective-permute-done.1.refs_1_), channel_id=1, source_target_pairs={{0,2},{2,4},{4,6},{6,7},{7,5},{5,3},{3,1},{1,0},{8,10},{10,12},{12... | collective-permute-start | bytes 786440 | tf_op jit(solution)/shard_map/ppermute | solution.py:476
  19.2 0.5 collective-permute-start.5
  19.7 2.1 %grow.4 = (f32[512,896]{1,0:T(8,128)S(1)}, f32[512,896]{1,0:T(8,128)S(1)}, f32[512,128]{1,0:T(8,128)S(1)}) custom-call(s32[11]{0:T(128)S(1)} %pad_add_fusion.refs_0_, bf16[512,256]{1,0:T(8,128)(2,1)S(1)} %collective-permute-done.1.refs_1_, ...), custom_call_target="tpu_custom_call", output_to_operand_aliasing={{0}: (6, {}), {1}: (7, {}), {2}: (8, {})} | custom-call | flops 5000000000 | bytes 1000000 | tf_op jit(solution)/shard_map/grow/pallas_call | solution.py:196
  21.8 0.6 %messages.1 = (bf16[64,3840]{1,0:T(8,128)(2,1)S(1)}, bf16[64,3840]{1,0:T(8,128)(2,1)S(1)}) custom-call(s32[11]{0:T(128)S(1)} %pad_add_fusion.refs_0_, f32[64,1]{1,0:T(8,128)S(1)} %copy.21.refs_1_, f32[128,896]{1,0:T(8,128)S(1)} %get-tuple-element.47.refs_9_.refs_2_, bf16[128,2048]{1,0:T(8,128)(2,1)S(1)} %get-tuple-element.37.refs_6_.refs_5_.refs_8_.refs_3_, ...), custom_call_target="tpu_custom_call" | custom-call | flops 2000000000 | bytes 1000000 | tf_op jit(solution)/shard_map/messages/pallas_call | solution.py:196
  22.5 1.5 %collective-permute-start.8 = (bf16[64,3840]{1,0:T(8,128)(2,1)S(1)}, bf16[64,3840]{1,0:T(8,128)(2,1)S(1)}, u32[]{:S(2)}, u32[]{:S(2)}) collective-permute-start(bf16[64,3840]{1,0:T(8,128)(2,1)S(1)} %get-tuple-element.56), channel_id=1, source_target_pairs={{0,16},{8,24},{16,0},{24,8},{1,17},{9,25},{17,1},{25,9},{2,18},{10... | collective-permute-start | bytes 1474568 | tf_op jit(solution)/shard_map/ppermute | solution.py:532
  24.0 0.3 collective-permute-done.2.refs_1_
  24.3 1.6 %collective-permute-start.6 = (bf16[256,256]{1,0:T(8,128)(2,1)S(1)}, bf16[256,256]{1,0:T(8,128)(2,1)S(1)}, u32[]{:S(2)}, u32[]{:S(2)}) collective-permute-start(bf16[256,256]{1,0:T(8,128)(2,1)S(1)} %slice.26), channel_id=1, source_target_pairs={{0,2},{2,4},{4,6},{6,7},{7,5},{5,3},{3,1},{1,0},{8,10},{10,12},{12... | collective-permute-start | bytes 393224 | tf_op jit(solution)/shard_map/ppermute | solution.py:476
  25.9 0.6 collective-permute-start.7
  26.4 2.1 %grow.5 = (f32[512,896]{1,0:T(8,128)S(1)}, f32[512,896]{1,0:T(8,128)S(1)}, f32[512,128]{1,0:T(8,128)S(1)}) custom-call(s32[11]{0:T(128)S(1)} %pad_add_fusion.refs_0_, bf16[512,256]{1,0:T(8,128)(2,1)S(1)} %collective-permute-done.2.refs_1_, ...), custom_call_target="tpu_custom_call", output_to_operand_aliasing={{0}: (6, {}), {1}: (7, {}), {2}: (8, {})} | custom-call | flops 5000000000 | bytes 1000000 | tf_op jit(solution)/shard_map/grow/pallas_call | solution.py:196
  28.6 1.4 %collective-permute-done.6.refs_4_ = bf16[256,256]{1,0:T(8,128)(2,1)S(1)} collective-permute-done((bf16[256,256]{1,0:T(8,128)(2,1)S(1)}, bf16[256,256]{1,0:T(8,128)(2,1)S(1)}, u32[]{:S(2)}, u32[]{:S(2)}) %collective-permute-start.6) | collective-permute-done | bytes 131104 | tf_op jit(solution)/shard_map/ppermute | solution.py:476
  30.0 1.4 %collective-permute-done.7.refs_5_ = bf16[256,256]{1,0:T(8,128)(2,1)S(1)} collective-permute-done((bf16[256,256]{1,0:T(8,128)(2,1)S(1)}, bf16[256,256]{1,0:T(8,128)(2,1)S(1)}, u32[]{:S(2)}, u32[]{:S(2)}) %collective-permute-start.7) | collective-permute-done | bytes 131104 | tf_op jit(solution)/shard_map/ppermute | solution.py:477
  31.3 2.8 %finish.1 = (bf16[512,896]{1,0:T(8,128)(2,1)S(1)}, f32[512,128]{1,0:T(8,128)S(1)}, bf16[256,256]{1,0:T(8,128)(2,1)S(1)}, bf16[256,256]{1,0:T(8,128)(2,1)S(1)}) custom-call(s32[11]{0:T(128)S(1)} %pad_add_fusion.refs_0_, f32[512,896]{1,0:T(8,128)S(1)} %get-tuple-element.44.refs_1_, f32[512,896]{1,0:T(8,128)S(1)} %get-tuple-element.45.refs_2_, ...), custom_call_target="tpu_custom_call" | custom-call | flops 4000000000 | bytes 1000000 | tf_op jit(solution)/shard_map/finish/pallas_call | solution.py:196
  34.2 1.6 %collective-permute-start.9 = (bf16[256,256]{1,0:T(8,128)(2,1)S(1)}, bf16[256,256]{1,0:T(8,128)(2,1)S(1)}, u32[]{:S(2)}, u32[]{:S(2)}) collective-permute-start(bf16[256,256]{1,0:T(8,128)(2,1)S(1)} %get-tuple-element.58), channel_id=1, source_target_pairs={{0,2},{2,4},{4,6},{6,7},{7,5},{5,3},{3,1},{1,0},{8,10},{10,12},{12... | collective-permute-start | bytes 393224 | tf_op jit(solution)/shard_map/ppermute | solution.py:476
  35.8 0.4 collective-permute-start.13
  36.3 1.3 %shares.5 = (f32[512,256]{1,0:T(8,128)S(1)}, f32[512,256]{1,0:T(8,128)S(1)}, bf16[64,3840]{1,0:T(8,128)(2,1)S(1)}) custom-call(s32[11]{0:T(128)S(1)} %pad_add_fusion.refs_0_, bf16[512,896]{1,0:T(8,128)(2,1)S(1)} %get-tuple-element.51.refs_1_, f32[512,128]{1,0:T(8,128)S(1)} %get-tuple-element.52.refs_2_, ...), custom_call_target="tpu_custom_call", output_to_operand_aliasing={{2}: (5, {})} | custom-call | flops 4000000000 | bytes 1000000 | tf_op jit(solution)/shard_map/shares/pallas_call | solution.py:196
  37.6 1.6 %collective-permute-done.9 = bf16[256,256]{1,0:T(8,128)(2,1)S(1)} collective-permute-done((bf16[256,256]{1,0:T(8,128)(2,1)S(1)}, bf16[256,256]{1,0:T(8,128)(2,1)S(1)}, u32[]{:S(2)}, u32[]{:S(2)}) %collective-permute-start.9) | collective-permute-done | bytes 131104 | tf_op jit(solution)/shard_map/ppermute | solution.py:476
  39.2 1.6 %collective-permute-start.10 = (bf16[512,256]{1,0:T(8,128)(2,1)S(1)}, bf16[512,256]{1,0:T(8,128)(2,1)S(1)}, u32[]{:S(2)}, u32[]{:S(2)}) collective-permute-start(bf16[512,256]{1,0:T(8,128)(2,1)S(1)} %pad_maximum_fusion), channel_id=1, source_target_pairs={{0,2},{2,4},{4,6},{6,7},{7,5},{5,3},{3,1},{1,0},{8,10},{10,12},{12... | collective-permute-start | bytes 786440 | tf_op jit(solution)/shard_map/ppermute | solution.py:476
  40.9 0.5 collective-permute-start.14
  41.4 1.3 %shares.4 = (f32[512,256]{1,0:T(8,128)S(1)}, f32[512,256]{1,0:T(8,128)S(1)}) custom-call(s32[11]{0:T(128)S(1)} %pad_add_fusion.refs_0_, bf16[512,896]{1,0:T(8,128)(2,1)S(1)} %get-tuple-element.51.refs_1_, f32[512,128]{1,0:T(8,128)S(1)} %get-tuple-element.52.refs_2_, bf16[896,2048]{1,0:T(8,128)(2,1)S(1)} %get-tuple-element.49.refs_11_.refs_3_, ...), custom_call_target="tpu_custom_call" | custom-call | flops 4000000000 | bytes 1000000 | tf_op jit(solution)/shard_map/shares/pallas_call | solution.py:196
  42.7 3.3 %collective-permute-done.10 = bf16[512,256]{1,0:T(8,128)(2,1)S(1)} collective-permute-done((bf16[512,256]{1,0:T(8,128)(2,1)S(1)}, bf16[512,256]{1,0:T(8,128)(2,1)S(1)}, u32[]{:S(2)}, u32[]{:S(2)}) %collective-permute-start.10) | collective-permute-done | bytes 262176 | tf_op jit(solution)/shard_map/ppermute | solution.py:476
  46.0 0.1 add_convert_fusion.4
  46.1 1.6 %collective-permute-start.11 = (bf16[512,256]{1,0:T(8,128)(2,1)S(1)}, bf16[512,256]{1,0:T(8,128)(2,1)S(1)}, u32[]{:S(2)}, u32[]{:S(2)}) collective-permute-start(bf16[512,256]{1,0:T(8,128)(2,1)S(1)} %add_convert_fusion.4), channel_id=1, source_target_pairs={{0,2},{2,4},{4,6},{6,7},{7,5},{5,3},{3,1},{1,0},{8,10},{10,12},{12... | collective-permute-start | bytes 786440 | tf_op jit(solution)/shard_map/ppermute | solution.py:476
  47.7 0.1 add_convert_fusion.2
  47.8 0.5 collective-permute-start.15
  48.3 1.5 %shares.3 = (f32[512,256]{1,0:T(8,128)S(1)}, f32[512,256]{1,0:T(8,128)S(1)}, f32[512,256]{1,0:T(8,128)S(1)}) custom-call(s32[11]{0:T(128)S(1)} %pad_add_fusion.refs_0_, bf16[512,896]{1,0:T(8,128)(2,1)S(1)} %get-tuple-element.51.refs_1_, f32[512,128]{1,0:T(8,128)S(1)} %get-tuple-element.52.refs_2_, bf16[896,2048]{1,0:T(8,128)(2,1)S(1)} %get-tuple-element.49.refs_11_.refs_3_, ...), custom_call_target="tpu_custom_call" | custom-call | flops 4000000000 | bytes 1000000 | tf_op jit(solution)/shard_map/shares/pallas_call | solution.py:196
  49.8 0.1 collective-permute-start.18
  49.9 2.6 %collective-permute-done.11 = bf16[512,256]{1,0:T(8,128)(2,1)S(1)} collective-permute-done((bf16[512,256]{1,0:T(8,128)(2,1)S(1)}, bf16[512,256]{1,0:T(8,128)(2,1)S(1)}, u32[]{:S(2)}, u32[]{:S(2)}) %collective-permute-start.11) | collective-permute-done | bytes 262176 | tf_op jit(solution)/shard_map/ppermute | solution.py:476
  52.5 0.1 add_convert_fusion.3
  52.6 1.6 %collective-permute-start.12 = (bf16[512,256]{1,0:T(8,128)(2,1)S(1)}, bf16[512,256]{1,0:T(8,128)(2,1)S(1)}, u32[]{:S(2)}, u32[]{:S(2)}) collective-permute-start(bf16[512,256]{1,0:T(8,128)(2,1)S(1)} %add_convert_fusion.3), channel_id=1, source_target_pairs={{0,2},{2,4},{4,6},{6,7},{7,5},{5,3},{3,1},{1,0},{8,10},{10,12},{12... | collective-permute-start | bytes 786440 | tf_op jit(solution)/shard_map/ppermute | solution.py:476
  54.2 0.0 collective-permute-done.15
  54.2 0.1 add_convert_fusion.1
  54.3 0.5 collective-permute-start.16
  54.8 2.2 %outers.1 = (bf16[512,896]{1,0:T(8,128)(2,1)}, bf16[512,896]{1,0:T(8,128)(2,1)}) custom-call(s32[11]{0:T(128)S(1)} %pad_add_fusion.refs_0_, bf16[64,3840]{1,0:T(8,128)(2,1)S(1)} %get-tuple-element.63.refs_1_, bf16[64,3840]{1,0:T(8,128)(2,1)S(1)} %collective-permute-done.17.refs_2_, bf16[64,3840]{1,0:T(8,128)(2,1)S(1)} %get-tuple-element.64.refs_3_, ...), custom_call_target="tpu_custom_call" | custom-call | flops 5000000000 | bytes 1000000 | tf_op jit(solution)/shard_map/outers/pallas_call | solution.py:196
  57.0 2.0 %collective-permute-done.12 = bf16[512,256]{1,0:T(8,128)(2,1)S(1)} collective-permute-done((bf16[512,256]{1,0:T(8,128)(2,1)S(1)}, bf16[512,256]{1,0:T(8,128)(2,1)S(1)}, u32[]{:S(2)}, u32[]{:S(2)}) %collective-permute-start.12) | collective-permute-done | bytes 262176 | tf_op jit(solution)/shard_map/ppermute | solution.py:476
  59.0 1.7 %collective-permute-done.16 = bf16[512,256]{1,0:T(8,128)(2,1)S(1)} collective-permute-done((bf16[512,256]{1,0:T(8,128)(2,1)S(1)}, bf16[512,256]{1,0:T(8,128)(2,1)S(1)}, u32[]{:S(2)}, u32[]{:S(2)}) %collective-permute-start.16) | collective-permute-done | bytes 262176 | tf_op jit(solution)/shard_map/ppermute | solution.py:477
  60.7 0.8 %add_convert_fusion = bf16[512,256]{1,0:T(8,128)(2,1)} fusion(bf16[512,256]{1,0:T(8,128)(2,1)S(1)} %collective-permute-done.16, f32[512,256]{1,0:T(8,128)S(1)} %get-tuple-element.53, bf16[512,256]{1,0:T(8,128)(2,1)S(1)} %collective-permute-done.12), kind=kLoop, calls=%fused_computation | loop fusion | flops 655360 | bytes 1310720 | tf_op jit(solution)/shard_map/convert_element_type | solution.py:520
  (20 shorter events, 0.2 us)
Async XLA Ops:
  0.6 9.5 %collective-permute-start = (bf16[512,256]{1,0:T(8,128)(2,1)}, bf16[512,256]{1,0:T(8,128)(2,1)S(1)}, u32[]{:S(2)}, u32[]{:S(2)}) collective-permute-start(bf16[512,256]{1,0:T(8,128)(2,1)} %refs_1_.4), channel_id=1, source_target_pairs={{0,2},{2,4},{4,6},{6,7},{7,5},{5,3},{3,1},{1,0},{8,10},{10,12},{12... | collective-permute-start | bytes 786440 | tf_op jit(solution)/shard_map/ppermute | solution.py:476
  3.7 8.3 %collective-permute-start.3 = (bf16[512,256]{1,0:T(8,128)(2,1)}, bf16[512,256]{1,0:T(8,128)(2,1)S(1)}, u32[]{:S(2)}, u32[]{:S(2)}) collective-permute-start(bf16[512,256]{1,0:T(8,128)(2,1)} %refs_1_.4), channel_id=1, source_target_pairs={{2,0},{4,2},{6,4},{7,6},{5,7},{3,5},{1,3},{0,1},{10,8},{12,10},{14... | collective-permute-start | bytes 786440 | tf_op jit(solution)/shard_map/ppermute | solution.py:477
  4.6 7.6 %copy-start = (bf16[512,256]{1,0:T(8,128)(2,1)S(1)}, bf16[512,256]{1,0:T(8,128)(2,1)}, u32[]{:S(2)}) copy-start(bf16[512,256]{1,0:T(8,128)(2,1)} %refs_1_.4) | copy-start | bytes 786436
  10.1 7.5 %collective-permute-start.1 = (bf16[512,256]{1,0:T(8,128)(2,1)S(1)}, bf16[512,256]{1,0:T(8,128)(2,1)S(1)}, u32[]{:S(2)}, u32[]{:S(2)}) collective-permute-start(bf16[512,256]{1,0:T(8,128)(2,1)S(1)} %collective-permute-done.refs_2_), channel_id=1, source_target_pairs={{0,2},{2,4},{4,6},{6,7},{7,5},{5,3},{3,1},{1,0},{8,10},{10,12},{12... | collective-permute-start | bytes 786440 | tf_op jit(solution)/shard_map/ppermute | solution.py:476
  12.0 7.2 %collective-permute-start.4 = (bf16[512,256]{1,0:T(8,128)(2,1)S(1)}, bf16[512,256]{1,0:T(8,128)(2,1)S(1)}, u32[]{:S(2)}, u32[]{:S(2)}) collective-permute-start(bf16[512,256]{1,0:T(8,128)(2,1)S(1)} %collective-permute-done.3.refs_3_), channel_id=1, source_target_pairs={{2,0},{4,2},{6,4},{7,6},{5,7},{3,5},{1,3},{0,1},{10,8},{12,10},{14... | collective-permute-start | bytes 786440 | tf_op jit(solution)/shard_map/ppermute | solution.py:477
  17.6 6.7 %collective-permute-start.2 = (bf16[512,256]{1,0:T(8,128)(2,1)S(1)}, bf16[512,256]{1,0:T(8,128)(2,1)S(1)}, u32[]{:S(2)}, u32[]{:S(2)}) collective-permute-start(bf16[512,256]{1,0:T(8,128)(2,1)S(1)} %collective-permute-done.1.refs_1_), channel_id=1, source_target_pairs={{0,2},{2,4},{4,6},{6,7},{7,5},{5,3},{3,1},{1,0},{8,10},{10,12},{12... | collective-permute-start | bytes 786440 | tf_op jit(solution)/shard_map/ppermute | solution.py:476
  19.2 6.7 %collective-permute-start.5 = (bf16[512,256]{1,0:T(8,128)(2,1)S(1)}, bf16[512,256]{1,0:T(8,128)(2,1)S(1)}, u32[]{:S(2)}, u32[]{:S(2)}) collective-permute-start(bf16[512,256]{1,0:T(8,128)(2,1)S(1)} %collective-permute-done.4.refs_2_), channel_id=1, source_target_pairs={{2,0},{4,2},{6,4},{7,6},{5,7},{3,5},{1,3},{0,1},{10,8},{12,10},{14... | collective-permute-start | bytes 786440 | tf_op jit(solution)/shard_map/ppermute | solution.py:477
  22.5 13.8 %collective-permute-start.8 = (bf16[64,3840]{1,0:T(8,128)(2,1)S(1)}, bf16[64,3840]{1,0:T(8,128)(2,1)S(1)}, u32[]{:S(2)}, u32[]{:S(2)}) collective-permute-start(bf16[64,3840]{1,0:T(8,128)(2,1)S(1)} %get-tuple-element.56), channel_id=1, source_target_pairs={{0,16},{8,24},{16,0},{24,8},{1,17},{9,25},{17,1},{25,9},{2,18},{10... | collective-permute-start | bytes 1474568 | tf_op jit(solution)/shard_map/ppermute | solution.py:532
  24.0 30.8 %collective-permute-start.17 = (bf16[64,3840]{1,0:T(8,128)(2,1)S(1)}, bf16[64,3840]{1,0:T(8,128)(2,1)S(1)}, u32[]{:S(2)}, u32[]{:S(2)}) collective-permute-start(bf16[64,3840]{1,0:T(8,128)(2,1)S(1)} %get-tuple-element.63.refs_1_), channel_id=1, source_target_pairs={{0,8},{8,0},{16,24},{24,16},{1,9},{9,1},{17,25},{25,17},{2,10},{10... | collective-permute-start | bytes 1474568 | tf_op jit(solution)/shard_map/ppermute | solution.py:533
  24.3 5.7 %collective-permute-start.6 = (bf16[256,256]{1,0:T(8,128)(2,1)S(1)}, bf16[256,256]{1,0:T(8,128)(2,1)S(1)}, u32[]{:S(2)}, u32[]{:S(2)}) collective-permute-start(bf16[256,256]{1,0:T(8,128)(2,1)S(1)} %slice.26), channel_id=1, source_target_pairs={{0,2},{2,4},{4,6},{6,7},{7,5},{5,3},{3,1},{1,0},{8,10},{10,12},{12... | collective-permute-start | bytes 393224 | tf_op jit(solution)/shard_map/ppermute | solution.py:476
  25.9 5.5 %collective-permute-start.7 = (bf16[256,256]{1,0:T(8,128)(2,1)S(1)}, bf16[256,256]{1,0:T(8,128)(2,1)S(1)}, u32[]{:S(2)}, u32[]{:S(2)}) collective-permute-start(bf16[256,256]{1,0:T(8,128)(2,1)S(1)} %slice.27), channel_id=1, source_target_pairs={{2,0},{4,2},{6,4},{7,6},{5,7},{3,5},{1,3},{0,1},{10,8},{12,10},{14... | collective-permute-start | bytes 393224 | tf_op jit(solution)/shard_map/ppermute | solution.py:477
  34.2 5.0 %collective-permute-start.9 = (bf16[256,256]{1,0:T(8,128)(2,1)S(1)}, bf16[256,256]{1,0:T(8,128)(2,1)S(1)}, u32[]{:S(2)}, u32[]{:S(2)}) collective-permute-start(bf16[256,256]{1,0:T(8,128)(2,1)S(1)} %get-tuple-element.58), channel_id=1, source_target_pairs={{0,2},{2,4},{4,6},{6,7},{7,5},{5,3},{3,1},{1,0},{8,10},{10,12},{12... | collective-permute-start | bytes 393224 | tf_op jit(solution)/shard_map/ppermute | solution.py:476
  35.8 5.1 %collective-permute-start.13 = (bf16[256,256]{1,0:T(8,128)(2,1)S(1)}, bf16[256,256]{1,0:T(8,128)(2,1)S(1)}, u32[]{:S(2)}, u32[]{:S(2)}) collective-permute-start(bf16[256,256]{1,0:T(8,128)(2,1)S(1)} %get-tuple-element.62), channel_id=1, source_target_pairs={{2,0},{4,2},{6,4},{7,6},{5,7},{3,5},{1,3},{0,1},{10,8},{12,10},{14... | collective-permute-start | bytes 393224 | tf_op jit(solution)/shard_map/ppermute | solution.py:477
  39.2 6.8 %collective-permute-start.10 = (bf16[512,256]{1,0:T(8,128)(2,1)S(1)}, bf16[512,256]{1,0:T(8,128)(2,1)S(1)}, u32[]{:S(2)}, u32[]{:S(2)}) collective-permute-start(bf16[512,256]{1,0:T(8,128)(2,1)S(1)} %pad_maximum_fusion), channel_id=1, source_target_pairs={{0,2},{2,4},{4,6},{6,7},{7,5},{5,3},{3,1},{1,0},{8,10},{10,12},{12... | collective-permute-start | bytes 786440 | tf_op jit(solution)/shard_map/ppermute | solution.py:476
  40.9 6.8 %collective-permute-start.14 = (bf16[512,256]{1,0:T(8,128)(2,1)S(1)}, bf16[512,256]{1,0:T(8,128)(2,1)S(1)}, u32[]{:S(2)}, u32[]{:S(2)}) collective-permute-start(bf16[512,256]{1,0:T(8,128)(2,1)S(1)} %pad_maximum_fusion.1), channel_id=1, source_target_pairs={{2,0},{4,2},{6,4},{7,6},{5,7},{3,5},{1,3},{0,1},{10,8},{12,10},{14... | collective-permute-start | bytes 786440 | tf_op jit(solution)/shard_map/ppermute | solution.py:477
  46.1 6.4 %collective-permute-start.11 = (bf16[512,256]{1,0:T(8,128)(2,1)S(1)}, bf16[512,256]{1,0:T(8,128)(2,1)S(1)}, u32[]{:S(2)}, u32[]{:S(2)}) collective-permute-start(bf16[512,256]{1,0:T(8,128)(2,1)S(1)} %add_convert_fusion.4), channel_id=1, source_target_pairs={{0,2},{2,4},{4,6},{6,7},{7,5},{5,3},{3,1},{1,0},{8,10},{10,12},{12... | collective-permute-start | bytes 786440 | tf_op jit(solution)/shard_map/ppermute | solution.py:476
  47.8 6.4 %collective-permute-start.15 = (bf16[512,256]{1,0:T(8,128)(2,1)S(1)}, bf16[512,256]{1,0:T(8,128)(2,1)S(1)}, u32[]{:S(2)}, u32[]{:S(2)}) collective-permute-start(bf16[512,256]{1,0:T(8,128)(2,1)S(1)} %add_convert_fusion.2), channel_id=1, source_target_pairs={{2,0},{4,2},{6,4},{7,6},{5,7},{3,5},{1,3},{0,1},{10,8},{12,10},{14... | collective-permute-start | bytes 786440 | tf_op jit(solution)/shard_map/ppermute | solution.py:477
  49.8 5.0 %collective-permute-start.18 = (bf16[64,3840]{1,0:T(8,128)(2,1)S(1)}, bf16[64,3840]{1,0:T(8,128)(2,1)S(1)}, u32[]{:S(2)}, u32[]{:S(2)}) collective-permute-start(bf16[64,3840]{1,0:T(8,128)(2,1)S(1)} %get-tuple-element.64.refs_3_), channel_id=1, source_target_pairs={{0,8},{8,0},{16,24},{24,16},{1,9},{9,1},{17,25},{25,17},{2,10},{10... | collective-permute-start | bytes 1474568 | tf_op jit(solution)/shard_map/ppermute | solution.py:540
  52.6 6.4 %collective-permute-start.12 = (bf16[512,256]{1,0:T(8,128)(2,1)S(1)}, bf16[512,256]{1,0:T(8,128)(2,1)S(1)}, u32[]{:S(2)}, u32[]{:S(2)}) collective-permute-start(bf16[512,256]{1,0:T(8,128)(2,1)S(1)} %add_convert_fusion.3), channel_id=1, source_target_pairs={{0,2},{2,4},{4,6},{6,7},{7,5},{5,3},{3,1},{1,0},{8,10},{10,12},{12... | collective-permute-start | bytes 786440 | tf_op jit(solution)/shard_map/ppermute | solution.py:476
  54.3 6.4 %collective-permute-start.16 = (bf16[512,256]{1,0:T(8,128)(2,1)S(1)}, bf16[512,256]{1,0:T(8,128)(2,1)S(1)}, u32[]{:S(2)}, u32[]{:S(2)}) collective-permute-start(bf16[512,256]{1,0:T(8,128)(2,1)S(1)} %add_convert_fusion.1), channel_id=1, source_target_pairs={{2,0},{4,2},{6,4},{7,6},{5,7},{3,5},{1,3},{0,1},{10,8},{12,10},{14... | collective-permute-start | bytes 786440 | tf_op jit(solution)/shard_map/ppermute | solution.py:477

commit v6 on v5

--- a/solution.py
+++ b/solution.py
@@ -346,7 +346,7 @@
 
 
 def finish_kernel(
-    slot, first, per_member, tall, at, gate_sum, up_sum, scores, top, bottom, gate_w, up_w, lefts,
+    slot, first, per_member, wide, at, gate_sum, up_sum, scores, top, bottom, gate_w, up_w, lefts,
     rights, down_l, down_w, down_r, hidden_out, score_out, on_out, back_out,
 ):
     rows = gate_sum.shape[0]
@@ -354,44 +354,42 @@
     half = rows // 2
     members = rows // per_member
     own = slice(first, first + members)
-    gate_rhs, up_rhs = row_block(gate_w, at[slot], span), row_block(up_w, at[slot], span)
+    cols = gate_sum.shape[1]
+    weight_rows = pl.ds(pl.multiple_of(at[slot] * span, span), span)
     group = lefts.shape[0] // 2
     own_up = slice(group + first, group + first + members)
     left = jnp.concatenate([lane_block(lefts, at[slot], span, own), lane_block(lefts, at[slot], span, own_up)], axis=0)
     down_rhs = lane_block(down_w, at[slot], span)
     down_left = down_l[own, :]
-    for start in range(0, rows, tall):
-        part = slice(start, start + tall)
-        source, shift, out = (top, 0, on_out) if start < half else (bottom, half, back_out)
-        inner = slice(start - shift, start - shift + tall)
-        mine = slice(first + start // per_member, first + (start + tall) // per_member)
-        mine_up = slice(group + mine.start, group + mine.stop)
-        piece = source[inner, :]
-        score = scores[part, :] + lax.dot_general(piece, left, dims(1, 1), preferred_element_type=jnp.float32)
-        member = (lax.broadcasted_iota(jnp.int32, (tall, 2 * members), 0) + start) // per_member
-        column = lax.broadcasted_iota(jnp.int32, (tall, 2 * members), 1)
-        gate_score = jnp.sum(jnp.where(column == member, score, 0.0), axis=1, keepdims=True)
-        up_score = jnp.sum(jnp.where(column == member + members, score, 0.0), axis=1, keepdims=True)
-        gate = gate_sum[part, :] + jnp.dot(piece, gate_rhs, preferred_element_type=jnp.float32)
-        up = up_sum[part, :] + jnp.dot(piece, up_rhs, preferred_element_type=jnp.float32)
-        gate = gate + spread_rows(noise_scale * gate_score, rights[mine, :], per_member)
-        up = up + spread_rows(noise_scale * up_score, rights[mine_up, :], per_member)
-        hidden = (silu(gate) * up).astype(jnp.bfloat16)
-        hidden_out[part, :] = hidden
-        down = lax.dot_general(hidden, down_left, dims(1, 1), preferred_element_type=jnp.float32)
-        down = jnp.where(column[:, :members] == member[:, :members], down, 0.0)
-        down_score = noise_scale * jnp.sum(down, axis=1, keepdims=True)
-        score_out[part, :] = jnp.broadcast_to(down_score, (tall, 128))
-        share = jnp.dot(hidden, down_rhs, preferred_element_type=jnp.float32)
-        share = share + spread_rows(down_score, lane_block(down_r, at[slot], span, mine), per_member)
-        out[inner, :] = share.astype(out.dtype)
+    piece = jnp.concatenate([top[...], bottom[...]], axis=0)
+    score = scores[...] + lax.dot_general(piece, left, dims(1, 1), preferred_element_type=jnp.float32)
+    member = lax.broadcasted_iota(jnp.int32, (rows, 2 * members), 0) // per_member
+    column = lax.broadcasted_iota(jnp.int32, (rows, 2 * members), 1)
+    gate_score = noise_scale * jnp.sum(jnp.where(column == member, score, 0.0), axis=1, keepdims=True)
+    up_score = noise_scale * jnp.sum(jnp.where(column == member + members, score, 0.0), axis=1, keepdims=True)
+    for at_col in range(0, cols, wide):
+        some = slice(at_col, at_col + wide)
+        rhs = jnp.concatenate([gate_w[weight_rows, some], up_w[weight_rows, some]], axis=1)
+        both = jnp.dot(piece, rhs, preferred_element_type=jnp.float32)
+        gate = gate_sum[:, some] + both[:, :wide] + spread_rows(gate_score, rights[own, some], per_member)
+        up = up_sum[:, some] + both[:, wide:] + spread_rows(up_score, rights[own_up, some], per_member)
+        hidden_out[:, some] = (silu(gate) * up).astype(jnp.bfloat16)
+    hidden = hidden_out[...]
+    down = lax.dot_general(hidden, down_left, dims(1, 1), preferred_element_type=jnp.float32)
+    down = jnp.where(column[:, :members] == member[:, :members], down, 0.0)
+    down_score = noise_scale * jnp.sum(down, axis=1, keepdims=True)
+    score_out[...] = jnp.broadcast_to(down_score, (rows, 128))
+    share = jnp.dot(hidden, down_rhs, preferred_element_type=jnp.float32)
+    share = (share + spread_rows(down_score, lane_block(down_r, at[slot], span, own), per_member)).astype(on_out.dtype)
+    on_out[...] = share[:half, :]
+    back_out[...] = share[half:, :]
 
 
 def finish(at, total, top, bottom, weights, others, slot, first, per_member, wire):
     rows, cols = total[0].shape
     span = top.shape[1]
     return call(
-        lambda *refs: finish_kernel(slot, first, per_member, rows // 2, *refs),
+        lambda *refs: finish_kernel(slot, first, per_member, 128, *refs),
         (at, *total, top, bottom, *weights, *others),
         (
             jax.ShapeDtypeStruct((rows, cols), jnp.bfloat16),

time: 61.6 us -> 61.6 us (level)
  no operation moved by 1% of the time
where the time goes in v6:
time: 61.6 us; the launch traced here: 61.4 us
  Pallas kernels  22.5 us (37%)
  starting transfers between devices  19.4 us (31%)
  waiting for transfers between devices  16.7 us (27%)
  other arithmetic  1.89 us (3%)
  between operations  0.79 us (1%)
    pallas_call x11, Pallas kernels, call(): pl.pallas_call(body, out_shape=out_shape, in_specs=in_specs or [SMEM] + [...  22.5 us
    ppermute x8, starting transfers between devices, per_device(): on = lambda a: lax.ppermute(a, 'wsh', onward)  14.5 us
    ppermute x8, waiting for transfers between devices, per_device(): on = lambda a: lax.ppermute(a, 'wsh', onward)  13.7 us
    ppermute x8, starting transfers between devices, per_device(): back_to = lambda a: lax.ppermute(a, 'wsh', back)  3.26 us
    ppermute x8, waiting for transfers between devices, per_device(): back_to = lambda a: lax.ppermute(a, 'wsh', back)  3.08 us
    ppermute x1, starting transfers between devices, per_device(): far_in = lax.ppermute(far, 'grp', pair)  1.55 us
  transfers between devices with their start and end apart: 19, of which 10 were waited for; matrix products, arithmetic and copies ran while one was open for 2% of the time, Pallas kernels for 37%

profile of v6, /device:TPU:0, one launch (start us, length us, event | category | flops | bytes accessed | tf_op | source)
XLA Modules:
  0.0 61.4 jit_solution(14156241899057789189)
XLA Ops:
  0.6 3.1 %collective-permute-start = (bf16[512,256]{1,0:T(8,128)(2,1)}, bf16[512,256]{1,0:T(8,128)(2,1)S(1)}, u32[]{:S(2)}, u32[]{:S(2)}) collective-permute-start(bf16[512,256]{1,0:T(8,128)(2,1)} %refs_1_.4), channel_id=1, source_target_pairs={{0,2},{2,4},{4,6},{6,7},{7,5},{5,3},{3,1},{1,0},{8,10},{10,12},{12... | collective-permute-start | bytes 786440 | tf_op jit(solution)/shard_map/ppermute | solution.py:474
  3.7 0.7 %multiply_bitcast_fusion = f32[64,1]{0,1:T(1,128)S(1)} fusion(s32[64]{0:T(128)} %param.21), kind=kLoop, calls=%fused_computation.17 | loop fusion | flops 256 | bytes 512 | tf_op jit(solution)/shard_map/broadcast_in_dim | solution.py:529
  4.4 0.1 copy.21.refs_1_
  4.5 0.1 pad_add_fusion.refs_0_
  4.6 3.4 %stage_one.1 = (bf16[128,2048]{1,0:T(8,128)(2,1)S(1)}, bf16[2048,896]{1,0:T(8,128)(2,1)S(1)}, bf16[2048,896]{1,0:T(8,128)(2,1)S(1)}) custom-call(bf16[64,2048]{1,0:T(8,128)(2,1)} %refs_0_.2, bf16[64,2048]{1,0:T(8,128)(2,1)} %refs_1_.3, bf16[2048,896]{1,0:T(8,128)(2,1)} %refs_2_.2, bf16[2048,896]{1,0:T(8,128)(2,1)} %refs_3_.2), custom_call_target="tpu_custom_call" | custom-call | flops 4000000000 | bytes 1000000 | tf_op jit(solution)/shard_map/stage_one/pallas_call | solution.py:196
  8.0 2.2 %collective-permute-done.refs_2_ = bf16[512,256]{1,0:T(8,128)(2,1)S(1)} collective-permute-done((bf16[512,256]{1,0:T(8,128)(2,1)}, bf16[512,256]{1,0:T(8,128)(2,1)S(1)}, u32[]{:S(2)}, u32[]{:S(2)}) %collective-permute-start) | collective-permute-done | bytes 262176 | tf_op jit(solution)/shard_map/ppermute | solution.py:474
  10.1 1.8 %collective-permute-start.1 = (bf16[512,256]{1,0:T(8,128)(2,1)S(1)}, bf16[512,256]{1,0:T(8,128)(2,1)S(1)}, u32[]{:S(2)}, u32[]{:S(2)}) collective-permute-start(bf16[512,256]{1,0:T(8,128)(2,1)S(1)} %collective-permute-done.refs_2_), channel_id=1, source_target_pairs={{0,2},{2,4},{4,6},{6,7},{7,5},{5,3},{3,1},{1,0},{8,10},{10,12},{12... | collective-permute-start | bytes 786440 | tf_op jit(solution)/shard_map/ppermute | solution.py:474
  12.0 0.2 collective-permute-start.4
  12.2 2.6 %grow.3 = (f32[512,896]{1,0:T(8,128)S(1)}, f32[512,896]{1,0:T(8,128)S(1)}, f32[512,128]{1,0:T(8,128)S(1)}) custom-call(s32[11]{0:T(128)S(1)} %pad_add_fusion.refs_0_, bf16[512,256]{1,0:T(8,128)(2,1)S(1)} %copy-done, bf16[512,256]{1,0:T(8,128)(2,1)S(1)} %collective-permute-done.refs_2_, bf16[512,256]{1,0:T(8,128)(2,1)S(1)} %collective-permute-done.3.refs_3_, ...), custom_call_target="tpu_custom_call" | custom-call | flops 5000000000 | bytes 1000000 | tf_op jit(solution)/shard_map/grow/pallas_call | solution.py:196
  14.7 2.5 %stage_two.1 = (f32[128,896]{1,0:T(8,128)S(1)}, bf16[64,896]{1,0:T(8,128)(2,1)S(1)}, f32[64,2048]{1,0:T(8,128)S(1)}, bf16[896,2048]{1,0:T(8,128)(2,1)S(1)}) custom-call(f32[64,896]{1,0:T(8,128)} %refs_0_.3, f32[64,896]{1,0:T(8,128)} %refs_1_.5, bf16[64,896]{1,0:T(8,128)(2,1)} %refs_2_.3, f32[64,2048]{1,0:T(8,128)} %refs_3_.3, bf16[896,2048]{1,0:T(8,128)(2,1)} %refs_4_.1, ...), custom_call_target="tpu_custom_call" | custom-call | flops 2000000000 | bytes 1000000 | tf_op jit(solution)/shard_map/stage_two/pallas_call | solution.py:196
  17.3 0.3 collective-permute-done.1.refs_1_
  17.6 1.5 %collective-permute-start.2 = (bf16[512,256]{1,0:T(8,128)(2,1)S(1)}, bf16[512,256]{1,0:T(8,128)(2,1)S(1)}, u32[]{:S(2)}, u32[]{:S(2)}) collective-permute-start(bf16[512,256]{1,0:T(8,128)(2,1)S(1)} %collective-permute-done.1.refs_1_), channel_id=1, source_target_pairs={{0,2},{2,4},{4,6},{6,7},{7,5},{5,3},{3,1},{1,0},{8,10},{10,12},{12... | collective-permute-start | bytes 786440 | tf_op jit(solution)/shard_map/ppermute | solution.py:474
  19.2 0.0 collective-permute-done.4.refs_2_
  19.2 0.5 collective-permute-start.5
  19.7 2.1 %grow.4 = (f32[512,896]{1,0:T(8,128)S(1)}, f32[512,896]{1,0:T(8,128)S(1)}, f32[512,128]{1,0:T(8,128)S(1)}) custom-call(s32[11]{0:T(128)S(1)} %pad_add_fusion.refs_0_, bf16[512,256]{1,0:T(8,128)(2,1)S(1)} %collective-permute-done.1.refs_1_, ...), custom_call_target="tpu_custom_call", output_to_operand_aliasing={{0}: (6, {}), {1}: (7, {}), {2}: (8, {})} | custom-call | flops 5000000000 | bytes 1000000 | tf_op jit(solution)/shard_map/grow/pallas_call | solution.py:196
  21.8 0.6 %messages.1 = (bf16[64,3840]{1,0:T(8,128)(2,1)S(1)}, bf16[64,3840]{1,0:T(8,128)(2,1)S(1)}) custom-call(s32[11]{0:T(128)S(1)} %pad_add_fusion.refs_0_, f32[64,1]{1,0:T(8,128)S(1)} %copy.21.refs_1_, f32[128,896]{1,0:T(8,128)S(1)} %get-tuple-element.47.refs_9_.refs_2_, bf16[128,2048]{1,0:T(8,128)(2,1)S(1)} %get-tuple-element.37.refs_6_.refs_5_.refs_8_.refs_3_, ...), custom_call_target="tpu_custom_call" | custom-call | flops 2000000000 | bytes 1000000 | tf_op jit(solution)/shard_map/messages/pallas_call | solution.py:196
  22.5 1.5 %collective-permute-start.8 = (bf16[64,3840]{1,0:T(8,128)(2,1)S(1)}, bf16[64,3840]{1,0:T(8,128)(2,1)S(1)}, u32[]{:S(2)}, u32[]{:S(2)}) collective-permute-start(bf16[64,3840]{1,0:T(8,128)(2,1)S(1)} %get-tuple-element.56), channel_id=1, source_target_pairs={{0,16},{8,24},{16,0},{24,8},{1,17},{9,25},{17,1},{25,9},{2,18},{10... | collective-permute-start | bytes 1474568 | tf_op jit(solution)/shard_map/ppermute | solution.py:530
  24.0 0.3 collective-permute-done.2.refs_1_
  24.3 1.6 %collective-permute-start.6 = (bf16[256,256]{1,0:T(8,128)(2,1)S(1)}, bf16[256,256]{1,0:T(8,128)(2,1)S(1)}, u32[]{:S(2)}, u32[]{:S(2)}) collective-permute-start(bf16[256,256]{1,0:T(8,128)(2,1)S(1)} %slice.26), channel_id=1, source_target_pairs={{0,2},{2,4},{4,6},{6,7},{7,5},{5,3},{3,1},{1,0},{8,10},{10,12},{12... | collective-permute-start | bytes 393224 | tf_op jit(solution)/shard_map/ppermute | solution.py:474
  25.9 0.6 collective-permute-start.7
  26.4 2.1 %grow.5 = (f32[512,896]{1,0:T(8,128)S(1)}, f32[512,896]{1,0:T(8,128)S(1)}, f32[512,128]{1,0:T(8,128)S(1)}) custom-call(s32[11]{0:T(128)S(1)} %pad_add_fusion.refs_0_, bf16[512,256]{1,0:T(8,128)(2,1)S(1)} %collective-permute-done.2.refs_1_, ...), custom_call_target="tpu_custom_call", output_to_operand_aliasing={{0}: (6, {}), {1}: (7, {}), {2}: (8, {})} | custom-call | flops 5000000000 | bytes 1000000 | tf_op jit(solution)/shard_map/grow/pallas_call | solution.py:196
  28.6 1.4 %collective-permute-done.6.refs_4_ = bf16[256,256]{1,0:T(8,128)(2,1)S(1)} collective-permute-done((bf16[256,256]{1,0:T(8,128)(2,1)S(1)}, bf16[256,256]{1,0:T(8,128)(2,1)S(1)}, u32[]{:S(2)}, u32[]{:S(2)}) %collective-permute-start.6) | collective-permute-done | bytes 131104 | tf_op jit(solution)/shard_map/ppermute | solution.py:474
  30.0 1.4 %collective-permute-done.7.refs_5_ = bf16[256,256]{1,0:T(8,128)(2,1)S(1)} collective-permute-done((bf16[256,256]{1,0:T(8,128)(2,1)S(1)}, bf16[256,256]{1,0:T(8,128)(2,1)S(1)}, u32[]{:S(2)}, u32[]{:S(2)}) %collective-permute-start.7) | collective-permute-done | bytes 131104 | tf_op jit(solution)/shard_map/ppermute | solution.py:475
  31.3 2.8 %finish.1 = (bf16[512,896]{1,0:T(8,128)(2,1)S(1)}, f32[512,128]{1,0:T(8,128)S(1)}, bf16[256,256]{1,0:T(8,128)(2,1)S(1)}, bf16[256,256]{1,0:T(8,128)(2,1)S(1)}) custom-call(s32[11]{0:T(128)S(1)} %pad_add_fusion.refs_0_, f32[512,896]{1,0:T(8,128)S(1)} %get-tuple-element.44.refs_1_, f32[512,896]{1,0:T(8,128)S(1)} %get-tuple-element.45.refs_2_, ...), custom_call_target="tpu_custom_call" | custom-call | flops 4000000000 | bytes 1000000 | tf_op jit(solution)/shard_map/finish/pallas_call | solution.py:196
  34.1 1.6 %collective-permute-start.9 = (bf16[256,256]{1,0:T(8,128)(2,1)S(1)}, bf16[256,256]{1,0:T(8,128)(2,1)S(1)}, u32[]{:S(2)}, u32[]{:S(2)}) collective-permute-start(bf16[256,256]{1,0:T(8,128)(2,1)S(1)} %get-tuple-element.58), channel_id=1, source_target_pairs={{0,2},{2,4},{4,6},{6,7},{7,5},{5,3},{3,1},{1,0},{8,10},{10,12},{12... | collective-permute-start | bytes 393224 | tf_op jit(solution)/shard_map/ppermute | solution.py:474
  35.7 0.5 collective-permute-start.13
  36.2 1.3 %shares.5 = (f32[512,256]{1,0:T(8,128)S(1)}, f32[512,256]{1,0:T(8,128)S(1)}, bf16[64,3840]{1,0:T(8,128)(2,1)S(1)}) custom-call(s32[11]{0:T(128)S(1)} %pad_add_fusion.refs_0_, bf16[512,896]{1,0:T(8,128)(2,1)S(1)} %get-tuple-element.51.refs_1_, f32[512,128]{1,0:T(8,128)S(1)} %get-tuple-element.52.refs_2_, ...), custom_call_target="tpu_custom_call", output_to_operand_aliasing={{2}: (5, {})} | custom-call | flops 4000000000 | bytes 1000000 | tf_op jit(solution)/shard_map/shares/pallas_call | solution.py:196
  37.5 1.6 %collective-permute-done.9 = bf16[256,256]{1,0:T(8,128)(2,1)S(1)} collective-permute-done((bf16[256,256]{1,0:T(8,128)(2,1)S(1)}, bf16[256,256]{1,0:T(8,128)(2,1)S(1)}, u32[]{:S(2)}, u32[]{:S(2)}) %collective-permute-start.9) | collective-permute-done | bytes 131104 | tf_op jit(solution)/shard_map/ppermute | solution.py:474
  39.2 1.6 %collective-permute-start.10 = (bf16[512,256]{1,0:T(8,128)(2,1)S(1)}, bf16[512,256]{1,0:T(8,128)(2,1)S(1)}, u32[]{:S(2)}, u32[]{:S(2)}) collective-permute-start(bf16[512,256]{1,0:T(8,128)(2,1)S(1)} %pad_maximum_fusion), channel_id=1, source_target_pairs={{0,2},{2,4},{4,6},{6,7},{7,5},{5,3},{3,1},{1,0},{8,10},{10,12},{12... | collective-permute-start | bytes 786440 | tf_op jit(solution)/shard_map/ppermute | solution.py:474
  40.9 0.5 collective-permute-start.14
  41.4 1.3 %shares.4 = (f32[512,256]{1,0:T(8,128)S(1)}, f32[512,256]{1,0:T(8,128)S(1)}) custom-call(s32[11]{0:T(128)S(1)} %pad_add_fusion.refs_0_, bf16[512,896]{1,0:T(8,128)(2,1)S(1)} %get-tuple-element.51.refs_1_, f32[512,128]{1,0:T(8,128)S(1)} %get-tuple-element.52.refs_2_, bf16[896,2048]{1,0:T(8,128)(2,1)S(1)} %get-tuple-element.49.refs_11_.refs_3_, ...), custom_call_target="tpu_custom_call" | custom-call | flops 4000000000 | bytes 1000000 | tf_op jit(solution)/shard_map/shares/pallas_call | solution.py:196
  42.7 3.3 %collective-permute-done.10 = bf16[512,256]{1,0:T(8,128)(2,1)S(1)} collective-permute-done((bf16[512,256]{1,0:T(8,128)(2,1)S(1)}, bf16[512,256]{1,0:T(8,128)(2,1)S(1)}, u32[]{:S(2)}, u32[]{:S(2)}) %collective-permute-start.10) | collective-permute-done | bytes 262176 | tf_op jit(solution)/shard_map/ppermute | solution.py:474
  46.0 0.1 add_convert_fusion.4
  46.0 1.6 %collective-permute-start.11 = (bf16[512,256]{1,0:T(8,128)(2,1)S(1)}, bf16[512,256]{1,0:T(8,128)(2,1)S(1)}, u32[]{:S(2)}, u32[]{:S(2)}) collective-permute-start(bf16[512,256]{1,0:T(8,128)(2,1)S(1)} %add_convert_fusion.4), channel_id=1, source_target_pairs={{0,2},{2,4},{4,6},{6,7},{7,5},{5,3},{3,1},{1,0},{8,10},{10,12},{12... | collective-permute-start | bytes 786440 | tf_op jit(solution)/shard_map/ppermute | solution.py:474
  47.7 0.1 add_convert_fusion.2
  47.7 0.5 collective-permute-start.15
  48.2 1.5 %shares.3 = (f32[512,256]{1,0:T(8,128)S(1)}, f32[512,256]{1,0:T(8,128)S(1)}, f32[512,256]{1,0:T(8,128)S(1)}) custom-call(s32[11]{0:T(128)S(1)} %pad_add_fusion.refs_0_, bf16[512,896]{1,0:T(8,128)(2,1)S(1)} %get-tuple-element.51.refs_1_, f32[512,128]{1,0:T(8,128)S(1)} %get-tuple-element.52.refs_2_, bf16[896,2048]{1,0:T(8,128)(2,1)S(1)} %get-tuple-element.49.refs_11_.refs_3_, ...), custom_call_target="tpu_custom_call" | custom-call | flops 4000000000 | bytes 1000000 | tf_op jit(solution)/shard_map/shares/pallas_call | solution.py:196
  49.8 0.1 collective-permute-start.18
  49.9 2.6 %collective-permute-done.11 = bf16[512,256]{1,0:T(8,128)(2,1)S(1)} collective-permute-done((bf16[512,256]{1,0:T(8,128)(2,1)S(1)}, bf16[512,256]{1,0:T(8,128)(2,1)S(1)}, u32[]{:S(2)}, u32[]{:S(2)}) %collective-permute-start.11) | collective-permute-done | bytes 262176 | tf_op jit(solution)/shard_map/ppermute | solution.py:474
  52.5 0.1 add_convert_fusion.3
  52.5 1.6 %collective-permute-start.12 = (bf16[512,256]{1,0:T(8,128)(2,1)S(1)}, bf16[512,256]{1,0:T(8,128)(2,1)S(1)}, u32[]{:S(2)}, u32[]{:S(2)}) collective-permute-start(bf16[512,256]{1,0:T(8,128)(2,1)S(1)} %add_convert_fusion.3), channel_id=1, source_target_pairs={{0,2},{2,4},{4,6},{6,7},{7,5},{5,3},{3,1},{1,0},{8,10},{10,12},{12... | collective-permute-start | bytes 786440 | tf_op jit(solution)/shard_map/ppermute | solution.py:474
  54.1 0.0 collective-permute-done.15
  54.1 0.1 add_convert_fusion.1
  54.2 0.5 collective-permute-start.16
  54.7 2.2 %outers.1 = (bf16[512,896]{1,0:T(8,128)(2,1)}, bf16[512,896]{1,0:T(8,128)(2,1)}) custom-call(s32[11]{0:T(128)S(1)} %pad_add_fusion.refs_0_, bf16[64,3840]{1,0:T(8,128)(2,1)S(1)} %get-tuple-element.63.refs_1_, bf16[64,3840]{1,0:T(8,128)(2,1)S(1)} %collective-permute-done.17.refs_2_, bf16[64,3840]{1,0:T(8,128)(2,1)S(1)} %get-tuple-element.64.refs_3_, ...), custom_call_target="tpu_custom_call" | custom-call | flops 5000000000 | bytes 1000000 | tf_op jit(solution)/shard_map/outers/pallas_call | solution.py:196
  57.0 2.0 %collective-permute-done.12 = bf16[512,256]{1,0:T(8,128)(2,1)S(1)} collective-permute-done((bf16[512,256]{1,0:T(8,128)(2,1)S(1)}, bf16[512,256]{1,0:T(8,128)(2,1)S(1)}, u32[]{:S(2)}, u32[]{:S(2)}) %collective-permute-start.12) | collective-permute-done | bytes 262176 | tf_op jit(solution)/shard_map/ppermute | solution.py:474
  58.9 1.7 %collective-permute-done.16 = bf16[512,256]{1,0:T(8,128)(2,1)S(1)} collective-permute-done((bf16[512,256]{1,0:T(8,128)(2,1)S(1)}, bf16[512,256]{1,0:T(8,128)(2,1)S(1)}, u32[]{:S(2)}, u32[]{:S(2)}) %collective-permute-start.16) | collective-permute-done | bytes 262176 | tf_op jit(solution)/shard_map/ppermute | solution.py:475
  60.6 0.8 %add_convert_fusion = bf16[512,256]{1,0:T(8,128)(2,1)} fusion(bf16[512,256]{1,0:T(8,128)(2,1)S(1)} %collective-permute-done.16, f32[512,256]{1,0:T(8,128)S(1)} %get-tuple-element.53, bf16[512,256]{1,0:T(8,128)(2,1)S(1)} %collective-permute-done.12), kind=kLoop, calls=%fused_computation | loop fusion | flops 655360 | bytes 1310720 | tf_op jit(solution)/shard_map/convert_element_type | solution.py:518
  (20 shorter events, 0.2 us)
Async XLA Ops:
  0.6 9.5 %collective-permute-start = (bf16[512,256]{1,0:T(8,128)(2,1)}, bf16[512,256]{1,0:T(8,128)(2,1)S(1)}, u32[]{:S(2)}, u32[]{:S(2)}) collective-permute-start(bf16[512,256]{1,0:T(8,128)(2,1)} %refs_1_.4), channel_id=1, source_target_pairs={{0,2},{2,4},{4,6},{6,7},{7,5},{5,3},{3,1},{1,0},{8,10},{10,12},{12... | collective-permute-start | bytes 786440 | tf_op jit(solution)/shard_map/ppermute | solution.py:474
  3.7 8.3 %collective-permute-start.3 = (bf16[512,256]{1,0:T(8,128)(2,1)}, bf16[512,256]{1,0:T(8,128)(2,1)S(1)}, u32[]{:S(2)}, u32[]{:S(2)}) collective-permute-start(bf16[512,256]{1,0:T(8,128)(2,1)} %refs_1_.4), channel_id=1, source_target_pairs={{2,0},{4,2},{6,4},{7,6},{5,7},{3,5},{1,3},{0,1},{10,8},{12,10},{14... | collective-permute-start | bytes 786440 | tf_op jit(solution)/shard_map/ppermute | solution.py:475
  4.6 7.6 %copy-start = (bf16[512,256]{1,0:T(8,128)(2,1)S(1)}, bf16[512,256]{1,0:T(8,128)(2,1)}, u32[]{:S(2)}) copy-start(bf16[512,256]{1,0:T(8,128)(2,1)} %refs_1_.4) | copy-start | bytes 786436
  10.1 7.5 %collective-permute-start.1 = (bf16[512,256]{1,0:T(8,128)(2,1)S(1)}, bf16[512,256]{1,0:T(8,128)(2,1)S(1)}, u32[]{:S(2)}, u32[]{:S(2)}) collective-permute-start(bf16[512,256]{1,0:T(8,128)(2,1)S(1)} %collective-permute-done.refs_2_), channel_id=1, source_target_pairs={{0,2},{2,4},{4,6},{6,7},{7,5},{5,3},{3,1},{1,0},{8,10},{10,12},{12... | collective-permute-start | bytes 786440 | tf_op jit(solution)/shard_map/ppermute | solution.py:474
  12.0 7.2 %collective-permute-start.4 = (bf16[512,256]{1,0:T(8,128)(2,1)S(1)}, bf16[512,256]{1,0:T(8,128)(2,1)S(1)}, u32[]{:S(2)}, u32[]{:S(2)}) collective-permute-start(bf16[512,256]{1,0:T(8,128)(2,1)S(1)} %collective-permute-done.3.refs_3_), channel_id=1, source_target_pairs={{2,0},{4,2},{6,4},{7,6},{5,7},{3,5},{1,3},{0,1},{10,8},{12,10},{14... | collective-permute-start | bytes 786440 | tf_op jit(solution)/shard_map/ppermute | solution.py:475
  17.6 6.7 %collective-permute-start.2 = (bf16[512,256]{1,0:T(8,128)(2,1)S(1)}, bf16[512,256]{1,0:T(8,128)(2,1)S(1)}, u32[]{:S(2)}, u32[]{:S(2)}) collective-permute-start(bf16[512,256]{1,0:T(8,128)(2,1)S(1)} %collective-permute-done.1.refs_1_), channel_id=1, source_target_pairs={{0,2},{2,4},{4,6},{6,7},{7,5},{5,3},{3,1},{1,0},{8,10},{10,12},{12... | collective-permute-start | bytes 786440 | tf_op jit(solution)/shard_map/ppermute | solution.py:474
  19.2 6.7 %collective-permute-start.5 = (bf16[512,256]{1,0:T(8,128)(2,1)S(1)}, bf16[512,256]{1,0:T(8,128)(2,1)S(1)}, u32[]{:S(2)}, u32[]{:S(2)}) collective-permute-start(bf16[512,256]{1,0:T(8,128)(2,1)S(1)} %collective-permute-done.4.refs_2_), channel_id=1, source_target_pairs={{2,0},{4,2},{6,4},{7,6},{5,7},{3,5},{1,3},{0,1},{10,8},{12,10},{14... | collective-permute-start | bytes 786440 | tf_op jit(solution)/shard_map/ppermute | solution.py:475
  22.5 13.8 %collective-permute-start.8 = (bf16[64,3840]{1,0:T(8,128)(2,1)S(1)}, bf16[64,3840]{1,0:T(8,128)(2,1)S(1)}, u32[]{:S(2)}, u32[]{:S(2)}) collective-permute-start(bf16[64,3840]{1,0:T(8,128)(2,1)S(1)} %get-tuple-element.56), channel_id=1, source_target_pairs={{0,16},{8,24},{16,0},{24,8},{1,17},{9,25},{17,1},{25,9},{2,18},{10... | collective-permute-start | bytes 1474568 | tf_op jit(solution)/shard_map/ppermute | solution.py:530
  24.0 30.7 %collective-permute-start.17 = (bf16[64,3840]{1,0:T(8,128)(2,1)S(1)}, bf16[64,3840]{1,0:T(8,128)(2,1)S(1)}, u32[]{:S(2)}, u32[]{:S(2)}) collective-permute-start(bf16[64,3840]{1,0:T(8,128)(2,1)S(1)} %get-tuple-element.63.refs_1_), channel_id=1, source_target_pairs={{0,8},{8,0},{16,24},{24,16},{1,9},{9,1},{17,25},{25,17},{2,10},{10... | collective-permute-start | bytes 1474568 | tf_op jit(solution)/shard_map/ppermute | solution.py:531
  24.3 5.7 %collective-permute-start.6 = (bf16[256,256]{1,0:T(8,128)(2,1)S(1)}, bf16[256,256]{1,0:T(8,128)(2,1)S(1)}, u32[]{:S(2)}, u32[]{:S(2)}) collective-permute-start(bf16[256,256]{1,0:T(8,128)(2,1)S(1)} %slice.26), channel_id=1, source_target_pairs={{0,2},{2,4},{4,6},{6,7},{7,5},{5,3},{3,1},{1,0},{8,10},{10,12},{12... | collective-permute-start | bytes 393224 | tf_op jit(solution)/shard_map/ppermute | solution.py:474
  25.9 5.5 %collective-permute-start.7 = (bf16[256,256]{1,0:T(8,128)(2,1)S(1)}, bf16[256,256]{1,0:T(8,128)(2,1)S(1)}, u32[]{:S(2)}, u32[]{:S(2)}) collective-permute-start(bf16[256,256]{1,0:T(8,128)(2,1)S(1)} %slice.27), channel_id=1, source_target_pairs={{2,0},{4,2},{6,4},{7,6},{5,7},{3,5},{1,3},{0,1},{10,8},{12,10},{14... | collective-permute-start | bytes 393224 | tf_op jit(solution)/shard_map/ppermute | solution.py:475
  34.1 5.0 %collective-permute-start.9 = (bf16[256,256]{1,0:T(8,128)(2,1)S(1)}, bf16[256,256]{1,0:T(8,128)(2,1)S(1)}, u32[]{:S(2)}, u32[]{:S(2)}) collective-permute-start(bf16[256,256]{1,0:T(8,128)(2,1)S(1)} %get-tuple-element.58), channel_id=1, source_target_pairs={{0,2},{2,4},{4,6},{6,7},{7,5},{5,3},{3,1},{1,0},{8,10},{10,12},{12... | collective-permute-start | bytes 393224 | tf_op jit(solution)/shard_map/ppermute | solution.py:474
  35.7 5.1 %collective-permute-start.13 = (bf16[256,256]{1,0:T(8,128)(2,1)S(1)}, bf16[256,256]{1,0:T(8,128)(2,1)S(1)}, u32[]{:S(2)}, u32[]{:S(2)}) collective-permute-start(bf16[256,256]{1,0:T(8,128)(2,1)S(1)} %get-tuple-element.62), channel_id=1, source_target_pairs={{2,0},{4,2},{6,4},{7,6},{5,7},{3,5},{1,3},{0,1},{10,8},{12,10},{14... | collective-permute-start | bytes 393224 | tf_op jit(solution)/shard_map/ppermute | solution.py:475
  39.2 6.8 %collective-permute-start.10 = (bf16[512,256]{1,0:T(8,128)(2,1)S(1)}, bf16[512,256]{1,0:T(8,128)(2,1)S(1)}, u32[]{:S(2)}, u32[]{:S(2)}) collective-permute-start(bf16[512,256]{1,0:T(8,128)(2,1)S(1)} %pad_maximum_fusion), channel_id=1, source_target_pairs={{0,2},{2,4},{4,6},{6,7},{7,5},{5,3},{3,1},{1,0},{8,10},{10,12},{12... | collective-permute-start | bytes 786440 | tf_op jit(solution)/shard_map/ppermute | solution.py:474
  40.9 6.8 %collective-permute-start.14 = (bf16[512,256]{1,0:T(8,128)(2,1)S(1)}, bf16[512,256]{1,0:T(8,128)(2,1)S(1)}, u32[]{:S(2)}, u32[]{:S(2)}) collective-permute-start(bf16[512,256]{1,0:T(8,128)(2,1)S(1)} %pad_maximum_fusion.1), channel_id=1, source_target_pairs={{2,0},{4,2},{6,4},{7,6},{5,7},{3,5},{1,3},{0,1},{10,8},{12,10},{14... | collective-permute-start | bytes 786440 | tf_op jit(solution)/shard_map/ppermute | solution.py:475
  46.0 6.4 %collective-permute-start.11 = (bf16[512,256]{1,0:T(8,128)(2,1)S(1)}, bf16[512,256]{1,0:T(8,128)(2,1)S(1)}, u32[]{:S(2)}, u32[]{:S(2)}) collective-permute-start(bf16[512,256]{1,0:T(8,128)(2,1)S(1)} %add_convert_fusion.4), channel_id=1, source_target_pairs={{0,2},{2,4},{4,6},{6,7},{7,5},{5,3},{3,1},{1,0},{8,10},{10,12},{12... | collective-permute-start | bytes 786440 | tf_op jit(solution)/shard_map/ppermute | solution.py:474
  47.7 6.4 %collective-permute-start.15 = (bf16[512,256]{1,0:T(8,128)(2,1)S(1)}, bf16[512,256]{1,0:T(8,128)(2,1)S(1)}, u32[]{:S(2)}, u32[]{:S(2)}) collective-permute-start(bf16[512,256]{1,0:T(8,128)(2,1)S(1)} %add_convert_fusion.2), channel_id=1, source_target_pairs={{2,0},{4,2},{6,4},{7,6},{5,7},{3,5},{1,3},{0,1},{10,8},{12,10},{14... | collective-permute-start | bytes 786440 | tf_op jit(solution)/shard_map/ppermute | solution.py:475
  49.8 5.0 %collective-permute-start.18 = (bf16[64,3840]{1,0:T(8,128)(2,1)S(1)}, bf16[64,3840]{1,0:T(8,128)(2,1)S(1)}, u32[]{:S(2)}, u32[]{:S(2)}) collective-permute-start(bf16[64,3840]{1,0:T(8,128)(2,1)S(1)} %get-tuple-element.64.refs_3_), channel_id=1, source_target_pairs={{0,8},{8,0},{16,24},{24,16},{1,9},{9,1},{17,25},{25,17},{2,10},{10... | collective-permute-start | bytes 1474568 | tf_op jit(solution)/shard_map/ppermute | solution.py:538
  52.5 6.4 %collective-permute-start.12 = (bf16[512,256]{1,0:T(8,128)(2,1)S(1)}, bf16[512,256]{1,0:T(8,128)(2,1)S(1)}, u32[]{:S(2)}, u32[]{:S(2)}) collective-permute-start(bf16[512,256]{1,0:T(8,128)(2,1)S(1)} %add_convert_fusion.3), channel_id=1, source_target_pairs={{0,2},{2,4},{4,6},{6,7},{7,5},{5,3},{3,1},{1,0},{8,10},{10,12},{12... | collective-permute-start | bytes 786440 | tf_op jit(solution)/shard_map/ppermute | solution.py:474
  54.2 6.4 %collective-permute-start.16 = (bf16[512,256]{1,0:T(8,128)(2,1)S(1)}, bf16[512,256]{1,0:T(8,128)(2,1)S(1)}, u32[]{:S(2)}, u32[]{:S(2)}) collective-permute-start(bf16[512,256]{1,0:T(8,128)(2,1)S(1)} %add_convert_fusion.1), channel_id=1, source_target_pairs={{2,0},{4,2},{6,4},{7,6},{5,7},{3,5},{1,3},{0,1},{10,8},{12,10},{14... | collective-permute-start | bytes 786440 | tf_op jit(solution)/shard_map/ppermute | solution.py:475
